TPU v7x, 128 devices: a whole 4x4x4 slice. The times are simulated.
128 devices in a mesh: batch: 16 (over x_lo, z, core), depth: 4 (over y), height: 2 (over x_hi).
Axes of the slice: x: 4 (x_hi: 2, x_lo: 2; x = x_hi * 2 + x_lo), y: 4, z: 4, core: 2. Of those that a mesh axis runs over, the one named last changes fastest.
Arguments:
- inputs: bfloat16 [256, 16, 16, 8, 128], P('batch', 'depth', 'height'), may hold values from -6 to 6
- conv_early: bfloat16 [4, 4, 4, 64, 128], replicated, may hold values from -0.09375 to 0.09375
- conv_late: bfloat16 [3, 3, 3, 128, 128], replicated, may hold values from -0.109375 to 0.109375
- cotangent: bfloat16 [256, 8, 8, 8, 128], P(('batch', 'depth', 'height')), may hold values from -0.032958984 to 0.032958984
Outputs:
- activated: bfloat16 [256, 8, 8, 8, 128], P(('batch', 'depth', 'height'))
- grad_early: float32 [4, 4, 4, 64, 128], replicated
- grad_late: float32 [3, 3, 3, 128, 128], replicated
All inputs are finite; a program needn't handle non-finite values.
Results may differ from a plain program's by a relative error of at most 0.0059.
Values may be sent and summed in bfloat16 or wider, within the bound.
No kernel may reach another device: no remote copies, remote signals or barrier semaphores. Data moves between devices by JAX's collectives and lax.ppermute only.
A program may use at most 128 MiB of HBM per device.

v0:
```python
import jax
import jax.numpy as jnp
from jax import lax
from jax.sharding import PartitionSpec as P


def padded_2(block, sides, width):
    for axis, dim in sides:
        count = lax.axis_size(axis)
        forward = [(i, i + 1) for i in range(count - 1)]
        backward = [(target, source) for source, target in forward]
        low = lax.ppermute(
            lax.slice_in_dim(block, block.shape[dim] - width, None, axis=dim), axis, forward
        )
        high = lax.ppermute(lax.slice_in_dim(block, 0, width, axis=dim), axis, backward)
        block = jnp.concatenate([low, block, high], axis=dim)
    return block


def slope(value):
    sigma = jax.nn.sigmoid(value)
    return sigma * (1.0 + value * (1.0 - sigma))


def stride_taps(padded, depth_tap, height_tap, out_depth, out_height):
    pair_count = padded.shape[3] - 2
    half_width = padded.shape[4] // 2
    layers = padded[
        :, depth_tap : depth_tap + 2 * out_depth : 2, height_tap : height_tap + 2 * out_height : 2
    ]
    return jnp.concatenate(
        [
            layers[:, :, :, 1 : 1 + pair_count],
            layers[:, :, :, 0:pair_count, half_width:],
            layers[:, :, :, 2 : 2 + pair_count, :half_width],
        ],
        axis=-1,
    )


def stride_conv(padded, kernel_pairs, out_depth, out_height):
    pair_count = padded.shape[3] - 2
    result = None
    for depth_tap in range(4):
        for height_tap in range(4):
            operand = stride_taps(padded, depth_tap, height_tap, out_depth, out_height)
            product = jnp.dot(
                operand.reshape(-1, operand.shape[-1]),
                kernel_pairs[depth_tap, height_tap],
                preferred_element_type=jnp.float32,
            )
            result = product if result is None else result + product
    return result.reshape(padded.shape[0], out_depth, out_height, pair_count, -1)


def stride_grad(padded, error_early, out_depth, out_height):
    half_width = padded.shape[4] // 2
    flat_error = error_early.reshape(-1, error_early.shape[-1])
    outer = []
    for depth_tap in range(4):
        inner = []
        for height_tap in range(4):
            operand = stride_taps(padded, depth_tap, height_tap, out_depth, out_height)
            grad_pairs = lax.dot_general(
                operand.reshape(-1, operand.shape[-1]),
                flat_error,
                (((0,), (0,)), ((), ())),
                preferred_element_type=jnp.float32,
            )
            inner.append(
                jnp.stack(
                    [
                        grad_pairs[2 * half_width : 3 * half_width],
                        grad_pairs[:half_width],
                        grad_pairs[half_width : 2 * half_width],
                        grad_pairs[3 * half_width :],
                    ],
                    axis=0,
                )
            )
        outer.append(jnp.stack(inner, axis=0))
    return jnp.stack(outer, axis=0)


def cube_taps(padded, depth_tap, height_tap, extent):
    layers = padded[:, depth_tap : depth_tap + extent, height_tap : height_tap + extent]
    return jnp.concatenate(
        [layers[:, :, :, width_tap : width_tap + extent] for width_tap in range(3)], axis=-1
    )


def arrange_whole(received, depth_count, height_count):
    owned, stacked, block_height, width_cells, channels = received.shape
    block_depth = stacked // (depth_count * height_count)
    moved = received.reshape(
        owned, depth_count, height_count, block_depth, block_height, width_cells, channels
    )
    moved = moved.transpose(0, 1, 3, 2, 4, 5, 6)
    return moved.reshape(
        owned, depth_count * block_depth, height_count * block_height, width_cells, channels
    )


def split_whole(whole, depth_count, height_count):
    owned, full_depth, full_height, width_cells, channels = whole.shape
    block_depth = full_depth // depth_count
    block_height = full_height // height_count
    moved = whole.reshape(
        owned, depth_count, block_depth, height_count, block_height, width_cells, channels
    )
    moved = moved.transpose(0, 1, 3, 2, 4, 5, 6)
    return moved.reshape(
        owned, depth_count * height_count * block_depth, block_height, width_cells, channels
    )


def per_device(inputs, conv_early, conv_late, cotangent):
    depth_count = lax.axis_size("depth")
    height_count = lax.axis_size("height")
    kernel_pairs = jnp.concatenate(
        [conv_early[:, :, 1], conv_early[:, :, 2], conv_early[:, :, 0], conv_early[:, :, 3]], axis=2
    )
    grown = padded_2(inputs, (("depth", 1), ("height", 2)), 1)
    padded = jnp.pad(grown, ((0, 0), (0, 0), (0, 0), (1, 1), (0, 0)))
    out_depth = inputs.shape[1] // 2
    out_height = inputs.shape[2] // 2
    early = stride_conv(padded, kernel_pairs, out_depth, out_height)
    hidden_local = jax.nn.silu(early).astype(jnp.bfloat16)
    received = lax.all_to_all(
        hidden_local, ("depth", "height"), split_axis=0, concat_axis=1, tiled=True
    )
    hidden = arrange_whole(received, depth_count, height_count)
    owned = hidden.shape[0]
    extent = hidden.shape[1]
    in_channels = hidden.shape[-1]
    out_channels = conv_late.shape[-1]
    hidden_padded = jnp.pad(hidden, ((0, 0), (1, 1), (1, 1), (1, 1), (0, 0)))
    late = None
    for depth_tap in range(3):
        for height_tap in range(3):
            operand = cube_taps(hidden_padded, depth_tap, height_tap, extent)
            product = jnp.dot(
                operand.reshape(-1, 3 * in_channels),
                conv_late[depth_tap, height_tap].reshape(3 * in_channels, out_channels),
                preferred_element_type=jnp.float32,
            )
            late = product if late is None else late + product
    late = late.reshape(owned, extent, extent, extent, out_channels)
    activated = jax.nn.silu(late).astype(jnp.bfloat16)
    error_late = (cotangent.astype(jnp.float32) * slope(late)).astype(jnp.bfloat16)
    flat_error = error_late.reshape(-1, out_channels)
    late_rows = []
    for depth_tap in range(3):
        inner = []
        for height_tap in range(3):
            operand = cube_taps(hidden_padded, depth_tap, height_tap, extent)
            grad_taps = lax.dot_general(
                operand.reshape(-1, 3 * in_channels),
                flat_error,
                (((0,), (0,)), ((), ())),
                preferred_element_type=jnp.float32,
            )
            inner.append(grad_taps.reshape(3, in_channels, out_channels))
        late_rows.append(jnp.stack(inner, axis=0))
    grad_late = jnp.stack(late_rows, axis=0)
    error_padded = jnp.pad(error_late, ((0, 0), (1, 1), (1, 1), (1, 1), (0, 0)))
    error_field = None
    for depth_tap in range(3):
        for height_tap in range(3):
            operand = cube_taps(error_padded, 2 - depth_tap, 2 - height_tap, extent)
            flipped = jnp.swapaxes(conv_late[depth_tap, height_tap, ::-1], 1, 2).reshape(
                3 * out_channels, in_channels
            )
            product = jnp.dot(
                operand.reshape(-1, 3 * out_channels), flipped, preferred_element_type=jnp.float32
            )
            error_field = product if error_field is None else error_field + product
    error_hidden = error_field.reshape(owned, extent, extent, extent, in_channels).astype(
        jnp.bfloat16
    )
    returned = lax.all_to_all(
        split_whole(error_hidden, depth_count, height_count),
        ("depth", "height"),
        split_axis=1,
        concat_axis=0,
        tiled=True,
    )
    error_early = (returned.astype(jnp.float32) * slope(early)).astype(jnp.bfloat16)
    grad_early = stride_grad(padded, error_early, out_depth, out_height)
    early_total, late_total = lax.psum((grad_early, grad_late), ("batch", "depth", "height"))
    return (activated, early_total, late_total)


def solution(mesh):
    return jax.shard_map(
        per_device,
        mesh=mesh,
        in_specs=(
            P("batch", "depth", "height", None, None),
            P(),
            P(),
            P(("batch", "depth", "height"), None, None, None, None),
        ),
        out_specs=(P(("batch", "depth", "height"), None, None, None, None), P(), P()),
        check_vma=False,
    )
```

profile of v0, /device:TPU:1, one launch (start us, length us, event | category | flops | bytes accessed | tf_op | source)
XLA Modules:
  0.0 313.3 jit_solution(5110627465356613806)
XLA Ops:
  7.2 1.1 fusion.29
  8.5 4.2 %collective-permute-start = (bf16[16,1,8,8,128]{4,0,3,2,1:T(8,128)(2,1)S(1)}, bf16[16,1,8,8,128]{4,0,3,2,1:T(8,128)(2,1)S(1)}, u32[]{:S(2)}, u32[]{:S(2)}) collective-permute-start(bf16[16,1,8,8,128]{4,0,3,2,1:T(8,128)(2,1)S(1)} %copy.298), channel_id=1, source_target_pairs={{0,2},{2,4},{4,6},{1,3},{3,5},{5,7},{8,10},{10,12},{12,14},{9,11},... | collective-permute-start | bytes 786440 | tf_op jit(solution)/shard_map/ppermute | solution.py:12
  12.9 1.3 collective-permute-start.1
  17.7 1.3 constant_dynamic-update-slice_fusion.1
  19.0 2.6 collective-permute-done.1
  22.4 5.3 %collective-permute-start.2 = (bf16[16,6,1,8,128]{4,0,3,2,1:T(8,128)(2,1)}, bf16[16,6,1,8,128]{4,0,3,2,1:T(8,128)(2,1)}, u32[]{:S(2)}, u32[]{:S(2)}) collective-permute-start(bf16[16,6,1,8,128]{4,0,3,2,1:T(8,128)(2,1)} %get-tuple-element.21), channel_id=1, source_target_pairs={{0,1},{2,3},{4,5},{6,7},{8,9},{10,11},{12,13},{14,15},{16,17},{18,... | collective-permute-start | bytes 589832 | tf_op jit(solution)/shard_map/ppermute | solution.py:12
  27.8 1.3 collective-permute-start.3
  32.9 1.0 pad_maximum_fusion.2
  33.9 2.1 collective-permute-done.3
  36.0 1.8 fusion.5
  37.8 1.0 fusion.27
  62.5 5.9 %all-to-all-start = ((bf16[16,2,4,8,128]{4,3,2,1,0:T(8,128)(2,1)}), bf16[16,2,4,8,128]{4,3,2,1,0:T(8,128)(2,1)S(1)}, u32[]{:S(2)}, u32[]{:S(2)}) async-start(bf16[16,2,4,8,128]{4,3,2,1,0:T(8,128)(2,1)} %multiply_convert_fusion.2), calls=%async_computation | async-start | bytes 524288 | tf_op jit(solution)/shard_map/all_to_all | solution.py:129
  71.5 4.5 %all-to-all-done = bf16[16,2,4,8,128]{4,3,2,1,0:T(8,128)(2,1)S(1)} async-done(((bf16[16,2,4,8,128]{4,3,2,1,0:T(8,128)(2,1)}), bf16[16,2,4,8,128]{4,3,2,1,0:T(8,128)(2,1)S(1)}, u32[]{:S(2)}, u32[]{:S(2)}) %all-to-all-start) | async-done | bytes 262176 | tf_op jit(solution)/shard_map/all_to_all | solution.py:129
  80.5 1.0 fusion.8
  86.0 2.5 pad_slice_fusion.2
  88.5 1.4 pad_slice_fusion.1
  89.9 1.2 copy.235
  91.1 2.4 copy.236
  93.5 1.0 convolution_bitcast_fusion.8
  94.6 2.2 convolution_bitcast_fusion.7
  97.0 1.0 convolution_bitcast_fusion.6
  98.4 1.1 convolution_bitcast_fusion.5
  99.7 1.1 convolution_bitcast_fusion.4
  101.1 1.1 convolution_bitcast_fusion.3
  102.4 1.0 convolution_bitcast_fusion.2
  115.0 3.4 %all-to-all-start.1 = ((bf16[2,16,4,8,128]{4,3,2,0,1:T(8,128)(2,1)}), bf16[2,16,4,8,128]{4,3,2,0,1:T(8,128)(2,1)S(1)}, u32[]{:S(2)}, u32[]{:S(2)}) async-start(bf16[2,16,4,8,128]{4,3,2,0,1:T(8,128)(2,1)} %copy.216), calls=%async_computation.1 | async-start | bytes 524288 | tf_op jit(solution)/shard_map/all_to_all | solution.py:181
  118.7 1.4 pad_maximum_fusion.1
  120.1 5.9 %all-to-all-done.1 = bf16[2,16,4,8,128]{4,3,2,0,1:T(8,128)(2,1)S(1)} async-done(((bf16[2,16,4,8,128]{4,3,2,0,1:T(8,128)(2,1)}), bf16[2,16,4,8,128]{4,3,2,0,1:T(8,128)(2,1)S(1)}, u32[]{:S(2)}, u32[]{:S(2)}) %all-to-all-start.1) | async-done | bytes 262176 | tf_op jit(solution)/shard_map/all_to_all | solution.py:181
  143.9 1.5 pad_maximum_fusion
  145.4 156.3 %all-reduce.6.cloned.1.call-done = (f32[4,4,4,64,128]{4,3,2,1,0:T(8,128)}, f32[3,3,3,128,128]{4,3,2,1,0:T(8,128)}) async-done(((f32[4,4,4,64,128]{4,3,2,1,0:T(8,128)}, f32[3,3,3,128,128]{4,3,2,1,0:T(8,128)}), (f32[4,4,4,64,128]{4,3,2,1,0:T(8,128)}, f32[3,3,3,128,128]{4,3,2,1,0:T(8,128)})) %all-reduce.6.cloned.1.call-update) | async-done | bytes 3866640 | tf_op jit(solution)/shard_map/psum | solution.py:190
  301.7 3.3 %copy.304 = f32[4,4,4,64,128]{4,3,2,1,0:T(8,128)} copy(f32[4,4,4,64,128]{4,3,2,1,0:T(8,128)} %get-tuple-element.213) | data formatting | bytes 4194304
  305.0 1.2 copy.305
  (427 shorter events, 73.4 us)
Async XLA Ops:
  7.2 7.0 %copy-start.72 = (bf16[3,3,3,128,128]{4,3,2,1,0:T(8,128)(2,1)S(1)}, bf16[3,3,3,128,128]{4,3,2,1,0:T(8,128)(2,1)}, u32[]{:S(2)}) copy-start(bf16[3,3,3,128,128]{4,3,2,1,0:T(8,128)(2,1)} %param.6) | copy-start | bytes 2654212
  8.5 7.9 %copy-start.45 = (bf16[4,4,4,64,128]{4,3,2,1,0:T(8,128)(2,1)S(1)}, bf16[4,4,4,64,128]{4,3,2,1,0:T(8,128)(2,1)}, u32[]{:S(2)}) copy-start(bf16[4,4,4,64,128]{4,3,2,1,0:T(8,128)(2,1)} %param.5) | copy-start | bytes 3145732
  8.5 9.1 %collective-permute-start = (bf16[16,1,8,8,128]{4,0,3,2,1:T(8,128)(2,1)S(1)}, bf16[16,1,8,8,128]{4,0,3,2,1:T(8,128)(2,1)S(1)}, u32[]{:S(2)}, u32[]{:S(2)}) collective-permute-start(bf16[16,1,8,8,128]{4,0,3,2,1:T(8,128)(2,1)S(1)} %copy.298), channel_id=1, source_target_pairs={{0,2},{2,4},{4,6},{1,3},{3,5},{5,7},{8,10},{10,12},{12,14},{9,11},... | collective-permute-start | bytes 786440 | tf_op jit(solution)/shard_map/ppermute | solution.py:12
  12.9 8.8 %collective-permute-start.1 = (bf16[16,1,8,8,128]{4,0,3,2,1:T(8,128)(2,1)S(1)}, bf16[16,1,8,8,128]{4,0,3,2,1:T(8,128)(2,1)S(1)}, u32[]{:S(2)}, u32[]{:S(2)}) collective-permute-start(bf16[16,1,8,8,128]{4,0,3,2,1:T(8,128)(2,1)S(1)} %copy.299), channel_id=1, source_target_pairs={{2,0},{4,2},{6,4},{3,1},{5,3},{7,5},{10,8},{12,10},{14,12},{11,9},... | collective-permute-start | bytes 786440 | tf_op jit(solution)/shard_map/ppermute | solution.py:15
  15.0 2.7 copy-start.79
  15.0 2.7 copy-start.81
  15.0 2.7 copy-start.83
  15.0 2.7 copy-start.94
  15.0 14.1 %copy-start.85 = (bf16[1,1,3,128,128]{4,3,2,1,0:T(8,128)(2,1)}, bf16[1,1,3,128,128]{4,3,2,1,0:T(8,128)(2,1)S(1)}, u32[]{:S(2)}) copy-start(bf16[1,1,3,128,128]{4,3,2,1,0:T(8,128)(2,1)S(1)} %get-tuple-element.36) | copy-start | bytes 294916
  15.8 1.9 copy-start.11
  17.7 12.2 %copy-start.100 = (bf16[3,128,128]{1,2,0:T(8,128)(2,1)S(1)}, bf16[3,128,128]{1,2,0:T(8,128)(2,1)}, u32[]{:S(2)}) copy-start(bf16[3,128,128]{1,2,0:T(8,128)(2,1)} %get-tuple-element.211) | copy-start | bytes 294916
  17.7 12.9 %copy-start.99 = (bf16[3,128,128]{1,2,0:T(8,128)(2,1)S(1)}, bf16[3,128,128]{1,2,0:T(8,128)(2,1)}, u32[]{:S(2)}) copy-start(bf16[3,128,128]{1,2,0:T(8,128)(2,1)} %get-tuple-element.210) | copy-start | bytes 294916
  19.0 12.4 %copy-start.98 = (bf16[3,128,128]{1,2,0:T(8,128)(2,1)S(1)}, bf16[3,128,128]{1,2,0:T(8,128)(2,1)}, u32[]{:S(2)}) copy-start(bf16[3,128,128]{1,2,0:T(8,128)(2,1)} %get-tuple-element.209) | copy-start | bytes 294916
  19.0 13.1 %copy-start.97 = (bf16[3,128,128]{1,2,0:T(8,128)(2,1)S(1)}, bf16[3,128,128]{1,2,0:T(8,128)(2,1)}, u32[]{:S(2)}) copy-start(bf16[3,128,128]{1,2,0:T(8,128)(2,1)} %get-tuple-element.208) | copy-start | bytes 294916
  22.4 11.5 %collective-permute-start.2 = (bf16[16,6,1,8,128]{4,0,3,2,1:T(8,128)(2,1)}, bf16[16,6,1,8,128]{4,0,3,2,1:T(8,128)(2,1)}, u32[]{:S(2)}, u32[]{:S(2)}) collective-permute-start(bf16[16,6,1,8,128]{4,0,3,2,1:T(8,128)(2,1)} %get-tuple-element.21), channel_id=1, source_target_pairs={{0,1},{2,3},{4,5},{6,7},{8,9},{10,11},{12,13},{14,15},{16,17},{18,... | collective-permute-start | bytes 589832 | tf_op jit(solution)/shard_map/ppermute | solution.py:12
  27.8 8.2 %collective-permute-start.3 = (bf16[16,6,1,8,128]{4,0,3,2,1:T(8,128)(2,1)}, bf16[16,6,1,8,128]{4,0,3,2,1:T(8,128)(2,1)}, u32[]{:S(2)}, u32[]{:S(2)}) collective-permute-start(bf16[16,6,1,8,128]{4,0,3,2,1:T(8,128)(2,1)} %get-tuple-element.22), channel_id=1, source_target_pairs={{1,0},{3,2},{5,4},{7,6},{9,8},{11,10},{13,12},{15,14},{17,16},{19,... | collective-permute-start | bytes 589832 | tf_op jit(solution)/shard_map/ppermute | solution.py:15
  60.5 7.9 %copy-start.75 = (bf16[1,1,3,128,128]{4,3,2,1,0:T(8,128)(2,1)S(1)}, bf16[1,1,3,128,128]{4,3,2,1,0:T(8,128)(2,1)}, u32[]{:S(2)}) copy-start(bf16[1,1,3,128,128]{4,3,2,1,0:T(8,128)(2,1)} %get-tuple-element.30) | copy-start | bytes 294916
  60.5 7.9 %copy-start.77 = (bf16[1,1,3,128,128]{4,3,2,1,0:T(8,128)(2,1)S(1)}, bf16[1,1,3,128,128]{4,3,2,1,0:T(8,128)(2,1)}, u32[]{:S(2)}) copy-start(bf16[1,1,3,128,128]{4,3,2,1,0:T(8,128)(2,1)} %get-tuple-element.31) | copy-start | bytes 294916
  60.5 9.5 %copy-start.73 = (bf16[1,1,3,128,128]{4,3,2,1,0:T(8,128)(2,1)S(1)}, bf16[1,1,3,128,128]{4,3,2,1,0:T(8,128)(2,1)}, u32[]{:S(2)}) copy-start(bf16[1,1,3,128,128]{4,3,2,1,0:T(8,128)(2,1)} %get-tuple-element.37) | copy-start | bytes 294916
  62.5 13.5 %all-to-all-start = ((bf16[16,2,4,8,128]{4,3,2,1,0:T(8,128)(2,1)}), bf16[16,2,4,8,128]{4,3,2,1,0:T(8,128)(2,1)S(1)}, u32[]{:S(2)}, u32[]{:S(2)}) async-start(bf16[16,2,4,8,128]{4,3,2,1,0:T(8,128)(2,1)} %multiply_convert_fusion.2), calls=%async_computation | async-start | bytes 524288 | tf_op jit(solution)/shard_map/all_to_all | solution.py:129
  91.1 2.4 copy-start.10
  113.8 4.7 %copy-start.87 = (f32[1,3,128,128]{3,2,1,0:T(8,128)S(1)}, f32[1,3,128,128]{3,2,1,0:T(8,128)}, u32[]{:S(2)}) copy-start(f32[1,3,128,128]{3,2,1,0:T(8,128)} %convolution_bitcast_fusion.8) | copy-start | bytes 589828
  113.8 4.7 %copy-start.88 = (f32[1,3,128,128]{3,2,1,0:T(8,128)S(1)}, f32[1,3,128,128]{3,2,1,0:T(8,128)}, u32[]{:S(2)}) copy-start(f32[1,3,128,128]{3,2,1,0:T(8,128)} %convolution_bitcast_fusion.7) | copy-start | bytes 589828
  113.8 4.7 %copy-start.89 = (f32[1,3,128,128]{3,2,1,0:T(8,128)S(1)}, f32[1,3,128,128]{3,2,1,0:T(8,128)}, u32[]{:S(2)}) copy-start(f32[1,3,128,128]{3,2,1,0:T(8,128)} %convolution_bitcast_fusion.6) | copy-start | bytes 589828
  114.2 4.3 %copy-start.90 = (f32[1,3,128,128]{3,2,1,0:T(8,128)S(1)}, f32[1,3,128,128]{3,2,1,0:T(8,128)}, u32[]{:S(2)}) copy-start(f32[1,3,128,128]{3,2,1,0:T(8,128)} %convolution_bitcast_fusion.5) | copy-start | bytes 589828
  114.2 4.3 %copy-start.91 = (f32[1,3,128,128]{3,2,1,0:T(8,128)S(1)}, f32[1,3,128,128]{3,2,1,0:T(8,128)}, u32[]{:S(2)}) copy-start(f32[1,3,128,128]{3,2,1,0:T(8,128)} %convolution_bitcast_fusion.4) | copy-start | bytes 589828
  114.2 4.3 %copy-start.92 = (f32[1,3,128,128]{3,2,1,0:T(8,128)S(1)}, f32[1,3,128,128]{3,2,1,0:T(8,128)}, u32[]{:S(2)}) copy-start(f32[1,3,128,128]{3,2,1,0:T(8,128)} %convolution_bitcast_fusion.3) | copy-start | bytes 589828
  114.3 4.4 %copy-start.93 = (f32[1,3,128,128]{3,2,1,0:T(8,128)S(1)}, f32[1,3,128,128]{3,2,1,0:T(8,128)}, u32[]{:S(2)}) copy-start(f32[1,3,128,128]{3,2,1,0:T(8,128)} %convolution_bitcast_fusion.2) | copy-start | bytes 589828
  115.0 11.0 %all-to-all-start.1 = ((bf16[2,16,4,8,128]{4,3,2,0,1:T(8,128)(2,1)}), bf16[2,16,4,8,128]{4,3,2,0,1:T(8,128)(2,1)S(1)}, u32[]{:S(2)}, u32[]{:S(2)}) async-start(bf16[2,16,4,8,128]{4,3,2,0,1:T(8,128)(2,1)} %copy.216), calls=%async_computation.1 | async-start | bytes 524288 | tf_op jit(solution)/shard_map/all_to_all | solution.py:181
  118.4 183.3 %all-reduce.6.cloned.1.call-start = ((), (), s32[]{:S(2)}) async-start(), calls=%async_computation.2 | async-start | bytes 7733248 | tf_op jit(solution)/shard_map/psum | solution.py:190
  120.1 6.1 %copy-start.8 = (f32[1024,128]{1,0:T(8,128)S(1)}, f32[1024,128]{1,0:T(8,128)}, u32[]{:S(2)}) copy-start(f32[1024,128]{1,0:T(8,128)} %copy-done.7) | copy-start | bytes 1572868
  301.7 3.3 %copy-start.44 = (f32[3,3,3,128,128]{4,3,2,1,0:T(8,128)S(1)}, f32[3,3,3,128,128]{4,3,2,1,0:T(8,128)}, u32[]{:S(2)}) copy-start(f32[3,3,3,128,128]{4,3,2,1,0:T(8,128)} %get-tuple-element.214) | copy-start | bytes 5308420
  (85 other events, 89.1 us)
Sparse Core Ops, SparseCore 0:
  145.6 156.1 all-reduce.5
where the time goes:
time: 318 us; the launch traced here: 313 us
  waiting for transfers between devices  172 us (54%)
  local copies, waits for them, and re-layouts  62.7 us (20%)
  matrix products  27.1 us (9%)
  starting transfers between devices  21.5 us (7%)
  between operations  16.4 us (5%)
  other arithmetic  13.8 us (4%)
    psum x1, waiting for transfers between devices, per_device(): lax.psum((grad_early, grad_late), ('batch', 'depth', 'height'))  156 us
    unnamed x226, local copies, waits for them, and re-layouts  33.3 us
    ppermute x2, starting transfers between devices, padded_2(): lax.ppermute(lax.slice_in_dim(block, block.shape[dim] - width, None, axis...  9.49 us
    dot_general x9, matrix products, per_device(): lax.dot_general(operand.reshape(-1, 3 * in_channels), flat_error, (((0,),...  9.22 us
    transpose x14, local copies, waits for them, and re-layouts, per_device(): jnp.swapaxes(conv_late[depth_tap, height_tap, ::-1], 1, 2)  8.23 us
  transfers between devices with their start and end apart: 7, of which 6 were waited for; matrix products, arithmetic and copies ran while one was open for 4% of the time, Pallas kernels for 0%

commit v1 on v0

v1 whole, which is shorter than its diff:
```python
import jax
import jax.numpy as jnp
from jax import lax
from jax.experimental import pallas as pl
from jax.experimental.pallas import tpu as pltpu
from jax.sharding import PartitionSpec as P

FINE = ("xl", "z", "core", "y", "xh")
BF16 = jnp.bfloat16
F32 = jnp.float32
SIDE = 8
LANES = 128
CELLS = SIDE * SIDE * 16
HALF = 4 * 4 * 4 * 64 // 2
HALF_LATE = 3 * 3 * 3 * 128 // 2
GRANULE = HALF_LATE // 9
SHARE = HALF // 64
RING = 4


def shifted(rows, by, lane=None):
    moved = pltpu.roll(rows, by % SIDE, 1)
    width = lax.broadcasted_iota(jnp.int32, rows.shape, 1)
    return jnp.where(width == (0 if by == 1 else SIDE - 1), 0.0, moved)


def three_widths(rows):
    return jnp.concatenate([shifted(rows, 1), rows, shifted(rows, -1)], axis=-1)


def clear_rim(ref, size):
    lanes = ref.shape[-1]
    slab = jnp.zeros((size, 16, lanes), BF16)
    ref[0] = slab
    ref[size - 1] = slab
    ref[:, 0] = slab
    ref[:, size - 1] = slab


def cube_conv(field, blocks, total):
    def product(first, count, weights, transposed):
        rows = jnp.concatenate([field[first : first + count, kh : kh + SIDE] for kh in range(3)], axis=-1)
        dims = (((1,), (1 if transposed else 0,)), ((), ()))
        return lax.dot_general(
            rows.reshape(count * LANES, 9 * LANES), weights, dims, preferred_element_type=F32
        )

    (first, transposed), (second, _), (third, _) = (blocks(kd) for kd in range(3))
    two = product(0, 9, jnp.concatenate([first, second], axis=0 if transposed else 1), transposed)
    total[...] = two[0:CELLS, 0:LANES] + two[LANES : LANES + CELLS, LANES:]
    total[...] += product(2, SIDE, third, transposed)


def early_kernel(received, conv_early, hidden, volume, slope_early, total):
    depth_blocks, height_blocks = 4, 2
    blank = jnp.zeros((9, 16, 2 * LANES), BF16)
    for dp in range(2):
        for hp in range(2):
            volume[2 * dp + hp, 0 if dp else 8] = blank
            volume[2 * dp + hp, :, 0 if hp else 8] = blank

    for block in range(depth_blocks * height_blocks):
        db, hb = divmod(block, height_blocks)
        for layer in range(4):
            half, dp = layer // 2, layer % 2
            samples = [
                received[block, s, layer].astype(F32).reshape(4, 2, SIDE, LANES) for s in range(2)
            ]
            for hp in range(2):
                centre = jnp.stack([x[:, hp] for x in samples], axis=1).reshape(8, SIDE, LANES)
                lane = lax.broadcasted_iota(jnp.int32, centre.shape, 2)
                sides = jnp.where(lane < LANES // 2, shifted(centre, -1), shifted(centre, 1))
                both = jnp.concatenate([centre, sides], axis=-1).reshape(4, 16, 2 * LANES)
                volume[2 * dp + hp, 2 * db + half + dp, 4 * hb + hp : 4 * hb + hp + 4] = both.astype(
                    BF16
                )

    def early_taps(kd, kh):
        tap = 4 * kd + kh
        return jnp.concatenate([conv_early[tap, 64:256], conv_early[tap, 0:64]], axis=0)

    for dp in range(2):
        rows = jnp.concatenate(
            [volume[2 * dp + (kh + 1) % 2, :, kh // 2 : kh // 2 + SIDE] for kh in range(4)], axis=-1
        )
        weights = [
            jnp.concatenate([early_taps(kd, kh) for kh in range(4)], axis=0) for kd in (1 - dp, 3 - dp)
        ]
        two = jnp.dot(
            rows.reshape(9 * LANES, 8 * LANES),
            jnp.concatenate(weights, axis=1),
            preferred_element_type=F32,
        )
        both = two[0:CELLS, 0:LANES] + two[LANES : LANES + CELLS, LANES:]
        if dp:
            total[...] += both
        else:
            total[...] = both

    clear_rim(hidden, 10)
    for d in range(SIDE):
        rows = pl.ds(d * LANES, LANES)
        early = total[rows]
        sigma = jax.nn.sigmoid(early)
        slope_early[rows] = sigma * (1.0 + early * (1.0 - sigma))
        value = (early * sigma).reshape(16, SIDE, LANES)
        hidden[d + 1, 1:9] = three_widths(value).reshape(SIDE, 16, 3 * LANES).astype(BF16)


def late_kernel(
    core, hidden, conv_late, cotangent, activated, kept, sent, error, hidden_t, total, grads
):
    def late_block(kd):
        return conv_late[3 * kd : 3 * kd + 3].reshape(9 * LANES, LANES), False

    cube_conv(hidden, late_block, total)

    clear_rim(error, 10)
    for d in range(SIDE):
        rows = pl.ds(d * LANES, LANES)
        late = total[rows]
        sigma = jax.nn.sigmoid(late)
        out = (late * sigma).reshape(SIDE, 2, SIDE, LANES)
        for s in range(2):
            activated[s, d] = out[:, s].reshape(SIDE * SIDE, LANES).astype(BF16)
        value = (cotangent[rows].astype(F32) * (sigma * (1.0 + late * (1.0 - sigma)))).reshape(16, SIDE, LANES)
        error[d + 1, 1:9] = three_widths(value).reshape(SIDE, 16, 3 * LANES).astype(BF16)

    grads[:, HALF_LATE:] = jnp.zeros((2, HALF - HALF_LATE, LANES), BF16)
    for d in range(SIDE):
        hidden_t[:, d * LANES : (d + 1) * LANES] = hidden[d + 1, 1:9].reshape(LANES, 3 * LANES).T

    for kh in range(3):
        for depth_taps in ((0, 1), (2,)):
            moved = [
                error[2 - kd : 10 - kd, 2 - kh : 10 - kh, :, LANES : 2 * LANES].reshape(CELLS, LANES)
                for kd in depth_taps
            ]
            side = moved[0] if len(moved) == 1 else jnp.concatenate(moved, axis=1)
            grad = jnp.dot(hidden_t[...], side, preferred_element_type=F32).astype(BF16)
            for column, kd in enumerate(depth_taps):
                for part in range(2):
                    half, granule = divmod(2 * (3 * kd + kh) + part, 9)
                    grads[
                        jnp.where(core[0] == half, 0, 1), granule * GRANULE : (granule + 1) * GRANULE
                    ] = grad[part * GRANULE : (part + 1) * GRANULE, column * LANES : (column + 1) * LANES]
    kept[...] = grads[0]
    sent[...] = grads[1]


def backward_kernel(
    core, conv_late, volume, error, slope_early, kept, sent, volume_t, error_early, total, grads
):
    clear_rim(error_early, 10)

    def back_block(kd):
        taps = [
            conv_late[3 * (2 - kd) + 2 - kh, (2 - kw) * LANES : (3 - kw) * LANES]
            for kh in range(3)
            for kw in range(3)
        ]
        return jnp.concatenate(taps, axis=1), True

    cube_conv(error, back_block, total)

    for d in range(SIDE):
        rows = pl.ds(d * LANES, LANES)
        value = total[rows].astype(BF16).astype(F32) * slope_early[rows]
        error_early[d + 1, 1:9] = value.astype(BF16).reshape(SIDE, 16, LANES)

    for phase in range(4):
        dp, hp = phase // 2, phase % 2
        for d in range(SIDE):
            volume_t[phase, :, d * LANES : (d + 1) * LANES] = (
                volume[phase, d + dp, hp : hp + SIDE].reshape(LANES, 2 * LANES).T
            )
    for phase in range(4):
        dp, hp = phase // 2, phase % 2
        for first in range(2):
            depth = dp + 1 - first
            moved = [
                error_early[depth : depth + SIDE, hp + 1 - second : hp + 1 - second + SIDE].reshape(
                    CELLS, LANES
                )
                for second in range(2)
            ]
            grad = jnp.dot(
                volume_t[phase], jnp.concatenate(moved, axis=1), preferred_element_type=F32
            ).astype(BF16)
            keep = jnp.where(core[0] == first, 0, 1)
            for second in range(2):
                tap = 4 * (2 * first + 1 - dp) + 2 * second + 1 - hp
                lanes = slice(second * LANES, (second + 1) * LANES)
                at = (tap - 8 * first) * 2 * LANES
                grads[keep, at + 64 : at + 256] = grad[0:192, lanes]
                grads[keep, at : at + 64] = grad[192:256, lanes]
    kept[...] = grads[0]
    sent[...] = grads[1]


VMEM = pl.BlockSpec(memory_space=pltpu.VMEM)
SMEM = pl.BlockSpec(memory_space=pltpu.SMEM)
ANY = pl.BlockSpec(memory_space=pl.ANY)
SMALL = pltpu.CompilerParams(vmem_limit_bytes=12 * 1024 * 1024)
LIMIT = pltpu.CompilerParams(vmem_limit_bytes=24 * 1024 * 1024)
VOLUME = (4, 9, 9, 16, 2 * LANES)
FIELD = (10, 10, 16, 3 * LANES)


HALF_ROWS = jax.ShapeDtypeStruct((HALF, LANES), BF16)


def cost(products, transcendentals=0):
    return pl.CostEstimate(
        flops=2 * CELLS * LANES * products,
        bytes_accessed=8 * 1024 * 1024,
        transcendentals=transcendentals,
    )


def early_layer(received, conv_early):
    return pl.pallas_call(
        early_kernel,
        out_shape=(
            jax.ShapeDtypeStruct(FIELD, BF16),
            jax.ShapeDtypeStruct(VOLUME, BF16),
            jax.ShapeDtypeStruct((CELLS, LANES), F32),
        ),
        in_specs=[VMEM, VMEM],
        out_specs=(VMEM,) * 3,
        scratch_shapes=[pltpu.VMEM((CELLS, LANES), F32)],
        compiler_params=LIMIT,
        cost_estimate=cost(16 * 256, CELLS * LANES),
    )(received, conv_early)


def late_layer(core, hidden, conv_late, cotangent):
    return pl.pallas_call(
        late_kernel,
        out_shape=(
            jax.ShapeDtypeStruct((2, SIDE, SIDE * SIDE, LANES), BF16),
            HALF_ROWS,
            HALF_ROWS,
            jax.ShapeDtypeStruct(FIELD, BF16),
        ),
        in_specs=[SMEM, VMEM, VMEM, VMEM],
        out_specs=(VMEM,) * 4,
        scratch_shapes=[
            pltpu.VMEM((3 * LANES, CELLS), BF16),
            pltpu.VMEM((CELLS, LANES), F32),
            pltpu.VMEM((2, HALF, LANES), BF16),
        ],
        compiler_params=LIMIT,
        cost_estimate=cost(2 * 27 * LANES, CELLS * LANES),
    )(core, hidden, conv_late, cotangent)


def backward(core, conv_late, volume, error, slope_early):
    return pl.pallas_call(
        backward_kernel,
        out_shape=(HALF_ROWS, HALF_ROWS),
        in_specs=[SMEM, VMEM, VMEM, VMEM, VMEM],
        out_specs=(VMEM, VMEM),
        scratch_shapes=[
            pltpu.VMEM((4, 2 * LANES, CELLS), BF16),
            pltpu.VMEM((10, 10, 16, LANES), BF16),
            pltpu.VMEM((CELLS, LANES), F32),
            pltpu.VMEM((2, HALF, LANES), BF16),
        ],
        compiler_params=LIMIT,
        cost_estimate=cost(16 * 256 + 27 * LANES),
    )(core, conv_late, volume, error, slope_early)


def ring_place(core):
    return jnp.where(core == 0, lax.axis_index("z"), lax.axis_index("y"))


def chip_routes():
    shifts = [[], [], [], []]
    planes = {}
    for xl in range(2):
        for z in range(RING):
            for core in range(2):
                for y in range(RING):
                    for xh in range(2):
                        index = lambda z, y: (((xl * RING + z) * 2 + core) * RING + y) * 2 + xh
                        for by, pairs in enumerate(shifts):
                            to = ((z + by) % RING, y) if core == 0 else (z, (y + by) % RING)
                            pairs.append((index(z, y), index(*to)))
                        planes.setdefault((core, z if core == 0 else y), []).append(index(z, y))
    return shifts, [planes[key] for key in sorted(planes)]


def pair_kernel(place, early, early_other, late, late_other, *blocks):
    rows = HALF // RING
    for n, block in enumerate(blocks):
        start = ((place[0] + n) % RING) * rows
        for kept, other, first in ((early, early_other, 0), (late, late_other, SHARE)):
            part = pl.ds(pl.multiple_of(start, rows), rows)
            value = (kept[part].astype(F32) + other[part].astype(F32)).astype(BF16)
            block[:, first : first + SHARE] = value.reshape(16, SHARE, LANES)


def pair_sums(place, early, early_other, late, late_other):
    block = jax.ShapeDtypeStruct((16, 2 * SHARE, LANES), BF16)
    return pl.pallas_call(
        pair_kernel,
        out_shape=(block,) * RING,
        in_specs=[SMEM] + [VMEM] * 4,
        out_specs=(VMEM,) * RING,
        compiler_params=SMALL,
        cost_estimate=pl.CostEstimate(flops=0, bytes_accessed=4 * 1024 * 1024, transcendentals=0),
    )(place.reshape(1), early, early_other, late, late_other)


def swapped(block):
    return lax.ppermute(block, "core", [(0, 1), (1, 0)])


def summed(core, early, early_other, late, late_other):
    shifts, planes = chip_routes()
    exchange = lambda blocks, groups: lax.all_to_all(
        blocks, FINE, split_axis=0, concat_axis=0, axis_index_groups=groups, tiled=True
    )
    blocks = pair_sums(ring_place(core), early, early_other, late, late_other)
    total = blocks[0].astype(F32)
    for by in range(1, RING):
        total += lax.ppermute(blocks[by], FINE, shifts[by]).astype(F32)
    shares = exchange(total.astype(BF16), planes)
    share = jnp.sum(shares.astype(F32), axis=0).astype(BF16)
    wholes = [sum(planes[core * RING : (core + 1) * RING], []) for core in range(2)]
    return exchange(jnp.broadcast_to(share[None], (64,) + share.shape), wholes)


def place_kernel(half, shares, *refs):
    early, late, wide_early, wide_late, sems = refs[-5:]
    copies = []
    for chunk in range(4):
        for n in range(16 * chunk, 16 * (chunk + 1)):
            at = n * SHARE
            wide_early[at : at + SHARE] = shares[n, :SHARE].astype(F32)
            if at < HALF_LATE:
                wide_late[at : at + SHARE] = shares[n, SHARE:].astype(F32)
        low, high = 16 * chunk * SHARE, 16 * (chunk + 1) * SHARE
        for wide, out, rows, sem in ((wide_early, early, HALF, 0), (wide_late, late, HALF_LATE, 4)):
            size = min(high, rows) - low
            start = pl.multiple_of(half[0] * rows + low, 8)
            copy = pltpu.make_async_copy(
                wide.at[pl.ds(low, size)], out.at[pl.ds(start, size)], sems.at[sem + chunk]
            )
            copy.start()
            copies.append(copy)
    for copy in copies:
        copy.wait()


def placed(half, shares, so_far=()):
    return pl.pallas_call(
        place_kernel,
        out_shape=(
            jax.ShapeDtypeStruct((2 * HALF, LANES), F32),
            jax.ShapeDtypeStruct((2 * HALF_LATE, LANES), F32),
        ),
        in_specs=[SMEM, VMEM] + [ANY] * len(so_far),
        out_specs=(ANY, ANY),
        input_output_aliases={2 + n: n for n in range(len(so_far))},
        scratch_shapes=[
            pltpu.VMEM((HALF, LANES), F32),
            pltpu.VMEM((HALF_LATE, LANES), F32),
            pltpu.SemaphoreType.DMA((8,)),
        ],
        compiler_params=SMALL,
        cost_estimate=pl.CostEstimate(flops=0, bytes_accessed=3 * 1024 * 1024, transcendentals=0),
    )(half.reshape(1), shares, *so_far)


def per_device(inputs, conv_early, conv_late, cotangent):
    owned = cotangent.shape[0]
    core = lax.axis_index("core")
    sent = inputs.reshape(inputs.shape[0] // owned, owned, inputs.shape[1], SIDE * SIDE, LANES)
    received = lax.all_to_all(sent, ("y", "xh"), split_axis=0, concat_axis=0, tiled=True)
    signal = cotangent.reshape(owned, SIDE * SIDE, SIDE, LANES).swapaxes(0, 1).reshape(CELLS, LANES)
    taps_late = conv_late.reshape(9, 3 * LANES, LANES)
    hidden, volume, slope_early = early_layer(received, conv_early.reshape(16, 2 * LANES, LANES))
    activated, late, late_sent, error = late_layer(core.reshape(1), hidden, taps_late, signal)
    late_other = swapped(late_sent)
    early, early_sent = backward(core.reshape(1), taps_late, volume, error, slope_early)
    shares = summed(core, early, swapped(early_sent), late, late_other)
    other = swapped(shares)
    early_total, late_total = placed(1 - core, other, placed(core, shares))
    return (
        activated.reshape(cotangent.shape),
        early_total.reshape(conv_early.shape),
        late_total.reshape(conv_late.shape),
    )


def solution(mesh):
    fine = jax.sharding.Mesh(mesh.devices.reshape(2, 4, 2, 4, 2), FINE)
    batch = ("xl", "z", "core")
    every = FINE
    return jax.shard_map(
        per_device,
        mesh=fine,
        in_specs=(
            P(batch, "y", "xh", None, None),
            P(),
            P(),
            P(every, None, None, None, None),
        ),
        out_specs=(P(every, None, None, None, None), P(), P()),
        check_vma=False,
    )
```

time: 318 us -> 89.9 us (0.28); the launches traced: 313 us -> 89.6 us
  waiting for transfers between devices: 172 us -> 26.6 us
  local copies, waits for them, and re-layouts: 62.7 us -> 0.3 us
  blocking collectives: 0 us -> 34.7 us
  matrix products: 27.1 us -> 0 us
  between operations: 16.4 us -> 0.71 us
  other arithmetic: 13.8 us -> 0.21 us
  Pallas kernels: 0 us -> 11.1 us
  starting transfers between devices: 21.5 us -> 16 us
    psum x1 -> x0, waiting for transfers between devices: 156 us -> none  [per_device(): lax.psum((grad_early, grad_late), ('batch', 'depth', 'height'))]
    all_to_all x0 -> x2, blocking collectives: none -> 34.7 us  [summed(): lax.all_to_all(blocks, FINE, split_axis=0, concat_axis=0, axis_index_grou...]
    unnamed x226 -> x6, local copies, waits for them, and re-layouts: 33.3 us -> 0.01 us
    dot_general x59 -> x0, matrix products: 27.1 us -> none  [the longest x9 9.22 us: per_device(): lax.dot_general(operand.reshape(-1, 3 * in_channels), flat_error, (((0,),...]
    slice x32 -> x0, local copies, waits for them, and re-layouts: 11.2 us -> none  [the longest x4 5.24 us: cube_taps(): layers[:, :, :, width_tap:width_tap + extent]]
    pallas_call x0 -> x6, Pallas kernels: none -> 11.1 us  [the longest x1 3.48 us: backward(): pl.pallas_call(backward_kernel, out_shape=(HALF_ROWS, HALF_ROWS), in_spec...]
    transpose x15 -> x0, local copies, waits for them, and re-layouts: 8.25 us -> none  [the longest x14 8.23 us: per_device(): jnp.swapaxes(conv_late[depth_tap, height_tap, ::-1], 1, 2)]
    concatenate x35 -> x0, other arithmetic: 7.39 us -> none  [the longest x16 2.7 us: stride_taps(): jnp.concatenate([layers[:, :, :, 1:1 + pair_count], layers[:, :, :, 0:pai...]
  transfers between devices with their start and end apart: 7 -> 7, of which waited for: 6 -> 6; matrix products, arithmetic and copies ran while one was open for 4% -> 0% of each run, Pallas kernels for 0% -> 1%
where the time goes in v1:
time: 89.9 us; the launch traced here: 89.6 us
  blocking collectives  34.7 us (39%)
  waiting for transfers between devices  26.6 us (30%)
  starting transfers between devices  16 us (18%)
  Pallas kernels  11.1 us (12%)
    all_to_all x2, blocking collectives, summed(): lax.all_to_all(blocks, FINE, split_axis=0, concat_axis=0, axis_index_grou...  34.7 us
    all_to_all x1, waiting for transfers between devices, per_device(): lax.all_to_all(sent, ('y', 'xh'), split_axis=0, concat_axis=0, tiled=True)  15.9 us
    all_to_all x1, starting transfers between devices, per_device(): lax.all_to_all(sent, ('y', 'xh'), split_axis=0, concat_axis=0, tiled=True)  7.62 us
    ppermute x3, waiting for transfers between devices, summed(): total += lax.ppermute(blocks[by], FINE, shifts[by]).astype(F32)  7.48 us
    ppermute x3, starting transfers between devices, swapped(): return lax.ppermute(block, 'core', [(0, 1), (1, 0)])  5.66 us
    pallas_call x1, Pallas kernels, backward(): pl.pallas_call(backward_kernel, out_shape=(HALF_ROWS, HALF_ROWS), in_spec...  3.48 us
    pallas_call x1, Pallas kernels, late_layer(): pl.pallas_call(late_kernel, out_shape=(jax.ShapeDtypeStruct((2, SIDE, SID...  3.28 us
    ppermute x3, waiting for transfers between devices, swapped(): return lax.ppermute(block, 'core', [(0, 1), (1, 0)])  3.14 us
  transfers between devices with their start and end apart: 7, of which 6 were waited for; matrix products, arithmetic and copies ran while one was open for 0% of the time, Pallas kernels for 1%

profile of v1, /device:TPU:1, one launch (start us, length us, event | category | flops | bytes accessed | tf_op | source)
XLA Modules:
  0.0 89.6 jit_solution(12776889651367919882)
XLA Ops:
  0.6 0.0 copy-start.2
  0.6 0.0 copy-start
  0.7 7.6 %all-to-all-start = ((bf16[8,2,4,64,128]{4,3,2,1,0:T(8,128)(2,1)}), bf16[8,2,4,64,128]{4,3,2,1,0:T(8,128)(2,1)S(1)}, u32[]{:S(2)}, u32[]{:S(2)}) async-start(bf16[8,2,4,64,128]{4,3,2,1,0:T(8,128)(2,1)} %bitcast.19), calls=%async_computation | async-start | bytes 2097152 | tf_op jit(solution)/shard_map/all_to_all | solution.py:382
  8.3 0.0 copy-done.2
  8.3 15.9 %all-to-all-done.received = bf16[8,2,4,64,128]{4,3,2,1,0:T(8,128)(2,1)S(1)} async-done(((bf16[8,2,4,64,128]{4,3,2,1,0:T(8,128)(2,1)}), bf16[8,2,4,64,128]{4,3,2,1,0:T(8,128)(2,1)S(1)}, u32[]{:S(2)}, u32[]{:S(2)}) %all-to-all-start) | async-done | bytes 1048608 | tf_op jit(solution)/shard_map/all_to_all | solution.py:382
  24.3 0.0 copy-done
  24.3 0.0 copy-start.1
  24.3 1.5 %shard_map.67 = (bf16[10,10,16,384]{3,2,1,0:T(8,128)(2,1)S(1)}, bf16[4,9,9,16,256]{4,3,2,1,0:T(8,128)(2,1)S(1)}, f32[1024,128]{1,0:T(8,128)S(1)}) custom-call(bf16[8,2,4,64,128]{4,3,2,1,0:T(8,128)(2,1)S(1)} %all-to-all-done.received, bf16[16,256,128]{2,1,0:T(8,128)(2,1)S(1)} %bitcast.14), custom_call_target="tpu_custom_call" | custom-call | flops 1073741824 | bytes 8388608 | tf_op jit(solution)/shard_map/pallas_call | solution.py:222
  25.8 0.0 copy-done.1
  25.8 3.3 %shard_map.68 = (bf16[2,8,64,128]{3,2,1,0:T(8,128)(2,1)}, bf16[2048,128]{1,0:T(8,128)(2,1)S(1)}, bf16[2048,128]{1,0:T(8,128)(2,1)S(1)}, bf16[10,10,16,384]{3,2,1,0:T(8,128)(2,1)S(1)}) custom-call(s32[1]{0:T(128)} %bitcast.core.half, bf16[10,10,16,384]{3,2,1,0:T(8,128)(2,1)S(1)} %get-tuple-element.20.hidden, bf16[9,384,128]{2,1,0:T(8,128)(2,1)S(1)} %bitcast.15, ...), custom_call_target="tpu_custom_call" | custom-call | flops 1811939328 | bytes 8388608 | tf_op jit(solution)/shard_map/pallas_call | solution.py:238
  29.0 3.5 %shard_map.69 = (bf16[2048,128]{1,0:T(8,128)(2,1)S(1)}, bf16[2048,128]{1,0:T(8,128)(2,1)S(1)}) custom-call(s32[1]{0:T(128)} %bitcast.core.half, bf16[9,384,128]{2,1,0:T(8,128)(2,1)S(1)} %bitcast.16, bf16[4,9,9,16,256]{4,3,2,1,0:T(8,128)(2,1)S(1)} %get-tuple-element.22.volume, bf16[10,10,16,384]{3,2,1,0:T(8,128)(2,1)S(1)} %get-tuple-element.23.error, ...), custom_call_target="tpu_custom_call" | custom-call | flops 1979711488 | bytes 8388608 | tf_op jit(solution)/shard_map/pallas_call | solution.py:259
  32.5 2.2 %collective-permute-start = (bf16[2048,128]{1,0:T(8,128)(2,1)S(1)}, bf16[2048,128]{1,0:T(8,128)(2,1)S(1)}, u32[]{:S(2)}, u32[]{:S(2)}) collective-permute-start(bf16[2048,128]{1,0:T(8,128)(2,1)S(1)} %get-tuple-element.26), channel_id=1, source_target_pairs={{0,8},{8,0},{1,9},{9,1},{2,10},{10,2},{3,11},{11,3},{4,12},{12,4},... | collective-permute-start | bytes 1572872 | tf_op jit(solution)/shard_map/ppermute | solution.py:318
  34.7 0.1 collective-permute-start.1
  34.8 1.4 %collective-permute-done.early_other = bf16[2048,128]{1,0:T(8,128)(2,1)S(1)} collective-permute-done((bf16[2048,128]{1,0:T(8,128)(2,1)S(1)}, bf16[2048,128]{1,0:T(8,128)(2,1)S(1)}, u32[]{:S(2)}, u32[]{:S(2)}) %collective-permute-start) | collective-permute-done | bytes 524320 | tf_op jit(solution)/shard_map/ppermute | solution.py:318
  36.3 0.7 collective-permute-done.1.late_other
  37.0 0.2 shard_map.70
  37.3 0.1 collective-permute-start.2
  37.4 1.7 %collective-permute-start.3 = (bf16[16,64,128]{2,1,0:T(8,128)(2,1)S(1)}, bf16[16,64,128]{2,1,0:T(8,128)(2,1)S(1)}, u32[]{:S(2)}, u32[]{:S(2)}) collective-permute-start(bf16[16,64,128]{2,1,0:T(8,128)(2,1)S(1)} %get-tuple-element.31), channel_id=1, source_target_pairs={{0,32},{1,33},{2,34},{3,35},{4,36},{5,37},{6,38},{7,39},{8,12},{9,... | collective-permute-start | bytes 786440 | tf_op jit(solution)/shard_map/ppermute | solution.py:329
  39.1 0.9 %collective-permute-start.4 = (bf16[16,64,128]{2,1,0:T(8,128)(2,1)S(1)}, bf16[16,64,128]{2,1,0:T(8,128)(2,1)S(1)}, u32[]{:S(2)}, u32[]{:S(2)}) collective-permute-start(bf16[16,64,128]{2,1,0:T(8,128)(2,1)S(1)} %get-tuple-element.32), channel_id=1, source_target_pairs={{0,48},{1,49},{2,50},{3,51},{4,52},{5,53},{6,54},{7,55},{8,14},{9,... | collective-permute-start | bytes 786440 | tf_op jit(solution)/shard_map/ppermute | solution.py:329
  40.0 6.6 %collective-permute-done.2 = bf16[16,64,128]{2,1,0:T(8,128)(2,1)S(1)} collective-permute-done((bf16[16,64,128]{2,1,0:T(8,128)(2,1)S(1)}, bf16[16,64,128]{2,1,0:T(8,128)(2,1)S(1)}, u32[]{:S(2)}, u32[]{:S(2)}) %collective-permute-start.2) | collective-permute-done | bytes 262176 | tf_op jit(solution)/shard_map/ppermute | solution.py:329
  46.6 0.0 collective-permute-done.3
  46.6 0.9 %collective-permute-done.4 = bf16[16,64,128]{2,1,0:T(8,128)(2,1)S(1)} collective-permute-done((bf16[16,64,128]{2,1,0:T(8,128)(2,1)S(1)}, bf16[16,64,128]{2,1,0:T(8,128)(2,1)S(1)}, u32[]{:S(2)}, u32[]{:S(2)}) %collective-permute-start.4) | collective-permute-done | bytes 262176 | tf_op jit(solution)/shard_map/ppermute | solution.py:329
  47.5 0.2 add_convert_fusion
  47.7 13.8 %all_to_all.15 = bf16[16,64,128]{2,1,0:T(8,128)(2,1)S(1)} all-to-all(bf16[16,64,128]{2,1,0:T(8,128)(2,1)S(1)} %add_convert_fusion), channel_id=1, replica_groups={{0,1,2,3,4,5,6,7,64,65,66,67,68,69,70,71},{16,17,18,19,20,21,22,23,80,8..., dimensions={0} | all-to-all | bytes 524288 | tf_op jit(solution)/shard_map/all_to_all | solution.py:323
  61.5 0.2 broadcast_in_dim.2
  61.7 21.0 %all_to_all.16.shares = bf16[64,64,128]{2,1,0:T(8,128)(2,1)S(1)} all-to-all(bf16[64,64,128]{2,1,0:T(8,128)(2,1)S(1)} %broadcast_in_dim.2), channel_id=1, replica_groups={{0,1,2,3,4,5,6,7,64,65,66,67,68,69,70,71,16,17,18,19,20,21,22,23,80,81,..., dimensions={0} | all-to-all | bytes 2097152 | tf_op jit(solution)/shard_map/all_to_all | solution.py:323
  82.7 3.3 %collective-permute-start.5 = (bf16[64,64,128]{2,1,0:T(8,128)(2,1)S(1)}, bf16[64,64,128]{2,1,0:T(8,128)(2,1)S(1)}, u32[]{:S(2)}, u32[]{:S(2)}) collective-permute-start(bf16[64,64,128]{2,1,0:T(8,128)(2,1)S(1)} %all_to_all.16.shares), channel_id=1, source_target_pairs={{0,8},{8,0},{1,9},{9,1},{2,10},{10,2},{3,11},{11,3},{4,12},{12,4},... | collective-permute-start | bytes 3145736 | tf_op jit(solution)/shard_map/ppermute | solution.py:318
  86.0 1.3 %shard_map.71 = (f32[4096,128]{1,0:T(8,128)}, f32[3456,128]{1,0:T(8,128)}) custom-call(s32[1]{0:T(128)} %bitcast.core.half, bf16[64,64,128]{2,1,0:T(8,128)(2,1)S(1)} %all_to_all.16.shares), custom_call_target="tpu_custom_call" | custom-call | bytes 3145728 | tf_op jit(solution)/shard_map/pallas_call | solution.py:359
  87.4 0.9 %collective-permute-done.5.shares = bf16[64,64,128]{2,1,0:T(8,128)(2,1)S(1)} collective-permute-done((bf16[64,64,128]{2,1,0:T(8,128)(2,1)S(1)}, bf16[64,64,128]{2,1,0:T(8,128)(2,1)S(1)}, u32[]{:S(2)}, u32[]{:S(2)}) %collective-permute-start.5) | collective-permute-done | bytes 1048608 | tf_op jit(solution)/shard_map/ppermute | solution.py:318
  88.3 1.3 %shard_map.72 = (f32[4096,128]{1,0:T(8,128)}, f32[3456,128]{1,0:T(8,128)}) custom-call(s32[1]{0:T(128)} %bitcast.8.half, bf16[64,64,128]{2,1,0:T(8,128)(2,1)S(1)} %collective-permute-done.5.shares, f32[4096,128]{1,0:T(8,128)} %get-tuple-element.33.refs_0_, f32[3456,128]{1,0:T(8,128)} %get-tuple-element.34.refs_1_), custom_call_target="tpu_custom_call", output_to_operand_aliasing={{0}: (2, {}), {1}: (3, {})} | custom-call | bytes 3145728 | tf_op jit(solution)/shard_map/pallas_call | solution.py:359
  (2 shorter events, 0.1 us)
Async XLA Ops:
  0.6 7.6 %copy-start.2 = (bf16[2,8,8,8,128]{4,3,2,1,0:T(8,128)(2,1)S(1)}, bf16[2,8,8,8,128]{4,3,2,1,0:T(8,128)(2,1)}, u32[]{:S(2)}) copy-start(bf16[2,8,8,8,128]{4,3,2,1,0:T(8,128)(2,1)} %param.7) | copy-start | bytes 786436
  0.6 23.6 %copy-start = (bf16[4,4,4,64,128]{4,3,2,1,0:T(8,128)(2,1)S(1)}, bf16[4,4,4,64,128]{4,3,2,1,0:T(8,128)(2,1)}, u32[]{:S(2)}) copy-start(bf16[4,4,4,64,128]{4,3,2,1,0:T(8,128)(2,1)} %param.5) | copy-start | bytes 3145732
  0.7 23.6 %all-to-all-start = ((bf16[8,2,4,64,128]{4,3,2,1,0:T(8,128)(2,1)}), bf16[8,2,4,64,128]{4,3,2,1,0:T(8,128)(2,1)S(1)}, u32[]{:S(2)}, u32[]{:S(2)}) async-start(bf16[8,2,4,64,128]{4,3,2,1,0:T(8,128)(2,1)} %bitcast.19), calls=%async_computation | async-start | bytes 2097152 | tf_op jit(solution)/shard_map/all_to_all | solution.py:382
  24.3 1.5 %copy-start.1 = (bf16[3,3,3,128,128]{4,3,2,1,0:T(8,128)(2,1)S(1)}, bf16[3,3,3,128,128]{4,3,2,1,0:T(8,128)(2,1)}, u32[]{:S(2)}) copy-start(bf16[3,3,3,128,128]{4,3,2,1,0:T(8,128)(2,1)} %param.6) | copy-start | bytes 2654212
  32.5 3.8 %collective-permute-start = (bf16[2048,128]{1,0:T(8,128)(2,1)S(1)}, bf16[2048,128]{1,0:T(8,128)(2,1)S(1)}, u32[]{:S(2)}, u32[]{:S(2)}) collective-permute-start(bf16[2048,128]{1,0:T(8,128)(2,1)S(1)} %get-tuple-element.26), channel_id=1, source_target_pairs={{0,8},{8,0},{1,9},{9,1},{2,10},{10,2},{3,11},{11,3},{4,12},{12,4},... | collective-permute-start | bytes 1572872 | tf_op jit(solution)/shard_map/ppermute | solution.py:318
  34.7 2.3 %collective-permute-start.1 = (bf16[2048,128]{1,0:T(8,128)(2,1)S(1)}, bf16[2048,128]{1,0:T(8,128)(2,1)S(1)}, u32[]{:S(2)}, u32[]{:S(2)}) collective-permute-start(bf16[2048,128]{1,0:T(8,128)(2,1)S(1)} %get-tuple-element.28), channel_id=1, source_target_pairs={{0,8},{8,0},{1,9},{9,1},{2,10},{10,2},{3,11},{11,3},{4,12},{12,4},... | collective-permute-start | bytes 1572872 | tf_op jit(solution)/shard_map/ppermute | solution.py:318
  37.3 9.3 %collective-permute-start.2 = (bf16[16,64,128]{2,1,0:T(8,128)(2,1)S(1)}, bf16[16,64,128]{2,1,0:T(8,128)(2,1)S(1)}, u32[]{:S(2)}, u32[]{:S(2)}) collective-permute-start(bf16[16,64,128]{2,1,0:T(8,128)(2,1)S(1)} %get-tuple-element.30), channel_id=1, source_target_pairs={{0,16},{1,17},{2,18},{3,19},{4,20},{5,21},{6,22},{7,23},{8,10},{9,... | collective-permute-start | bytes 786440 | tf_op jit(solution)/shard_map/ppermute | solution.py:329
  37.4 9.2 %collective-permute-start.3 = (bf16[16,64,128]{2,1,0:T(8,128)(2,1)S(1)}, bf16[16,64,128]{2,1,0:T(8,128)(2,1)S(1)}, u32[]{:S(2)}, u32[]{:S(2)}) collective-permute-start(bf16[16,64,128]{2,1,0:T(8,128)(2,1)S(1)} %get-tuple-element.31), channel_id=1, source_target_pairs={{0,32},{1,33},{2,34},{3,35},{4,36},{5,37},{6,38},{7,39},{8,12},{9,... | collective-permute-start | bytes 786440 | tf_op jit(solution)/shard_map/ppermute | solution.py:329
  39.1 8.4 %collective-permute-start.4 = (bf16[16,64,128]{2,1,0:T(8,128)(2,1)S(1)}, bf16[16,64,128]{2,1,0:T(8,128)(2,1)S(1)}, u32[]{:S(2)}, u32[]{:S(2)}) collective-permute-start(bf16[16,64,128]{2,1,0:T(8,128)(2,1)S(1)} %get-tuple-element.32), channel_id=1, source_target_pairs={{0,48},{1,49},{2,50},{3,51},{4,52},{5,53},{6,54},{7,55},{8,14},{9,... | collective-permute-start | bytes 786440 | tf_op jit(solution)/shard_map/ppermute | solution.py:329
  82.7 5.6 %collective-permute-start.5 = (bf16[64,64,128]{2,1,0:T(8,128)(2,1)S(1)}, bf16[64,64,128]{2,1,0:T(8,128)(2,1)S(1)}, u32[]{:S(2)}, u32[]{:S(2)}) collective-permute-start(bf16[64,64,128]{2,1,0:T(8,128)(2,1)S(1)} %all_to_all.16.shares), channel_id=1, source_target_pairs={{0,8},{8,0},{1,9},{9,1},{2,10},{10,2},{3,11},{11,3},{4,12},{12,4},... | collective-permute-start | bytes 3145736 | tf_op jit(solution)/shard_map/ppermute | solution.py:318

commit v2 on v1

--- a/solution.py
+++ b/solution.py
@@ -1,3 +1,5 @@
+import functools
+
 import jax
 import jax.numpy as jnp
 from jax import lax
@@ -329,50 +331,58 @@
         total += lax.ppermute(blocks[by], FINE, shifts[by]).astype(F32)
     shares = exchange(total.astype(BF16), planes)
     share = jnp.sum(shares.astype(F32), axis=0).astype(BF16)
-    wholes = [sum(planes[core * RING : (core + 1) * RING], []) for core in range(2)]
-    return exchange(jnp.broadcast_to(share[None], (64,) + share.shape), wholes)
-
-
-def place_kernel(half, shares, *refs):
+    quarter = exchange(jnp.broadcast_to(share[None], (16,) + share.shape), planes)
+    return [quarter] + [lax.ppermute(quarter, FINE, shifts[by]) for by in range(1, RING)]
+
+
+def place_kernel(shifts, where, *refs):
     early, late, wide_early, wide_late, sems = refs[-5:]
+    rows = HALF // RING
+    last = HALF_LATE - 3 * rows
     copies = []
-    for chunk in range(4):
-        for n in range(16 * chunk, 16 * (chunk + 1)):
-            at = n * SHARE
-            wide_early[at : at + SHARE] = shares[n, :SHARE].astype(F32)
-            if at < HALF_LATE:
-                wide_late[at : at + SHARE] = shares[n, SHARE:].astype(F32)
-        low, high = 16 * chunk * SHARE, 16 * (chunk + 1) * SHARE
-        for wide, out, rows, sem in ((wide_early, early, HALF, 0), (wide_late, late, HALF_LATE, 4)):
-            size = min(high, rows) - low
-            start = pl.multiple_of(half[0] * rows + low, 8)
-            copy = pltpu.make_async_copy(
-                wide.at[pl.ds(low, size)], out.at[pl.ds(start, size)], sems.at[sem + chunk]
-            )
-            copy.start()
-            copies.append(copy)
-    for copy in copies:
-        copy.wait()
-
-
-def placed(half, shares, so_far=()):
+    for n in range(2 * len(shifts)):
+        other, shift = n % 2, shifts[n // 2]
+        half = where[0] ^ other
+        quarter = (where[1 + other] - shift + RING) % RING
+        piece = refs[n]
+        wide_early[n] = piece[:, :SHARE].astype(F32).reshape(rows, LANES)
+        wide_late[n] = piece[:, SHARE:].astype(F32).reshape(rows, LANES)
+        at_early = pl.multiple_of(half * HALF + quarter * rows, rows)
+        at_late = pl.multiple_of(half * HALF_LATE + quarter * rows, 64)
+        to_early = pltpu.make_async_copy(wide_early.at[n], early.at[pl.ds(at_early, rows)], sems.at[n, 0])
+        to_late = pltpu.make_async_copy(wide_late.at[n], late.at[pl.ds(at_late, rows)], sems.at[n, 1])
+        to_end = pltpu.make_async_copy(
+            wide_late.at[n, pl.ds(0, last)], late.at[pl.ds(at_late, last)], sems.at[n, 1]
+        )
+        to_early.start()
+        pl.when(quarter < RING - 1)(to_late.start)
+        pl.when(quarter == RING - 1)(to_end.start)
+        copies.append((quarter, to_early, to_late, to_end))
+    for quarter, to_early, to_late, to_end in copies:
+        to_early.wait()
+        pl.when(quarter < RING - 1)(to_late.wait)
+        pl.when(quarter == RING - 1)(to_end.wait)
+
+
+def placed(where, shifts, pieces, so_far):
+    count = len(pieces)
     return pl.pallas_call(
-        place_kernel,
+        functools.partial(place_kernel, shifts),
         out_shape=(
             jax.ShapeDtypeStruct((2 * HALF, LANES), F32),
             jax.ShapeDtypeStruct((2 * HALF_LATE, LANES), F32),
         ),
-        in_specs=[SMEM, VMEM] + [ANY] * len(so_far),
+        in_specs=[SMEM] + [VMEM] * count + [ANY] * len(so_far),
         out_specs=(ANY, ANY),
-        input_output_aliases={2 + n: n for n in range(len(so_far))},
+        input_output_aliases={1 + count + n: n for n in range(len(so_far))},
         scratch_shapes=[
-            pltpu.VMEM((HALF, LANES), F32),
-            pltpu.VMEM((HALF_LATE, LANES), F32),
-            pltpu.SemaphoreType.DMA((8,)),
+            pltpu.VMEM((count, HALF // RING, LANES), F32),
+            pltpu.VMEM((count, HALF // RING, LANES), F32),
+            pltpu.SemaphoreType.DMA((count, 2)),
         ],
         compiler_params=SMALL,
-        cost_estimate=pl.CostEstimate(flops=0, bytes_accessed=3 * 1024 * 1024, transcendentals=0),
-    )(half.reshape(1), shares, *so_far)
+        cost_estimate=pl.CostEstimate(flops=0, bytes_accessed=count * 768 * 1024, transcendentals=0),
+    )(where, *pieces, *so_far)
 
 
 def per_device(inputs, conv_early, conv_late, cotangent):
@@ -386,9 +396,12 @@
     activated, late, late_sent, error = late_layer(core.reshape(1), hidden, taps_late, signal)
     late_other = swapped(late_sent)
     early, early_sent = backward(core.reshape(1), taps_late, volume, error, slope_early)
-    shares = summed(core, early, swapped(early_sent), late, late_other)
-    other = swapped(shares)
-    early_total, late_total = placed(1 - core, other, placed(core, shares))
+    pieces = summed(core, early, swapped(early_sent), late, late_other)
+    where = jnp.stack([core, ring_place(core), ring_place(1 - core)])
+    totals = placed(where, (0,), [pieces[0], swapped(pieces[0])], ())
+    *totals, one, three = lax.optimization_barrier((*totals, pieces[1], pieces[3]))
+    totals = placed(where, (1, 3), [one, swapped(one), three, swapped(three)], totals)
+    early_total, late_total = placed(where, (2,), [pieces[2], swapped(pieces[2])], totals)
     return (
         activated.reshape(cotangent.shape),
         early_total.reshape(conv_early.shape),

time: 89.9 us -> 89 us (0.990)
  blocking collectives: 34.7 us -> 24.1 us
  starting transfers between devices: 16 us -> 19.8 us
  waiting for transfers between devices: 26.6 us -> 30.3 us
  Pallas kernels: 11.1 us -> 13.4 us
    all_to_all x2, blocking collectives: 34.7 us -> 24.1 us  [summed(): lax.all_to_all(blocks, FINE, split_axis=0, concat_axis=0, axis_index_grou...]
    ppermute x0 -> x3, waiting for transfers between devices: none -> 4.48 us  [summed(): lax.ppermute(quarter, FINE, shifts[by])]
    ppermute x0 -> x3, starting transfers between devices: none -> 2.68 us  [summed(): lax.ppermute(quarter, FINE, shifts[by])]
    pallas_call x2 -> x3, Pallas kernels: 2.66 us -> 4.94 us  [placed(): pl.pallas_call(functools.partial(place_kernel, shifts), out_shape=(jax.Sh...]
    ppermute x3 -> x6, starting transfers between devices: 5.66 us -> 6.72 us  [swapped(): return lax.ppermute(block, 'core', [(0, 1), (1, 0)])]
    ppermute x3 -> x6, waiting for transfers between devices: 3.14 us -> 2.41 us  [swapped(): return lax.ppermute(block, 'core', [(0, 1), (1, 0)])]
  transfers between devices with their start and end apart: 7 -> 13, of which waited for: 6 -> 8; matrix products, arithmetic and copies ran while one was open for 0% -> 0% of each run, Pallas kernels for 1% -> 4%
where the time goes in v2:
time: 89 us; the launch traced here: 88.7 us
  waiting for transfers between devices  30.3 us (34%)
  blocking collectives  24.1 us (27%)
  starting transfers between devices  19.8 us (22%)
  Pallas kernels  13.4 us (15%)
    all_to_all x2, blocking collectives, summed(): lax.all_to_all(blocks, FINE, split_axis=0, concat_axis=0, axis_index_grou...  24.1 us
    all_to_all x1, waiting for transfers between devices, per_device(): lax.all_to_all(sent, ('y', 'xh'), split_axis=0, concat_axis=0, tiled=True)  15.9 us
    all_to_all x1, starting transfers between devices, per_device(): lax.all_to_all(sent, ('y', 'xh'), split_axis=0, concat_axis=0, tiled=True)  7.62 us
    ppermute x3, waiting for transfers between devices, summed(): total += lax.ppermute(blocks[by], FINE, shifts[by]).astype(F32)  7.48 us
    ppermute x6, starting transfers between devices, swapped(): return lax.ppermute(block, 'core', [(0, 1), (1, 0)])  6.72 us
    pallas_call x3, Pallas kernels, placed(): pl.pallas_call(functools.partial(place_kernel, shifts), out_shape=(jax.Sh...  4.94 us
    ppermute x3, waiting for transfers between devices, summed(): lax.ppermute(quarter, FINE, shifts[by])  4.48 us
    pallas_call x1, Pallas kernels, backward(): pl.pallas_call(backward_kernel, out_shape=(HALF_ROWS, HALF_ROWS), in_spec...  3.48 us
  transfers between devices with their start and end apart: 13, of which 8 were waited for; matrix products, arithmetic and copies ran while one was open for 0% of the time, Pallas kernels for 4%

profile of v2, /device:TPU:1, one launch (start us, length us, event | category | flops | bytes accessed | tf_op | source)
XLA Modules:
  0.0 88.7 jit_solution(2348887804385977738)
XLA Ops:
  0.7 7.6 %all-to-all-start = ((bf16[8,2,4,64,128]{4,3,2,1,0:T(8,128)(2,1)}), bf16[8,2,4,64,128]{4,3,2,1,0:T(8,128)(2,1)S(1)}, u32[]{:S(2)}, u32[]{:S(2)}) async-start(bf16[8,2,4,64,128]{4,3,2,1,0:T(8,128)(2,1)} %bitcast.19), calls=%async_computation | async-start | bytes 2097152 | tf_op jit(solution)/shard_map/all_to_all | solution.py:392
  8.3 15.9 %all-to-all-done.received = bf16[8,2,4,64,128]{4,3,2,1,0:T(8,128)(2,1)S(1)} async-done(((bf16[8,2,4,64,128]{4,3,2,1,0:T(8,128)(2,1)}), bf16[8,2,4,64,128]{4,3,2,1,0:T(8,128)(2,1)S(1)}, u32[]{:S(2)}, u32[]{:S(2)}) %all-to-all-start) | async-done | bytes 1048608 | tf_op jit(solution)/shard_map/all_to_all | solution.py:392
  24.3 1.5 %shard_map.67 = (bf16[10,10,16,384]{3,2,1,0:T(8,128)(2,1)S(1)}, bf16[4,9,9,16,256]{4,3,2,1,0:T(8,128)(2,1)S(1)}, f32[1024,128]{1,0:T(8,128)S(1)}) custom-call(bf16[8,2,4,64,128]{4,3,2,1,0:T(8,128)(2,1)S(1)} %all-to-all-done.received, bf16[16,256,128]{2,1,0:T(8,128)(2,1)S(1)} %bitcast.14), custom_call_target="tpu_custom_call" | custom-call | flops 1073741824 | bytes 8388608 | tf_op jit(solution)/shard_map/pallas_call | solution.py:224
  25.8 3.3 %shard_map.68 = (bf16[2,8,64,128]{3,2,1,0:T(8,128)(2,1)}, bf16[2048,128]{1,0:T(8,128)(2,1)S(1)}, bf16[2048,128]{1,0:T(8,128)(2,1)S(1)}, bf16[10,10,16,384]{3,2,1,0:T(8,128)(2,1)S(1)}) custom-call(s32[1]{0:T(128)} %bitcast.core, bf16[10,10,16,384]{3,2,1,0:T(8,128)(2,1)S(1)} %get-tuple-element.26.hidden, bf16[9,384,128]{2,1,0:T(8,128)(2,1)S(1)} %bitcast.15, ...), custom_call_target="tpu_custom_call" | custom-call | flops 1811939328 | bytes 8388608 | tf_op jit(solution)/shard_map/pallas_call | solution.py:240
  29.0 3.5 %shard_map.69 = (bf16[2048,128]{1,0:T(8,128)(2,1)S(1)}, bf16[2048,128]{1,0:T(8,128)(2,1)S(1)}) custom-call(s32[1]{0:T(128)} %bitcast.core, bf16[9,384,128]{2,1,0:T(8,128)(2,1)S(1)} %bitcast.16, bf16[4,9,9,16,256]{4,3,2,1,0:T(8,128)(2,1)S(1)} %get-tuple-element.28.volume, bf16[10,10,16,384]{3,2,1,0:T(8,128)(2,1)S(1)} %get-tuple-element.29.error, ...), custom_call_target="tpu_custom_call" | custom-call | flops 1979711488 | bytes 8388608 | tf_op jit(solution)/shard_map/pallas_call | solution.py:261
  32.5 2.2 %collective-permute-start = (bf16[2048,128]{1,0:T(8,128)(2,1)S(1)}, bf16[2048,128]{1,0:T(8,128)(2,1)S(1)}, u32[]{:S(2)}, u32[]{:S(2)}) collective-permute-start(bf16[2048,128]{1,0:T(8,128)(2,1)S(1)} %get-tuple-element.32), channel_id=1, source_target_pairs={{0,8},{8,0},{1,9},{9,1},{2,10},{10,2},{3,11},{11,3},{4,12},{12,4},... | collective-permute-start | bytes 1572872 | tf_op jit(solution)/shard_map/ppermute | solution.py:320
  34.7 0.1 collective-permute-start.1
  34.8 1.4 %collective-permute-done.early_other = bf16[2048,128]{1,0:T(8,128)(2,1)S(1)} collective-permute-done((bf16[2048,128]{1,0:T(8,128)(2,1)S(1)}, bf16[2048,128]{1,0:T(8,128)(2,1)S(1)}, u32[]{:S(2)}, u32[]{:S(2)}) %collective-permute-start) | collective-permute-done | bytes 524320 | tf_op jit(solution)/shard_map/ppermute | solution.py:320
  36.3 0.7 collective-permute-done.1.late_other
  37.0 0.2 shard_map.70
  37.3 0.1 collective-permute-start.2
  37.4 1.7 %collective-permute-start.3 = (bf16[16,64,128]{2,1,0:T(8,128)(2,1)S(1)}, bf16[16,64,128]{2,1,0:T(8,128)(2,1)S(1)}, u32[]{:S(2)}, u32[]{:S(2)}) collective-permute-start(bf16[16,64,128]{2,1,0:T(8,128)(2,1)S(1)} %get-tuple-element.37), channel_id=1, source_target_pairs={{0,32},{1,33},{2,34},{3,35},{4,36},{5,37},{6,38},{7,39},{8,12},{9,... | collective-permute-start | bytes 786440 | tf_op jit(solution)/shard_map/ppermute | solution.py:331
  39.1 0.9 %collective-permute-start.4 = (bf16[16,64,128]{2,1,0:T(8,128)(2,1)S(1)}, bf16[16,64,128]{2,1,0:T(8,128)(2,1)S(1)}, u32[]{:S(2)}, u32[]{:S(2)}) collective-permute-start(bf16[16,64,128]{2,1,0:T(8,128)(2,1)S(1)} %get-tuple-element.38), channel_id=1, source_target_pairs={{0,48},{1,49},{2,50},{3,51},{4,52},{5,53},{6,54},{7,55},{8,14},{9,... | collective-permute-start | bytes 786440 | tf_op jit(solution)/shard_map/ppermute | solution.py:331
  40.0 6.6 %collective-permute-done.2 = bf16[16,64,128]{2,1,0:T(8,128)(2,1)S(1)} collective-permute-done((bf16[16,64,128]{2,1,0:T(8,128)(2,1)S(1)}, bf16[16,64,128]{2,1,0:T(8,128)(2,1)S(1)}, u32[]{:S(2)}, u32[]{:S(2)}) %collective-permute-start.2) | collective-permute-done | bytes 262176 | tf_op jit(solution)/shard_map/ppermute | solution.py:331
  46.6 0.0 collective-permute-done.3
  46.6 0.9 %collective-permute-done.4 = bf16[16,64,128]{2,1,0:T(8,128)(2,1)S(1)} collective-permute-done((bf16[16,64,128]{2,1,0:T(8,128)(2,1)S(1)}, bf16[16,64,128]{2,1,0:T(8,128)(2,1)S(1)}, u32[]{:S(2)}, u32[]{:S(2)}) %collective-permute-start.4) | collective-permute-done | bytes 262176 | tf_op jit(solution)/shard_map/ppermute | solution.py:331
  47.5 0.2 add_convert_fusion
  47.7 13.8 %all_to_all.15 = bf16[16,64,128]{2,1,0:T(8,128)(2,1)S(1)} all-to-all(bf16[16,64,128]{2,1,0:T(8,128)(2,1)S(1)} %add_convert_fusion), channel_id=1, replica_groups={{0,1,2,3,4,5,6,7,64,65,66,67,68,69,70,71},{16,17,18,19,20,21,22,23,80,8..., dimensions={0} | all-to-all | bytes 524288 | tf_op jit(solution)/shard_map/all_to_all | solution.py:325
  61.5 10.4 %all_to_all.16.refs_0_ = bf16[16,64,128]{2,1,0:T(8,128)(2,1)S(1)} all-to-all(bf16[16,64,128]{2,1,0:T(8,128)(2,1)S(1)} %broadcast_in_dim.2), channel_id=1, replica_groups={{0,1,2,3,4,5,6,7,64,65,66,67,68,69,70,71},{16,17,18,19,20,21,22,23,80,8..., dimensions={0} | all-to-all | bytes 524288 | tf_op jit(solution)/shard_map/all_to_all | solution.py:325
  71.9 1.9 %collective-permute-start.7 = (bf16[16,64,128]{2,1,0:T(8,128)(2,1)S(1)}, bf16[16,64,128]{2,1,0:T(8,128)(2,1)S(1)}, u32[]{:S(2)}, u32[]{:S(2)}) collective-permute-start(bf16[16,64,128]{2,1,0:T(8,128)(2,1)S(1)} %all_to_all.16.refs_0_), channel_id=1, source_target_pairs={{0,8},{8,0},{1,9},{9,1},{2,10},{10,2},{3,11},{11,3},{4,12},{12,4},... | collective-permute-start | bytes 786440 | tf_op jit(solution)/shard_map/ppermute | solution.py:320
  73.8 0.1 collective-permute-start.8
  73.9 2.6 %collective-permute-start.9 = (bf16[16,64,128]{2,1,0:T(8,128)(2,1)S(1)}, bf16[16,64,128]{2,1,0:T(8,128)(2,1)S(1)}, u32[]{:S(2)}, u32[]{:S(2)}) collective-permute-start(bf16[16,64,128]{2,1,0:T(8,128)(2,1)S(1)} %all_to_all.16.refs_0_), channel_id=1, source_target_pairs={{0,48},{1,49},{2,50},{3,51},{4,52},{5,53},{6,54},{7,55},{8,14},{9,... | collective-permute-start | bytes 786440 | tf_op jit(solution)/shard_map/ppermute | solution.py:335
  76.5 0.1 pad_add_fusion.where
  76.6 0.0 collective-permute-done.7.refs_1_
  76.6 1.6 %shard_map.71 = (f32[4096,128]{1,0:T(8,128)}, f32[3456,128]{1,0:T(8,128)}) custom-call(s32[3]{0:T(128)S(1)} %pad_add_fusion.where, bf16[16,64,128]{2,1,0:T(8,128)(2,1)S(1)} %all_to_all.16.refs_0_, bf16[16,64,128]{2,1,0:T(8,128)(2,1)S(1)} %collective-permute-done.7.refs_1_), custom_call_target="tpu_custom_call" | custom-call | bytes 1572864 | tf_op jit(solution)/shard_map/pallas_call | solution.py:369
  78.1 2.4 %collective-permute-done.8.refs_0_ = bf16[16,64,128]{2,1,0:T(8,128)(2,1)S(1)} collective-permute-done((bf16[16,64,128]{2,1,0:T(8,128)(2,1)S(1)}, bf16[16,64,128]{2,1,0:T(8,128)(2,1)S(1)}, u32[]{:S(2)}, u32[]{:S(2)}) %collective-permute-start.8) | collective-permute-done | bytes 262176 | tf_op jit(solution)/shard_map/ppermute | solution.py:335
  80.5 2.1 %collective-permute-done.9.refs_2_ = bf16[16,64,128]{2,1,0:T(8,128)(2,1)S(1)} collective-permute-done((bf16[16,64,128]{2,1,0:T(8,128)(2,1)S(1)}, bf16[16,64,128]{2,1,0:T(8,128)(2,1)S(1)}, u32[]{:S(2)}, u32[]{:S(2)}) %collective-permute-start.9) | collective-permute-done | bytes 262176 | tf_op jit(solution)/shard_map/ppermute | solution.py:335
  82.6 1.2 %collective-permute-start.10 = (bf16[16,64,128]{2,1,0:T(8,128)(2,1)S(1)}, bf16[16,64,128]{2,1,0:T(8,128)(2,1)S(1)}, u32[]{:S(2)}, u32[]{:S(2)}) collective-permute-start(bf16[16,64,128]{2,1,0:T(8,128)(2,1)S(1)} %collective-permute-done.8.refs_0_), channel_id=1, source_target_pairs={{0,8},{8,0},{1,9},{9,1},{2,10},{10,2},{3,11},{11,3},{4,12},{12,4},... | collective-permute-start | bytes 786440 | tf_op jit(solution)/shard_map/ppermute | solution.py:320
  83.8 1.3 %collective-permute-start.6 = (bf16[16,64,128]{2,1,0:T(8,128)(2,1)S(1)}, bf16[16,64,128]{2,1,0:T(8,128)(2,1)S(1)}, u32[]{:S(2)}, u32[]{:S(2)}) collective-permute-start(bf16[16,64,128]{2,1,0:T(8,128)(2,1)S(1)} %collective-permute-done.5.refs_0_), channel_id=1, source_target_pairs={{0,8},{8,0},{1,9},{9,1},{2,10},{10,2},{3,11},{11,3},{4,12},{12,4},... | collective-permute-start | bytes 786440 | tf_op jit(solution)/shard_map/ppermute | solution.py:320
  85.1 0.2 collective-permute-done.11.refs_3_
  85.3 1.8 %shard_map.72 = (f32[4096,128]{1,0:T(8,128)}, f32[3456,128]{1,0:T(8,128)}) custom-call(s32[3]{0:T(128)S(1)} %pad_add_fusion.where, bf16[16,64,128]{2,1,0:T(8,128)(2,1)S(1)} %collective-permute-done.8.refs_0_, bf16[16,64,128]{2,1,0:T(8,128)(2,1)S(1)} %collective-permute-done.10.refs_1_, ...), custom_call_target="tpu_custom_call", output_to_operand_aliasing={{0}: (5, {}), {1}: (6, {})} | custom-call | bytes 3145728 | tf_op jit(solution)/shard_map/pallas_call | solution.py:369
  87.2 1.6 %shard_map.73 = (f32[4096,128]{1,0:T(8,128)}, f32[3456,128]{1,0:T(8,128)}) custom-call(s32[3]{0:T(128)S(1)} %pad_add_fusion.where, bf16[16,64,128]{2,1,0:T(8,128)(2,1)S(1)} %collective-permute-done.5.refs_0_, bf16[16,64,128]{2,1,0:T(8,128)(2,1)S(1)} %collective-permute-done.6.refs_1_, ...), custom_call_target="tpu_custom_call", output_to_operand_aliasing={{0}: (3, {}), {1}: (4, {})} | custom-call | bytes 1572864 | tf_op jit(solution)/shard_map/pallas_call | solution.py:369
  (14 shorter events, 0.2 us)
Async XLA Ops:
  0.6 7.6 %copy-start.2 = (bf16[2,8,8,8,128]{4,3,2,1,0:T(8,128)(2,1)S(1)}, bf16[2,8,8,8,128]{4,3,2,1,0:T(8,128)(2,1)}, u32[]{:S(2)}) copy-start(bf16[2,8,8,8,128]{4,3,2,1,0:T(8,128)(2,1)} %param.7) | copy-start | bytes 786436
  0.6 23.6 %copy-start = (bf16[4,4,4,64,128]{4,3,2,1,0:T(8,128)(2,1)S(1)}, bf16[4,4,4,64,128]{4,3,2,1,0:T(8,128)(2,1)}, u32[]{:S(2)}) copy-start(bf16[4,4,4,64,128]{4,3,2,1,0:T(8,128)(2,1)} %param.5) | copy-start | bytes 3145732
  0.7 23.6 %all-to-all-start = ((bf16[8,2,4,64,128]{4,3,2,1,0:T(8,128)(2,1)}), bf16[8,2,4,64,128]{4,3,2,1,0:T(8,128)(2,1)S(1)}, u32[]{:S(2)}, u32[]{:S(2)}) async-start(bf16[8,2,4,64,128]{4,3,2,1,0:T(8,128)(2,1)} %bitcast.19), calls=%async_computation | async-start | bytes 2097152 | tf_op jit(solution)/shard_map/all_to_all | solution.py:392
  24.3 1.5 %copy-start.1 = (bf16[3,3,3,128,128]{4,3,2,1,0:T(8,128)(2,1)S(1)}, bf16[3,3,3,128,128]{4,3,2,1,0:T(8,128)(2,1)}, u32[]{:S(2)}) copy-start(bf16[3,3,3,128,128]{4,3,2,1,0:T(8,128)(2,1)} %param.6) | copy-start | bytes 2654212
  32.5 3.8 %collective-permute-start = (bf16[2048,128]{1,0:T(8,128)(2,1)S(1)}, bf16[2048,128]{1,0:T(8,128)(2,1)S(1)}, u32[]{:S(2)}, u32[]{:S(2)}) collective-permute-start(bf16[2048,128]{1,0:T(8,128)(2,1)S(1)} %get-tuple-element.32), channel_id=1, source_target_pairs={{0,8},{8,0},{1,9},{9,1},{2,10},{10,2},{3,11},{11,3},{4,12},{12,4},... | collective-permute-start | bytes 1572872 | tf_op jit(solution)/shard_map/ppermute | solution.py:320
  34.7 2.3 %collective-permute-start.1 = (bf16[2048,128]{1,0:T(8,128)(2,1)S(1)}, bf16[2048,128]{1,0:T(8,128)(2,1)S(1)}, u32[]{:S(2)}, u32[]{:S(2)}) collective-permute-start(bf16[2048,128]{1,0:T(8,128)(2,1)S(1)} %get-tuple-element.34), channel_id=1, source_target_pairs={{0,8},{8,0},{1,9},{9,1},{2,10},{10,2},{3,11},{11,3},{4,12},{12,4},... | collective-permute-start | bytes 1572872 | tf_op jit(solution)/shard_map/ppermute | solution.py:320
  37.3 9.3 %collective-permute-start.2 = (bf16[16,64,128]{2,1,0:T(8,128)(2,1)S(1)}, bf16[16,64,128]{2,1,0:T(8,128)(2,1)S(1)}, u32[]{:S(2)}, u32[]{:S(2)}) collective-permute-start(bf16[16,64,128]{2,1,0:T(8,128)(2,1)S(1)} %get-tuple-element.36), channel_id=1, source_target_pairs={{0,16},{1,17},{2,18},{3,19},{4,20},{5,21},{6,22},{7,23},{8,10},{9,... | collective-permute-start | bytes 786440 | tf_op jit(solution)/shard_map/ppermute | solution.py:331
  37.4 9.2 %collective-permute-start.3 = (bf16[16,64,128]{2,1,0:T(8,128)(2,1)S(1)}, bf16[16,64,128]{2,1,0:T(8,128)(2,1)S(1)}, u32[]{:S(2)}, u32[]{:S(2)}) collective-permute-start(bf16[16,64,128]{2,1,0:T(8,128)(2,1)S(1)} %get-tuple-element.37), channel_id=1, source_target_pairs={{0,32},{1,33},{2,34},{3,35},{4,36},{5,37},{6,38},{7,39},{8,12},{9,... | collective-permute-start | bytes 786440 | tf_op jit(solution)/shard_map/ppermute | solution.py:331
  39.1 8.4 %collective-permute-start.4 = (bf16[16,64,128]{2,1,0:T(8,128)(2,1)S(1)}, bf16[16,64,128]{2,1,0:T(8,128)(2,1)S(1)}, u32[]{:S(2)}, u32[]{:S(2)}) collective-permute-start(bf16[16,64,128]{2,1,0:T(8,128)(2,1)S(1)} %get-tuple-element.38), channel_id=1, source_target_pairs={{0,48},{1,49},{2,50},{3,51},{4,52},{5,53},{6,54},{7,55},{8,14},{9,... | collective-permute-start | bytes 786440 | tf_op jit(solution)/shard_map/ppermute | solution.py:331
  71.9 4.7 %collective-permute-start.7 = (bf16[16,64,128]{2,1,0:T(8,128)(2,1)S(1)}, bf16[16,64,128]{2,1,0:T(8,128)(2,1)S(1)}, u32[]{:S(2)}, u32[]{:S(2)}) collective-permute-start(bf16[16,64,128]{2,1,0:T(8,128)(2,1)S(1)} %all_to_all.16.refs_0_), channel_id=1, source_target_pairs={{0,8},{8,0},{1,9},{9,1},{2,10},{10,2},{3,11},{11,3},{4,12},{12,4},... | collective-permute-start | bytes 786440 | tf_op jit(solution)/shard_map/ppermute | solution.py:320
  73.8 6.7 %collective-permute-start.8 = (bf16[16,64,128]{2,1,0:T(8,128)(2,1)S(1)}, bf16[16,64,128]{2,1,0:T(8,128)(2,1)S(1)}, u32[]{:S(2)}, u32[]{:S(2)}) collective-permute-start(bf16[16,64,128]{2,1,0:T(8,128)(2,1)S(1)} %all_to_all.16.refs_0_), channel_id=1, source_target_pairs={{0,16},{1,17},{2,18},{3,19},{4,20},{5,21},{6,22},{7,23},{8,10},{9,... | collective-permute-start | bytes 786440 | tf_op jit(solution)/shard_map/ppermute | solution.py:335
  73.9 8.7 %collective-permute-start.9 = (bf16[16,64,128]{2,1,0:T(8,128)(2,1)S(1)}, bf16[16,64,128]{2,1,0:T(8,128)(2,1)S(1)}, u32[]{:S(2)}, u32[]{:S(2)}) collective-permute-start(bf16[16,64,128]{2,1,0:T(8,128)(2,1)S(1)} %all_to_all.16.refs_0_), channel_id=1, source_target_pairs={{0,48},{1,49},{2,50},{3,51},{4,52},{5,53},{6,54},{7,55},{8,14},{9,... | collective-permute-start | bytes 786440 | tf_op jit(solution)/shard_map/ppermute | solution.py:335
  76.5 7.3 %collective-permute-start.5 = (bf16[16,64,128]{2,1,0:T(8,128)(2,1)S(1)}, bf16[16,64,128]{2,1,0:T(8,128)(2,1)S(1)}, u32[]{:S(2)}, u32[]{:S(2)}) collective-permute-start(bf16[16,64,128]{2,1,0:T(8,128)(2,1)S(1)} %all_to_all.16.refs_0_), channel_id=1, source_target_pairs={{0,32},{1,33},{2,34},{3,35},{4,36},{5,37},{6,38},{7,39},{8,12},{9,... | collective-permute-start | bytes 786440 | tf_op jit(solution)/shard_map/ppermute | solution.py:335
  82.6 2.5 %collective-permute-start.10 = (bf16[16,64,128]{2,1,0:T(8,128)(2,1)S(1)}, bf16[16,64,128]{2,1,0:T(8,128)(2,1)S(1)}, u32[]{:S(2)}, u32[]{:S(2)}) collective-permute-start(bf16[16,64,128]{2,1,0:T(8,128)(2,1)S(1)} %collective-permute-done.8.refs_0_), channel_id=1, source_target_pairs={{0,8},{8,0},{1,9},{9,1},{2,10},{10,2},{3,11},{11,3},{4,12},{12,4},... | collective-permute-start | bytes 786440 | tf_op jit(solution)/shard_map/ppermute | solution.py:320
  83.8 1.5 %collective-permute-start.11 = (bf16[16,64,128]{2,1,0:T(8,128)(2,1)S(1)}, bf16[16,64,128]{2,1,0:T(8,128)(2,1)S(1)}, u32[]{:S(2)}, u32[]{:S(2)}) collective-permute-start(bf16[16,64,128]{2,1,0:T(8,128)(2,1)S(1)} %collective-permute-done.9.refs_2_), channel_id=1, source_target_pairs={{0,8},{8,0},{1,9},{9,1},{2,10},{10,2},{3,11},{11,3},{4,12},{12,4},... | collective-permute-start | bytes 786440 | tf_op jit(solution)/shard_map/ppermute | solution.py:320
  83.8 3.4 %collective-permute-start.6 = (bf16[16,64,128]{2,1,0:T(8,128)(2,1)S(1)}, bf16[16,64,128]{2,1,0:T(8,128)(2,1)S(1)}, u32[]{:S(2)}, u32[]{:S(2)}) collective-permute-start(bf16[16,64,128]{2,1,0:T(8,128)(2,1)S(1)} %collective-permute-done.5.refs_0_), channel_id=1, source_target_pairs={{0,8},{8,0},{1,9},{9,1},{2,10},{10,2},{3,11},{11,3},{4,12},{12,4},... | collective-permute-start | bytes 786440 | tf_op jit(solution)/shard_map/ppermute | solution.py:320

commit v3 on v2

--- a/solution.py
+++ b/solution.py
@@ -17,7 +17,10 @@
 HALF_LATE = 3 * 3 * 3 * 128 // 2
 GRANULE = HALF_LATE // 9
 SHARE = HALF // 64
+SHARE_LATE = HALF_LATE // 64
 RING = 4
+QUARTER = HALF // RING
+QUARTER_LATE = HALF_LATE // RING
 
 
 def shifted(rows, by, lane=None):
@@ -128,7 +131,6 @@
         value = (cotangent[rows].astype(F32) * (sigma * (1.0 + late * (1.0 - sigma)))).reshape(16, SIDE, LANES)
         error[d + 1, 1:9] = three_widths(value).reshape(SIDE, 16, 3 * LANES).astype(BF16)
 
-    grads[:, HALF_LATE:] = jnp.zeros((2, HALF - HALF_LATE, LANES), BF16)
     for d in range(SIDE):
         hidden_t[:, d * LANES : (d + 1) * LANES] = hidden[d + 1, 1:9].reshape(LANES, 3 * LANES).T
 
@@ -150,9 +152,7 @@
     sent[...] = grads[1]
 
 
-def backward_kernel(
-    core, conv_late, volume, error, slope_early, kept, sent, volume_t, error_early, total, grads
-):
+def backward_kernel(conv_late, volume, error, slope_early, error_early, volume_t, total):
     clear_rim(error_early, 10)
 
     def back_block(kd):
@@ -176,6 +176,10 @@
             volume_t[phase, :, d * LANES : (d + 1) * LANES] = (
                 volume[phase, d + dp, hp : hp + SIDE].reshape(LANES, 2 * LANES).T
             )
+
+
+def early_grad_kernel(core, error_early, volume_t, late, late_other, kept, sent, late_sum, grads):
+    late_sum[...] = (late[...].astype(F32) + late_other[...].astype(F32)).astype(BF16)
     for phase in range(4):
         dp, hp = phase // 2, phase % 2
         for first in range(2):
@@ -209,7 +213,8 @@
 FIELD = (10, 10, 16, 3 * LANES)
 
 
-HALF_ROWS = jax.ShapeDtypeStruct((HALF, LANES), BF16)
+EARLY_ROWS = jax.ShapeDtypeStruct((HALF, LANES), BF16)
+LATE_ROWS = jax.ShapeDtypeStruct((HALF_LATE, LANES), BF16)
 
 
 def cost(products, transcendentals=0):
@@ -241,8 +246,8 @@
         late_kernel,
         out_shape=(
             jax.ShapeDtypeStruct((2, SIDE, SIDE * SIDE, LANES), BF16),
-            HALF_ROWS,
-            HALF_ROWS,
+            LATE_ROWS,
+            LATE_ROWS,
             jax.ShapeDtypeStruct(FIELD, BF16),
         ),
         in_specs=[SMEM, VMEM, VMEM, VMEM],
@@ -250,28 +255,38 @@
         scratch_shapes=[
             pltpu.VMEM((3 * LANES, CELLS), BF16),
             pltpu.VMEM((CELLS, LANES), F32),
-            pltpu.VMEM((2, HALF, LANES), BF16),
+            pltpu.VMEM((2, HALF_LATE, LANES), BF16),
         ],
         compiler_params=LIMIT,
         cost_estimate=cost(2 * 27 * LANES, CELLS * LANES),
     )(core, hidden, conv_late, cotangent)
 
 
-def backward(core, conv_late, volume, error, slope_early):
+def backward(conv_late, volume, error, slope_early):
     return pl.pallas_call(
         backward_kernel,
-        out_shape=(HALF_ROWS, HALF_ROWS),
-        in_specs=[SMEM, VMEM, VMEM, VMEM, VMEM],
+        out_shape=(
+            jax.ShapeDtypeStruct((10, 10, 16, LANES), BF16),
+            jax.ShapeDtypeStruct((4, 2 * LANES, CELLS), BF16),
+        ),
+        in_specs=[VMEM] * 4,
         out_specs=(VMEM, VMEM),
-        scratch_shapes=[
-            pltpu.VMEM((4, 2 * LANES, CELLS), BF16),
-            pltpu.VMEM((10, 10, 16, LANES), BF16),
-            pltpu.VMEM((CELLS, LANES), F32),
-            pltpu.VMEM((2, HALF, LANES), BF16),
-        ],
+        scratch_shapes=[pltpu.VMEM((CELLS, LANES), F32)],
         compiler_params=LIMIT,
-        cost_estimate=cost(16 * 256 + 27 * LANES),
-    )(core, conv_late, volume, error, slope_early)
+        cost_estimate=cost(27 * LANES),
+    )(conv_late, volume, error, slope_early)
+
+
+def early_grad(core, error_early, volume_t, late, late_other):
+    return pl.pallas_call(
+        early_grad_kernel,
+        out_shape=(EARLY_ROWS, EARLY_ROWS, LATE_ROWS),
+        in_specs=[SMEM] + [VMEM] * 4,
+        out_specs=(VMEM,) * 3,
+        scratch_shapes=[pltpu.VMEM((2, HALF, LANES), BF16)],
+        compiler_params=LIMIT,
+        cost_estimate=cost(16 * 256),
+    )(core, error_early, volume_t, late, late_other)
 
 
 def ring_place(core):
@@ -294,80 +309,104 @@
     return shifts, [planes[key] for key in sorted(planes)]
 
 
-def pair_kernel(place, early, early_other, late, late_other, *blocks):
-    rows = HALF // RING
+def small_call(kernel, out_shape, scratch, *args):
+    return pl.pallas_call(
+        kernel,
+        out_shape=out_shape,
+        in_specs=[SMEM if arg.ndim == 1 else VMEM for arg in args],
+        out_specs=jax.tree.map(lambda _: VMEM, out_shape),
+        scratch_shapes=scratch,
+        compiler_params=SMALL,
+        cost_estimate=pl.CostEstimate(flops=0, bytes_accessed=2 * 1024 * 1024, transcendentals=0),
+    )(*args)
+
+
+def pair_kernel(place, early, early_other, late_sum, *blocks):
     for n, block in enumerate(blocks):
-        start = ((place[0] + n) % RING) * rows
-        for kept, other, first in ((early, early_other, 0), (late, late_other, SHARE)):
-            part = pl.ds(pl.multiple_of(start, rows), rows)
-            value = (kept[part].astype(F32) + other[part].astype(F32)).astype(BF16)
-            block[:, first : first + SHARE] = value.reshape(16, SHARE, LANES)
-
-
-def pair_sums(place, early, early_other, late, late_other):
-    block = jax.ShapeDtypeStruct((16, 2 * SHARE, LANES), BF16)
-    return pl.pallas_call(
-        pair_kernel,
-        out_shape=(block,) * RING,
-        in_specs=[SMEM] + [VMEM] * 4,
-        out_specs=(VMEM,) * RING,
-        compiler_params=SMALL,
-        cost_estimate=pl.CostEstimate(flops=0, bytes_accessed=4 * 1024 * 1024, transcendentals=0),
-    )(place.reshape(1), early, early_other, late, late_other)
+        quarter = (place[0] + n) % RING
+        part = pl.ds(pl.multiple_of(quarter * QUARTER, QUARTER), QUARTER)
+        block[:QUARTER] = (early[part].astype(F32) + early_other[part].astype(F32)).astype(BF16)
+        block[QUARTER:] = late_sum[pl.ds(pl.multiple_of(quarter * QUARTER_LATE, 16), QUARTER_LATE)]
+
+
+def pair_sums(place, early, early_other, late_sum):
+    block = jax.ShapeDtypeStruct((QUARTER + QUARTER_LATE, LANES), BF16)
+    return small_call(pair_kernel, (block,) * RING, [], place.reshape(1), early, early_other, late_sum)
+
+
+def ring_kernel(first, second, third, fourth, shares, late):
+    total = first[...].astype(F32) + second[...].astype(F32)
+    total = total + third[...].astype(F32) + fourth[...].astype(F32)
+    shares[:, :SHARE] = total[:QUARTER].astype(BF16).reshape(16, SHARE, LANES)
+    late[:QUARTER_LATE] = total[QUARTER:]
+    late[QUARTER_LATE:] = jnp.zeros((late.shape[0] - QUARTER_LATE, LANES), F32)
+    for n in range(16):
+        shares[n, SHARE:] = late[n * SHARE_LATE : n * SHARE_LATE + SHARE].astype(BF16)
+
+
+def share_kernel(shares, spread):
+    total = jnp.sum(shares[...].astype(F32), axis=0).astype(BF16)
+    for n in range(16):
+        spread[n] = total
+
+
+def join_kernel(shares, rows, late):
+    rows[:QUARTER] = shares[:, :SHARE].reshape(QUARTER, LANES)
+    for n in range(16):
+        late[n * SHARE_LATE : n * SHARE_LATE + SHARE] = shares[n, SHARE:].astype(F32)
+    rows[QUARTER:] = late[:QUARTER_LATE].astype(BF16)
 
 
 def swapped(block):
     return lax.ppermute(block, "core", [(0, 1), (1, 0)])
 
 
-def summed(core, early, early_other, late, late_other):
+def summed(core, early, early_other, late_sum):
     shifts, planes = chip_routes()
-    exchange = lambda blocks, groups: lax.all_to_all(
-        blocks, FINE, split_axis=0, concat_axis=0, axis_index_groups=groups, tiled=True
+    exchange = lambda blocks: lax.all_to_all(
+        blocks, FINE, split_axis=0, concat_axis=0, axis_index_groups=planes, tiled=True
     )
-    blocks = pair_sums(ring_place(core), early, early_other, late, late_other)
-    total = blocks[0].astype(F32)
+    blocks = list(pair_sums(ring_place(core), early, early_other, late_sum))
     for by in range(1, RING):
-        total += lax.ppermute(blocks[by], FINE, shifts[by]).astype(F32)
-    shares = exchange(total.astype(BF16), planes)
-    share = jnp.sum(shares.astype(F32), axis=0).astype(BF16)
-    quarter = exchange(jnp.broadcast_to(share[None], (16,) + share.shape), planes)
+        blocks[by] = lax.ppermute(blocks[by], FINE, shifts[by])
+    shares = jax.ShapeDtypeStruct((16, 2 * SHARE, LANES), BF16)
+    uneven = [pltpu.VMEM((QUARTER_LATE + 8, LANES), F32)]
+    sent = exchange(small_call(ring_kernel, shares, uneven, *blocks))
+    spread = exchange(small_call(share_kernel, shares, [], sent))
+    rows = jax.ShapeDtypeStruct((QUARTER + QUARTER_LATE, LANES), BF16)
+    quarter = small_call(join_kernel, rows, uneven, spread)
     return [quarter] + [lax.ppermute(quarter, FINE, shifts[by]) for by in range(1, RING)]
 
 
-def place_kernel(shifts, where, *refs):
-    early, late, wide_early, wide_late, sems = refs[-5:]
-    rows = HALF // RING
-    last = HALF_LATE - 3 * rows
+def place_kernel(origins, where, *refs):
+    early, late, wide, sems = refs[-4:]
     copies = []
-    for n in range(2 * len(shifts)):
-        other, shift = n % 2, shifts[n // 2]
+    for n, (shift, other) in enumerate(origins):
         half = where[0] ^ other
         quarter = (where[1 + other] - shift + RING) % RING
-        piece = refs[n]
-        wide_early[n] = piece[:, :SHARE].astype(F32).reshape(rows, LANES)
-        wide_late[n] = piece[:, SHARE:].astype(F32).reshape(rows, LANES)
-        at_early = pl.multiple_of(half * HALF + quarter * rows, rows)
-        at_late = pl.multiple_of(half * HALF_LATE + quarter * rows, 64)
-        to_early = pltpu.make_async_copy(wide_early.at[n], early.at[pl.ds(at_early, rows)], sems.at[n, 0])
-        to_late = pltpu.make_async_copy(wide_late.at[n], late.at[pl.ds(at_late, rows)], sems.at[n, 1])
-        to_end = pltpu.make_async_copy(
-            wide_late.at[n, pl.ds(0, last)], late.at[pl.ds(at_late, last)], sems.at[n, 1]
-        )
-        to_early.start()
-        pl.when(quarter < RING - 1)(to_late.start)
-        pl.when(quarter == RING - 1)(to_end.start)
-        copies.append((quarter, to_early, to_late, to_end))
-    for quarter, to_early, to_late, to_end in copies:
-        to_early.wait()
-        pl.when(quarter < RING - 1)(to_late.wait)
-        pl.when(quarter == RING - 1)(to_end.wait)
-
-
-def placed(where, shifts, pieces, so_far):
+        wide[n] = refs[n][...].astype(F32)
+        at_early = pl.multiple_of(half * HALF + quarter * QUARTER, QUARTER)
+        at_late = pl.multiple_of(half * HALF_LATE + quarter * QUARTER_LATE, 16)
+        copies += [
+            pltpu.make_async_copy(
+                wide.at[n, pl.ds(0, QUARTER)], early.at[pl.ds(at_early, QUARTER)], sems.at[n, 0]
+            ),
+            pltpu.make_async_copy(
+                wide.at[n, pl.ds(QUARTER, QUARTER_LATE)],
+                late.at[pl.ds(at_late, QUARTER_LATE)],
+                sems.at[n, 1],
+            ),
+        ]
+        for copy in copies[-2:]:
+            copy.start()
+    for copy in copies:
+        copy.wait()
+
+
+def placed(where, origins, pieces, so_far):
     count = len(pieces)
     return pl.pallas_call(
-        functools.partial(place_kernel, shifts),
+        functools.partial(place_kernel, origins),
         out_shape=(
             jax.ShapeDtypeStruct((2 * HALF, LANES), F32),
             jax.ShapeDtypeStruct((2 * HALF_LATE, LANES), F32),
@@ -376,8 +415,7 @@
         out_specs=(ANY, ANY),
         input_output_aliases={1 + count + n: n for n in range(len(so_far))},
         scratch_shapes=[
-            pltpu.VMEM((count, HALF // RING, LANES), F32),
-            pltpu.VMEM((count, HALF // RING, LANES), F32),
+            pltpu.VMEM((count, QUARTER + QUARTER_LATE, LANES), F32),
             pltpu.SemaphoreType.DMA((count, 2)),
         ],
         compiler_params=SMALL,
@@ -395,13 +433,17 @@
     hidden, volume, slope_early = early_layer(received, conv_early.reshape(16, 2 * LANES, LANES))
     activated, late, late_sent, error = late_layer(core.reshape(1), hidden, taps_late, signal)
     late_other = swapped(late_sent)
-    early, early_sent = backward(core.reshape(1), taps_late, volume, error, slope_early)
-    pieces = summed(core, early, swapped(early_sent), late, late_other)
+    error_early, volume_t = backward(taps_late, volume, error, slope_early)
+    early, early_sent, late_sum = early_grad(core.reshape(1), error_early, volume_t, late, late_other)
+    zero, one, two, three = summed(core, early, swapped(early_sent), late_sum)
     where = jnp.stack([core, ring_place(core), ring_place(1 - core)])
-    totals = placed(where, (0,), [pieces[0], swapped(pieces[0])], ())
-    *totals, one, three = lax.optimization_barrier((*totals, pieces[1], pieces[3]))
-    totals = placed(where, (1, 3), [one, swapped(one), three, swapped(three)], totals)
-    early_total, late_total = placed(where, (2,), [pieces[2], swapped(pieces[2])], totals)
+    totals = placed(where, ((0, 0), (0, 1)), [zero, swapped(zero)], ())
+    *totals, one, three = lax.optimization_barrier((*totals, one, three))
+    swaps = [swapped(piece) for piece in (one, three, two)]
+    totals = placed(where, ((1, 0), (3, 0)), [one, three], totals)
+    early_total, late_total = placed(
+        where, ((2, 0), (1, 1), (3, 1), (2, 1)), [two, *swaps], totals
+    )
     return (
         activated.reshape(cotangent.shape),
         early_total.reshape(conv_early.shape),

time: 89 us -> 89.9 us (1.010)
    ppermute x3, waiting for transfers between devices: 4.48 us -> 6.07 us  [summed(): lax.ppermute(quarter, FINE, shifts[by])]
    pallas_call x5 -> x9, Pallas kernels: 8.65 us -> 8.78 us  [the longest x3 4.97 us: placed(): pl.pallas_call(functools.partial(place_kernel, origins), out_shape=(jax.S...]
  transfers between devices with their start and end apart: 13 -> 13, of which waited for: 8 -> 6; matrix products, arithmetic and copies ran while one was open for 0% -> 0% of each run, Pallas kernels for 4% -> 5%
where the time goes in v3:
time: 89.9 us; the launch traced here: 89.7 us
  waiting for transfers between devices  30.9 us (34%)
  blocking collectives  24.9 us (28%)
  starting transfers between devices  19.5 us (22%)
  Pallas kernels  13.5 us (15%)
    all_to_all x2, blocking collectives, summed(): lax.all_to_all(blocks, FINE, split_axis=0, concat_axis=0, axis_index_grou...  24.9 us
    all_to_all x1, waiting for transfers between devices, per_device(): lax.all_to_all(sent, ('y', 'xh'), split_axis=0, concat_axis=0, tiled=True)  15.9 us
    all_to_all x1, starting transfers between devices, per_device(): lax.all_to_all(sent, ('y', 'xh'), split_axis=0, concat_axis=0, tiled=True)  7.62 us
    ppermute x3, waiting for transfers between devices, summed(): blocks[by] = lax.ppermute(blocks[by], FINE, shifts[by])  7.04 us
    ppermute x6, starting transfers between devices, swapped(): return lax.ppermute(block, 'core', [(0, 1), (1, 0)])  6.75 us
    ppermute x3, waiting for transfers between devices, summed(): lax.ppermute(quarter, FINE, shifts[by])  6.07 us
    pallas_call x3, Pallas kernels, placed(): pl.pallas_call(functools.partial(place_kernel, origins), out_shape=(jax.S...  4.97 us
    pallas_call x1, Pallas kernels, late_layer(): pl.pallas_call(late_kernel, out_shape=(jax.ShapeDtypeStruct((2, SIDE, SID...  3.26 us
  transfers between devices with their start and end apart: 13, of which 6 were waited for; matrix products, arithmetic and copies ran while one was open for 0% of the time, Pallas kernels for 5%

profile of v3, /device:TPU:1, one launch (start us, length us, event | category | flops | bytes accessed | tf_op | source)
XLA Modules:
  0.0 89.7 jit_solution(4844657897561566886)
XLA Ops:
  0.7 7.6 %all-to-all-start = ((bf16[8,2,4,64,128]{4,3,2,1,0:T(8,128)(2,1)}), bf16[8,2,4,64,128]{4,3,2,1,0:T(8,128)(2,1)S(1)}, u32[]{:S(2)}, u32[]{:S(2)}) async-start(bf16[8,2,4,64,128]{4,3,2,1,0:T(8,128)(2,1)} %bitcast.19), calls=%async_computation | async-start | bytes 2097152 | tf_op jit(solution)/shard_map/all_to_all | solution.py:430
  8.3 0.0 copy-start
  8.3 15.9 %all-to-all-done.received = bf16[8,2,4,64,128]{4,3,2,1,0:T(8,128)(2,1)S(1)} async-done(((bf16[8,2,4,64,128]{4,3,2,1,0:T(8,128)(2,1)}), bf16[8,2,4,64,128]{4,3,2,1,0:T(8,128)(2,1)S(1)}, u32[]{:S(2)}, u32[]{:S(2)}) %all-to-all-start) | async-done | bytes 1048608 | tf_op jit(solution)/shard_map/all_to_all | solution.py:430
  24.3 1.5 %shard_map.67 = (bf16[10,10,16,384]{3,2,1,0:T(8,128)(2,1)S(1)}, bf16[4,9,9,16,256]{4,3,2,1,0:T(8,128)(2,1)S(1)}, f32[1024,128]{1,0:T(8,128)S(1)}) custom-call(bf16[8,2,4,64,128]{4,3,2,1,0:T(8,128)(2,1)S(1)} %all-to-all-done.received, bf16[16,256,128]{2,1,0:T(8,128)(2,1)S(1)} %bitcast.16), custom_call_target="tpu_custom_call" | custom-call | flops 1073741824 | bytes 8388608 | tf_op jit(solution)/shard_map/pallas_call | solution.py:229
  25.8 3.3 %shard_map.68 = (bf16[2,8,64,128]{3,2,1,0:T(8,128)(2,1)}, bf16[1728,128]{1,0:T(8,128)(2,1)S(1)}, bf16[1728,128]{1,0:T(8,128)(2,1)S(1)}, bf16[10,10,16,384]{3,2,1,0:T(8,128)(2,1)S(1)}) custom-call(s32[1]{0:T(128)} %bitcast.core, bf16[10,10,16,384]{3,2,1,0:T(8,128)(2,1)S(1)} %get-tuple-element.29.hidden, bf16[9,384,128]{2,1,0:T(8,128)(2,1)S(1)} %bitcast.13, ...), custom_call_target="tpu_custom_call" | custom-call | flops 1811939328 | bytes 8388608 | tf_op jit(solution)/shard_map/pallas_call | solution.py:245
  29.0 2.2 %collective-permute-start = (bf16[1728,128]{1,0:T(8,128)(2,1)S(1)}, bf16[1728,128]{1,0:T(8,128)(2,1)S(1)}, u32[]{:S(2)}, u32[]{:S(2)}) collective-permute-start(bf16[1728,128]{1,0:T(8,128)(2,1)S(1)} %get-tuple-element.37), channel_id=1, source_target_pairs={{0,8},{8,0},{1,9},{9,1},{2,10},{10,2},{3,11},{11,3},{4,12},{12,4},... | collective-permute-start | bytes 1327112 | tf_op jit(solution)/shard_map/ppermute | solution.py:361
  31.3 1.7 %shard_map.69 = (bf16[10,10,16,128]{3,2,1,0:T(8,128)(2,1)S(1)}, bf16[4,256,1024]{2,1,0:T(8,128)(2,1)S(1)}) custom-call(bf16[9,384,128]{2,1,0:T(8,128)(2,1)S(1)} %bitcast.14, bf16[4,9,9,16,256]{4,3,2,1,0:T(8,128)(2,1)S(1)} %get-tuple-element.31.volume, bf16[10,10,16,384]{3,2,1,0:T(8,128)(2,1)S(1)} %get-tuple-element.32.error, ...), custom_call_target="tpu_custom_call" | custom-call | flops 905969664 | bytes 8388608 | tf_op jit(solution)/shard_map/pallas_call | solution.py:266
  33.0 1.7 %shard_map.70 = (bf16[2048,128]{1,0:T(8,128)(2,1)S(1)}, bf16[2048,128]{1,0:T(8,128)(2,1)S(1)}, bf16[1728,128]{1,0:T(8,128)(2,1)S(1)}) custom-call(s32[1]{0:T(128)} %bitcast.core, bf16[10,10,16,128]{3,2,1,0:T(8,128)(2,1)S(1)} %get-tuple-element.34.error_early, bf16[4,256,1024]{2,1,0:T(8,128)(2,1)S(1)} %get-tuple-element.35.volume_t, ...), custom_call_target="tpu_custom_call" | custom-call | flops 1073741824 | bytes 8388608 | tf_op jit(solution)/shard_map/pallas_call | solution.py:281
  34.7 0.2 collective-permute-start.1
  34.9 1.8 %collective-permute-done.1.early_other = bf16[2048,128]{1,0:T(8,128)(2,1)S(1)} collective-permute-done((bf16[2048,128]{1,0:T(8,128)(2,1)S(1)}, bf16[2048,128]{1,0:T(8,128)(2,1)S(1)}, u32[]{:S(2)}, u32[]{:S(2)}) %collective-permute-start.1) | collective-permute-done | bytes 524320 | tf_op jit(solution)/shard_map/ppermute | solution.py:361
  36.7 0.1 shard_map.71
  36.8 0.1 collective-permute-start.2
  36.9 1.7 %collective-permute-start.3 = (bf16[944,128]{1,0:T(8,128)(2,1)S(1)}, bf16[944,128]{1,0:T(8,128)(2,1)S(1)}, u32[]{:S(2)}, u32[]{:S(2)}) collective-permute-start(bf16[944,128]{1,0:T(8,128)(2,1)S(1)} %get-tuple-element.43), channel_id=1, source_target_pairs={{0,32},{1,33},{2,34},{3,35},{4,36},{5,37},{6,38},{7,39},{8,12},{9,... | collective-permute-start | bytes 725000 | tf_op jit(solution)/shard_map/ppermute | solution.py:371
  38.6 0.9 %collective-permute-start.4 = (bf16[944,128]{1,0:T(8,128)(2,1)S(1)}, bf16[944,128]{1,0:T(8,128)(2,1)S(1)}, u32[]{:S(2)}, u32[]{:S(2)}) collective-permute-start(bf16[944,128]{1,0:T(8,128)(2,1)S(1)} %get-tuple-element.44), channel_id=1, source_target_pairs={{0,48},{1,49},{2,50},{3,51},{4,52},{5,53},{6,54},{7,55},{8,14},{9,... | collective-permute-start | bytes 725000 | tf_op jit(solution)/shard_map/ppermute | solution.py:371
  39.6 6.1 %collective-permute-done.2.second = bf16[944,128]{1,0:T(8,128)(2,1)S(1)} collective-permute-done((bf16[944,128]{1,0:T(8,128)(2,1)S(1)}, bf16[944,128]{1,0:T(8,128)(2,1)S(1)}, u32[]{:S(2)}, u32[]{:S(2)}) %collective-permute-start.2) | collective-permute-done | bytes 241696 | tf_op jit(solution)/shard_map/ppermute | solution.py:371
  45.7 0.9 %collective-permute-done.4.fourth = bf16[944,128]{1,0:T(8,128)(2,1)S(1)} collective-permute-done((bf16[944,128]{1,0:T(8,128)(2,1)S(1)}, bf16[944,128]{1,0:T(8,128)(2,1)S(1)}, u32[]{:S(2)}, u32[]{:S(2)}) %collective-permute-start.4) | collective-permute-done | bytes 241696 | tf_op jit(solution)/shard_map/ppermute | solution.py:371
  46.6 0.2 shard_map.72
  46.8 13.7 %all_to_all.15.shares = bf16[16,64,128]{2,1,0:T(8,128)(2,1)S(1)} all-to-all(bf16[16,64,128]{2,1,0:T(8,128)(2,1)S(1)} %shard_map.72), channel_id=1, replica_groups={{0,1,2,3,4,5,6,7,64,65,66,67,68,69,70,71},{16,17,18,19,20,21,22,23,80,8..., dimensions={0} | all-to-all | bytes 524288 | tf_op jit(solution)/shard_map/all_to_all | solution.py:366
  60.6 11.2 %all_to_all.16.shares = bf16[16,64,128]{2,1,0:T(8,128)(2,1)S(1)} all-to-all(bf16[16,64,128]{2,1,0:T(8,128)(2,1)S(1)} %shard_map.73), channel_id=1, replica_groups={{0,1,2,3,4,5,6,7,64,65,66,67,68,69,70,71},{16,17,18,19,20,21,22,23,80,8..., dimensions={0} | all-to-all | bytes 524288 | tf_op jit(solution)/shard_map/all_to_all | solution.py:366
  71.8 1.2 %collective-permute-start.6 = (bf16[944,128]{1,0:T(8,128)(2,1)S(1)}, bf16[944,128]{1,0:T(8,128)(2,1)S(1)}, u32[]{:S(2)}, u32[]{:S(2)}) collective-permute-start(bf16[944,128]{1,0:T(8,128)(2,1)S(1)} %shard_map.74.refs_0_), channel_id=1, source_target_pairs={{0,8},{8,0},{1,9},{9,1},{2,10},{10,2},{3,11},{11,3},{4,12},{12,4},... | collective-permute-start | bytes 725000 | tf_op jit(solution)/shard_map/ppermute | solution.py:361
  73.0 1.0 %collective-permute-start.8 = (bf16[944,128]{1,0:T(8,128)(2,1)S(1)}, bf16[944,128]{1,0:T(8,128)(2,1)S(1)}, u32[]{:S(2)}, u32[]{:S(2)}) collective-permute-start(bf16[944,128]{1,0:T(8,128)(2,1)S(1)} %shard_map.74.refs_0_), channel_id=1, source_target_pairs={{0,48},{1,49},{2,50},{3,51},{4,52},{5,53},{6,54},{7,55},{8,14},{9,... | collective-permute-start | bytes 725000 | tf_op jit(solution)/shard_map/ppermute | solution.py:378
  74.0 0.5 collective-permute-start.7
  74.5 0.9 %collective-permute-start.5 = (bf16[944,128]{1,0:T(8,128)(2,1)S(1)}, bf16[944,128]{1,0:T(8,128)(2,1)S(1)}, u32[]{:S(2)}, u32[]{:S(2)}) collective-permute-start(bf16[944,128]{1,0:T(8,128)(2,1)S(1)} %shard_map.74.refs_0_), channel_id=1, source_target_pairs={{0,32},{1,33},{2,34},{3,35},{4,36},{5,37},{6,38},{7,39},{8,12},{9,... | collective-permute-start | bytes 725000 | tf_op jit(solution)/shard_map/ppermute | solution.py:378
  75.4 0.1 pad_add_fusion.where
  75.5 1.5 %shard_map.75 = (f32[4096,128]{1,0:T(8,128)}, f32[3456,128]{1,0:T(8,128)}) custom-call(s32[3]{0:T(128)S(1)} %pad_add_fusion.where, bf16[944,128]{1,0:T(8,128)(2,1)S(1)} %shard_map.74.refs_0_, bf16[944,128]{1,0:T(8,128)(2,1)S(1)} %collective-permute-done.6.refs_1_), custom_call_target="tpu_custom_call" | custom-call | bytes 1572864 | tf_op jit(solution)/shard_map/pallas_call | solution.py:408
  77.0 1.3 %collective-permute-done.8.refs_1_ = bf16[944,128]{1,0:T(8,128)(2,1)S(1)} collective-permute-done((bf16[944,128]{1,0:T(8,128)(2,1)S(1)}, bf16[944,128]{1,0:T(8,128)(2,1)S(1)}, u32[]{:S(2)}, u32[]{:S(2)}) %collective-permute-start.8) | collective-permute-done | bytes 241696 | tf_op jit(solution)/shard_map/ppermute | solution.py:378
  78.3 4.8 %collective-permute-done.7.refs_0_ = bf16[944,128]{1,0:T(8,128)(2,1)S(1)} collective-permute-done((bf16[944,128]{1,0:T(8,128)(2,1)S(1)}, bf16[944,128]{1,0:T(8,128)(2,1)S(1)}, u32[]{:S(2)}, u32[]{:S(2)}) %collective-permute-start.7) | collective-permute-done | bytes 241696 | tf_op jit(solution)/shard_map/ppermute | solution.py:378
  83.1 2.6 %collective-permute-start.9 = (bf16[944,128]{1,0:T(8,128)(2,1)S(1)}, bf16[944,128]{1,0:T(8,128)(2,1)S(1)}, u32[]{:S(2)}, u32[]{:S(2)}) collective-permute-start(bf16[944,128]{1,0:T(8,128)(2,1)S(1)} %collective-permute-done.7.refs_0_), channel_id=1, source_target_pairs={{0,8},{8,0},{1,9},{9,1},{2,10},{10,2},{3,11},{11,3},{4,12},{12,4},... | collective-permute-start | bytes 725000 | tf_op jit(solution)/shard_map/ppermute | solution.py:361
  85.7 0.0 collective-permute-start.11
  85.7 0.5 collective-permute-start.10
  86.2 1.5 %shard_map.76 = (f32[4096,128]{1,0:T(8,128)}, f32[3456,128]{1,0:T(8,128)}) custom-call(s32[3]{0:T(128)S(1)} %pad_add_fusion.where, bf16[944,128]{1,0:T(8,128)(2,1)S(1)} %collective-permute-done.7.refs_0_, bf16[944,128]{1,0:T(8,128)(2,1)S(1)} %collective-permute-done.8.refs_1_, ...), custom_call_target="tpu_custom_call", output_to_operand_aliasing={{0}: (3, {}), {1}: (4, {})} | custom-call | bytes 1572864 | tf_op jit(solution)/shard_map/pallas_call | solution.py:408
  87.8 1.9 %shard_map.77 = (f32[4096,128]{1,0:T(8,128)}, f32[3456,128]{1,0:T(8,128)}) custom-call(s32[3]{0:T(128)S(1)} %pad_add_fusion.where, bf16[944,128]{1,0:T(8,128)(2,1)S(1)} %collective-permute-done.5.refs_0_, bf16[944,128]{1,0:T(8,128)(2,1)S(1)} %collective-permute-done.9.refs_1_, ...), custom_call_target="tpu_custom_call", output_to_operand_aliasing={{0}: (5, {}), {1}: (6, {})} | custom-call | bytes 3145728 | tf_op jit(solution)/shard_map/pallas_call | solution.py:408
  (15 shorter events, 0.2 us)
Async XLA Ops:
  0.6 7.6 %copy-start.2 = (bf16[2,8,8,8,128]{4,3,2,1,0:T(8,128)(2,1)S(1)}, bf16[2,8,8,8,128]{4,3,2,1,0:T(8,128)(2,1)}, u32[]{:S(2)}) copy-start(bf16[2,8,8,8,128]{4,3,2,1,0:T(8,128)(2,1)} %param.7) | copy-start | bytes 786436
  0.6 23.6 %copy-start.1 = (bf16[4,4,4,64,128]{4,3,2,1,0:T(8,128)(2,1)S(1)}, bf16[4,4,4,64,128]{4,3,2,1,0:T(8,128)(2,1)}, u32[]{:S(2)}) copy-start(bf16[4,4,4,64,128]{4,3,2,1,0:T(8,128)(2,1)} %param.5) | copy-start | bytes 3145732
  0.7 23.6 %all-to-all-start = ((bf16[8,2,4,64,128]{4,3,2,1,0:T(8,128)(2,1)}), bf16[8,2,4,64,128]{4,3,2,1,0:T(8,128)(2,1)S(1)}, u32[]{:S(2)}, u32[]{:S(2)}) async-start(bf16[8,2,4,64,128]{4,3,2,1,0:T(8,128)(2,1)} %bitcast.19), calls=%async_computation | async-start | bytes 2097152 | tf_op jit(solution)/shard_map/all_to_all | solution.py:430
  8.3 17.4 %copy-start = (bf16[3,3,3,128,128]{4,3,2,1,0:T(8,128)(2,1)S(1)}, bf16[3,3,3,128,128]{4,3,2,1,0:T(8,128)(2,1)}, u32[]{:S(2)}) copy-start(bf16[3,3,3,128,128]{4,3,2,1,0:T(8,128)(2,1)} %param.6) | copy-start | bytes 2654212
  29.0 3.9 %collective-permute-start = (bf16[1728,128]{1,0:T(8,128)(2,1)S(1)}, bf16[1728,128]{1,0:T(8,128)(2,1)S(1)}, u32[]{:S(2)}, u32[]{:S(2)}) collective-permute-start(bf16[1728,128]{1,0:T(8,128)(2,1)S(1)} %get-tuple-element.37), channel_id=1, source_target_pairs={{0,8},{8,0},{1,9},{9,1},{2,10},{10,2},{3,11},{11,3},{4,12},{12,4},... | collective-permute-start | bytes 1327112 | tf_op jit(solution)/shard_map/ppermute | solution.py:361
  34.7 2.0 %collective-permute-start.1 = (bf16[2048,128]{1,0:T(8,128)(2,1)S(1)}, bf16[2048,128]{1,0:T(8,128)(2,1)S(1)}, u32[]{:S(2)}, u32[]{:S(2)}) collective-permute-start(bf16[2048,128]{1,0:T(8,128)(2,1)S(1)} %get-tuple-element.39), channel_id=1, source_target_pairs={{0,8},{8,0},{1,9},{9,1},{2,10},{10,2},{3,11},{11,3},{4,12},{12,4},... | collective-permute-start | bytes 1572872 | tf_op jit(solution)/shard_map/ppermute | solution.py:361
  36.8 8.9 %collective-permute-start.2 = (bf16[944,128]{1,0:T(8,128)(2,1)S(1)}, bf16[944,128]{1,0:T(8,128)(2,1)S(1)}, u32[]{:S(2)}, u32[]{:S(2)}) collective-permute-start(bf16[944,128]{1,0:T(8,128)(2,1)S(1)} %get-tuple-element.42), channel_id=1, source_target_pairs={{0,16},{1,17},{2,18},{3,19},{4,20},{5,21},{6,22},{7,23},{8,10},{9,... | collective-permute-start | bytes 725000 | tf_op jit(solution)/shard_map/ppermute | solution.py:371
  36.9 8.8 %collective-permute-start.3 = (bf16[944,128]{1,0:T(8,128)(2,1)S(1)}, bf16[944,128]{1,0:T(8,128)(2,1)S(1)}, u32[]{:S(2)}, u32[]{:S(2)}) collective-permute-start(bf16[944,128]{1,0:T(8,128)(2,1)S(1)} %get-tuple-element.43), channel_id=1, source_target_pairs={{0,32},{1,33},{2,34},{3,35},{4,36},{5,37},{6,38},{7,39},{8,12},{9,... | collective-permute-start | bytes 725000 | tf_op jit(solution)/shard_map/ppermute | solution.py:371
  38.6 8.0 %collective-permute-start.4 = (bf16[944,128]{1,0:T(8,128)(2,1)S(1)}, bf16[944,128]{1,0:T(8,128)(2,1)S(1)}, u32[]{:S(2)}, u32[]{:S(2)}) collective-permute-start(bf16[944,128]{1,0:T(8,128)(2,1)S(1)} %get-tuple-element.44), channel_id=1, source_target_pairs={{0,48},{1,49},{2,50},{3,51},{4,52},{5,53},{6,54},{7,55},{8,14},{9,... | collective-permute-start | bytes 725000 | tf_op jit(solution)/shard_map/ppermute | solution.py:371
  71.8 3.7 %collective-permute-start.6 = (bf16[944,128]{1,0:T(8,128)(2,1)S(1)}, bf16[944,128]{1,0:T(8,128)(2,1)S(1)}, u32[]{:S(2)}, u32[]{:S(2)}) collective-permute-start(bf16[944,128]{1,0:T(8,128)(2,1)S(1)} %shard_map.74.refs_0_), channel_id=1, source_target_pairs={{0,8},{8,0},{1,9},{9,1},{2,10},{10,2},{3,11},{11,3},{4,12},{12,4},... | collective-permute-start | bytes 725000 | tf_op jit(solution)/shard_map/ppermute | solution.py:361
  73.0 5.3 %collective-permute-start.8 = (bf16[944,128]{1,0:T(8,128)(2,1)S(1)}, bf16[944,128]{1,0:T(8,128)(2,1)S(1)}, u32[]{:S(2)}, u32[]{:S(2)}) collective-permute-start(bf16[944,128]{1,0:T(8,128)(2,1)S(1)} %shard_map.74.refs_0_), channel_id=1, source_target_pairs={{0,48},{1,49},{2,50},{3,51},{4,52},{5,53},{6,54},{7,55},{8,14},{9,... | collective-permute-start | bytes 725000 | tf_op jit(solution)/shard_map/ppermute | solution.py:378
  74.0 9.1 %collective-permute-start.7 = (bf16[944,128]{1,0:T(8,128)(2,1)S(1)}, bf16[944,128]{1,0:T(8,128)(2,1)S(1)}, u32[]{:S(2)}, u32[]{:S(2)}) collective-permute-start(bf16[944,128]{1,0:T(8,128)(2,1)S(1)} %shard_map.74.refs_0_), channel_id=1, source_target_pairs={{0,16},{1,17},{2,18},{3,19},{4,20},{5,21},{6,22},{7,23},{8,10},{9,... | collective-permute-start | bytes 725000 | tf_op jit(solution)/shard_map/ppermute | solution.py:378
  74.5 11.2 %collective-permute-start.5 = (bf16[944,128]{1,0:T(8,128)(2,1)S(1)}, bf16[944,128]{1,0:T(8,128)(2,1)S(1)}, u32[]{:S(2)}, u32[]{:S(2)}) collective-permute-start(bf16[944,128]{1,0:T(8,128)(2,1)S(1)} %shard_map.74.refs_0_), channel_id=1, source_target_pairs={{0,32},{1,33},{2,34},{3,35},{4,36},{5,37},{6,38},{7,39},{8,12},{9,... | collective-permute-start | bytes 725000 | tf_op jit(solution)/shard_map/ppermute | solution.py:378
  83.1 4.7 %collective-permute-start.9 = (bf16[944,128]{1,0:T(8,128)(2,1)S(1)}, bf16[944,128]{1,0:T(8,128)(2,1)S(1)}, u32[]{:S(2)}, u32[]{:S(2)}) collective-permute-start(bf16[944,128]{1,0:T(8,128)(2,1)S(1)} %collective-permute-done.7.refs_0_), channel_id=1, source_target_pairs={{0,8},{8,0},{1,9},{9,1},{2,10},{10,2},{3,11},{11,3},{4,12},{12,4},... | collective-permute-start | bytes 725000 | tf_op jit(solution)/shard_map/ppermute | solution.py:361
  85.7 2.1 %collective-permute-start.11 = (bf16[944,128]{1,0:T(8,128)(2,1)S(1)}, bf16[944,128]{1,0:T(8,128)(2,1)S(1)}, u32[]{:S(2)}, u32[]{:S(2)}) collective-permute-start(bf16[944,128]{1,0:T(8,128)(2,1)S(1)} %collective-permute-done.5.refs_0_), channel_id=1, source_target_pairs={{0,8},{8,0},{1,9},{9,1},{2,10},{10,2},{3,11},{11,3},{4,12},{12,4},... | collective-permute-start | bytes 725000 | tf_op jit(solution)/shard_map/ppermute | solution.py:361
  85.7 2.1 %collective-permute-start.10 = (bf16[944,128]{1,0:T(8,128)(2,1)S(1)}, bf16[944,128]{1,0:T(8,128)(2,1)S(1)}, u32[]{:S(2)}, u32[]{:S(2)}) collective-permute-start(bf16[944,128]{1,0:T(8,128)(2,1)S(1)} %collective-permute-done.8.refs_1_), channel_id=1, source_target_pairs={{0,8},{8,0},{1,9},{9,1},{2,10},{10,2},{3,11},{11,3},{4,12},{12,4},... | collective-permute-start | bytes 725000 | tf_op jit(solution)/shard_map/ppermute | solution.py:361

commit v4 on v3

--- a/solution.py
+++ b/solution.py
@@ -367,15 +367,15 @@
         blocks, FINE, split_axis=0, concat_axis=0, axis_index_groups=planes, tiled=True
     )
     blocks = list(pair_sums(ring_place(core), early, early_other, late_sum))
-    for by in range(1, RING):
-        blocks[by] = lax.ppermute(blocks[by], FINE, shifts[by])
+    order = (2, 1, 3)
+    others = [lax.ppermute(blocks[by], FINE, shifts[by]) for by in order]
     shares = jax.ShapeDtypeStruct((16, 2 * SHARE, LANES), BF16)
     uneven = [pltpu.VMEM((QUARTER_LATE + 8, LANES), F32)]
-    sent = exchange(small_call(ring_kernel, shares, uneven, *blocks))
+    sent = exchange(small_call(ring_kernel, shares, uneven, blocks[0], *others))
     spread = exchange(small_call(share_kernel, shares, [], sent))
     rows = jax.ShapeDtypeStruct((QUARTER + QUARTER_LATE, LANES), BF16)
     quarter = small_call(join_kernel, rows, uneven, spread)
-    return [quarter] + [lax.ppermute(quarter, FINE, shifts[by]) for by in range(1, RING)]
+    return [quarter] + [lax.ppermute(quarter, FINE, shifts[by]) for by in order]
 
 
 def place_kernel(origins, where, *refs):
@@ -435,15 +435,13 @@
     late_other = swapped(late_sent)
     error_early, volume_t = backward(taps_late, volume, error, slope_early)
     early, early_sent, late_sum = early_grad(core.reshape(1), error_early, volume_t, late, late_other)
-    zero, one, two, three = summed(core, early, swapped(early_sent), late_sum)
+    zero, two, one, three = summed(core, early, swapped(early_sent), late_sum)
     where = jnp.stack([core, ring_place(core), ring_place(1 - core)])
     totals = placed(where, ((0, 0), (0, 1)), [zero, swapped(zero)], ())
-    *totals, one, three = lax.optimization_barrier((*totals, one, three))
-    swaps = [swapped(piece) for piece in (one, three, two)]
-    totals = placed(where, ((1, 0), (3, 0)), [one, three], totals)
-    early_total, late_total = placed(
-        where, ((2, 0), (1, 1), (3, 1), (2, 1)), [two, *swaps], totals
-    )
+    *totals, three, one, two = lax.optimization_barrier((*totals, three, one, two))
+    swaps = [swapped(piece) for piece in (two, one, three)]
+    totals = placed(where, ((2, 0), (1, 0)), [two, one], totals)
+    early_total, late_total = placed(where, ((3, 0), (2, 1), (1, 1), (3, 1)), [three, *swaps], totals)
     return (
         activated.reshape(cotangent.shape),
         early_total.reshape(conv_early.shape),

time: 89.9 us -> 87.2 us (0.970)
  waiting for transfers between devices: 30.9 us -> 28.1 us
    ppermute x6, waiting for transfers between devices: 13.1 us -> 10.3 us  [the longest x3 6.14 us: summed(): others = [lax.ppermute(blocks[by], FINE, shifts[by]) for by in order]]
    ppermute x6, starting transfers between devices: 5.13 us -> 6.9 us  [the longest x3 3.57 us: summed(): return [quarter] + [lax.ppermute(quarter, FINE, shifts[by]) for by in order]]
    ppermute x6, starting transfers between devices: 6.75 us -> 5.25 us  [swapped(): return lax.ppermute(block, 'core', [(0, 1), (1, 0)])]
where the time goes in v4:
time: 87.2 us; the launch traced here: 86.9 us
  waiting for transfers between devices  28.1 us (32%)
  blocking collectives  24.6 us (28%)
  starting transfers between devices  19.8 us (23%)
  Pallas kernels  13.5 us (15%)
    all_to_all x2, blocking collectives, summed(): lax.all_to_all(blocks, FINE, split_axis=0, concat_axis=0, axis_index_grou...  24.6 us
    all_to_all x1, waiting for transfers between devices, per_device(): lax.all_to_all(sent, ('y', 'xh'), split_axis=0, concat_axis=0, tiled=True)  15.9 us
    all_to_all x1, starting transfers between devices, per_device(): lax.all_to_all(sent, ('y', 'xh'), split_axis=0, concat_axis=0, tiled=True)  7.62 us
    ppermute x3, waiting for transfers between devices, summed(): others = [lax.ppermute(blocks[by], FINE, shifts[by]) for by in order]  6.14 us
    ppermute x6, starting transfers between devices, swapped(): return lax.ppermute(block, 'core', [(0, 1), (1, 0)])  5.25 us
    pallas_call x3, Pallas kernels, placed(): pl.pallas_call(functools.partial(place_kernel, origins), out_shape=(jax.S...  4.97 us
    ppermute x3, waiting for transfers between devices, summed(): return [quarter] + [lax.ppermute(quarter, FINE, shifts[by]) for by in order]  4.2 us
    ppermute x3, starting transfers between devices, summed(): return [quarter] + [lax.ppermute(quarter, FINE, shifts[by]) for by in order]  3.57 us
  transfers between devices with their start and end apart: 13, of which 6 were waited for; matrix products, arithmetic and copies ran while one was open for 0% of the time, Pallas kernels for 5%

profile of v4, /device:TPU:1, one launch (start us, length us, event | category | flops | bytes accessed | tf_op | source)
XLA Modules:
  0.0 86.9 jit_solution(5927840779151472229)
XLA Ops:
  0.7 7.6 %all-to-all-start = ((bf16[8,2,4,64,128]{4,3,2,1,0:T(8,128)(2,1)}), bf16[8,2,4,64,128]{4,3,2,1,0:T(8,128)(2,1)S(1)}, u32[]{:S(2)}, u32[]{:S(2)}) async-start(bf16[8,2,4,64,128]{4,3,2,1,0:T(8,128)(2,1)} %bitcast.19), calls=%async_computation | async-start | bytes 2097152 | tf_op jit(solution)/shard_map/all_to_all | solution.py:430
  8.3 0.0 copy-start
  8.3 15.9 %all-to-all-done.received = bf16[8,2,4,64,128]{4,3,2,1,0:T(8,128)(2,1)S(1)} async-done(((bf16[8,2,4,64,128]{4,3,2,1,0:T(8,128)(2,1)}), bf16[8,2,4,64,128]{4,3,2,1,0:T(8,128)(2,1)S(1)}, u32[]{:S(2)}, u32[]{:S(2)}) %all-to-all-start) | async-done | bytes 1048608 | tf_op jit(solution)/shard_map/all_to_all | solution.py:430
  24.3 1.5 %shard_map.67 = (bf16[10,10,16,384]{3,2,1,0:T(8,128)(2,1)S(1)}, bf16[4,9,9,16,256]{4,3,2,1,0:T(8,128)(2,1)S(1)}, f32[1024,128]{1,0:T(8,128)S(1)}) custom-call(bf16[8,2,4,64,128]{4,3,2,1,0:T(8,128)(2,1)S(1)} %all-to-all-done.received, bf16[16,256,128]{2,1,0:T(8,128)(2,1)S(1)} %bitcast.16), custom_call_target="tpu_custom_call" | custom-call | flops 1073741824 | bytes 8388608 | tf_op jit(solution)/shard_map/pallas_call | solution.py:229
  25.8 3.3 %shard_map.68 = (bf16[2,8,64,128]{3,2,1,0:T(8,128)(2,1)}, bf16[1728,128]{1,0:T(8,128)(2,1)S(1)}, bf16[1728,128]{1,0:T(8,128)(2,1)S(1)}, bf16[10,10,16,384]{3,2,1,0:T(8,128)(2,1)S(1)}) custom-call(s32[1]{0:T(128)} %bitcast.core, bf16[10,10,16,384]{3,2,1,0:T(8,128)(2,1)S(1)} %get-tuple-element.30.hidden, bf16[9,384,128]{2,1,0:T(8,128)(2,1)S(1)} %bitcast.13, ...), custom_call_target="tpu_custom_call" | custom-call | flops 1811939328 | bytes 8388608 | tf_op jit(solution)/shard_map/pallas_call | solution.py:245
  29.0 2.2 %collective-permute-start = (bf16[1728,128]{1,0:T(8,128)(2,1)S(1)}, bf16[1728,128]{1,0:T(8,128)(2,1)S(1)}, u32[]{:S(2)}, u32[]{:S(2)}) collective-permute-start(bf16[1728,128]{1,0:T(8,128)(2,1)S(1)} %get-tuple-element.38), channel_id=1, source_target_pairs={{0,8},{8,0},{1,9},{9,1},{2,10},{10,2},{3,11},{11,3},{4,12},{12,4},... | collective-permute-start | bytes 1327112 | tf_op jit(solution)/shard_map/ppermute | solution.py:361
  31.3 1.7 %shard_map.69 = (bf16[10,10,16,128]{3,2,1,0:T(8,128)(2,1)S(1)}, bf16[4,256,1024]{2,1,0:T(8,128)(2,1)S(1)}) custom-call(bf16[9,384,128]{2,1,0:T(8,128)(2,1)S(1)} %bitcast.14, bf16[4,9,9,16,256]{4,3,2,1,0:T(8,128)(2,1)S(1)} %get-tuple-element.32.volume, bf16[10,10,16,384]{3,2,1,0:T(8,128)(2,1)S(1)} %get-tuple-element.33.error, ...), custom_call_target="tpu_custom_call" | custom-call | flops 905969664 | bytes 8388608 | tf_op jit(solution)/shard_map/pallas_call | solution.py:266
  33.0 1.7 %shard_map.70 = (bf16[2048,128]{1,0:T(8,128)(2,1)S(1)}, bf16[2048,128]{1,0:T(8,128)(2,1)S(1)}, bf16[1728,128]{1,0:T(8,128)(2,1)S(1)}) custom-call(s32[1]{0:T(128)} %bitcast.core, bf16[10,10,16,128]{3,2,1,0:T(8,128)(2,1)S(1)} %get-tuple-element.35.error_early, bf16[4,256,1024]{2,1,0:T(8,128)(2,1)S(1)} %get-tuple-element.36.volume_t, ...), custom_call_target="tpu_custom_call" | custom-call | flops 1073741824 | bytes 8388608 | tf_op jit(solution)/shard_map/pallas_call | solution.py:281
  34.7 0.2 collective-permute-start.1
  34.9 1.8 %collective-permute-done.1.early_other = bf16[2048,128]{1,0:T(8,128)(2,1)S(1)} collective-permute-done((bf16[2048,128]{1,0:T(8,128)(2,1)S(1)}, bf16[2048,128]{1,0:T(8,128)(2,1)S(1)}, u32[]{:S(2)}, u32[]{:S(2)}) %collective-permute-start.1) | collective-permute-done | bytes 524320 | tf_op jit(solution)/shard_map/ppermute | solution.py:361
  36.7 0.1 shard_map.71
  36.8 0.7 collective-permute-start.2
  37.5 0.6 collective-permute-start.3
  38.1 2.1 %collective-permute-start.4 = (bf16[944,128]{1,0:T(8,128)(2,1)S(1)}, bf16[944,128]{1,0:T(8,128)(2,1)S(1)}, u32[]{:S(2)}, u32[]{:S(2)}) collective-permute-start(bf16[944,128]{1,0:T(8,128)(2,1)S(1)} %get-tuple-element.45), channel_id=1, source_target_pairs={{0,48},{1,49},{2,50},{3,51},{4,52},{5,53},{6,54},{7,55},{8,14},{9,... | collective-permute-start | bytes 725000 | tf_op jit(solution)/shard_map/ppermute | solution.py:371
  40.2 3.6 %collective-permute-done.2.second = bf16[944,128]{1,0:T(8,128)(2,1)S(1)} collective-permute-done((bf16[944,128]{1,0:T(8,128)(2,1)S(1)}, bf16[944,128]{1,0:T(8,128)(2,1)S(1)}, u32[]{:S(2)}, u32[]{:S(2)}) %collective-permute-start.2) | collective-permute-done | bytes 241696 | tf_op jit(solution)/shard_map/ppermute | solution.py:371
  43.7 2.5 %collective-permute-done.3.third = bf16[944,128]{1,0:T(8,128)(2,1)S(1)} collective-permute-done((bf16[944,128]{1,0:T(8,128)(2,1)S(1)}, bf16[944,128]{1,0:T(8,128)(2,1)S(1)}, u32[]{:S(2)}, u32[]{:S(2)}) %collective-permute-start.3) | collective-permute-done | bytes 241696 | tf_op jit(solution)/shard_map/ppermute | solution.py:371
  46.3 0.2 shard_map.72
  46.5 13.4 %all_to_all.15.shares = bf16[16,64,128]{2,1,0:T(8,128)(2,1)S(1)} all-to-all(bf16[16,64,128]{2,1,0:T(8,128)(2,1)S(1)} %shard_map.72), channel_id=1, replica_groups={{0,1,2,3,4,5,6,7,64,65,66,67,68,69,70,71},{16,17,18,19,20,21,22,23,80,8..., dimensions={0} | all-to-all | bytes 524288 | tf_op jit(solution)/shard_map/all_to_all | solution.py:366
  60.0 11.2 %all_to_all.16.shares = bf16[16,64,128]{2,1,0:T(8,128)(2,1)S(1)} all-to-all(bf16[16,64,128]{2,1,0:T(8,128)(2,1)S(1)} %shard_map.73), channel_id=1, replica_groups={{0,1,2,3,4,5,6,7,64,65,66,67,68,69,70,71},{16,17,18,19,20,21,22,23,80,8..., dimensions={0} | all-to-all | bytes 524288 | tf_op jit(solution)/shard_map/all_to_all | solution.py:366
  71.2 1.4 %collective-permute-start.5 = (bf16[944,128]{1,0:T(8,128)(2,1)S(1)}, bf16[944,128]{1,0:T(8,128)(2,1)S(1)}, u32[]{:S(2)}, u32[]{:S(2)}) collective-permute-start(bf16[944,128]{1,0:T(8,128)(2,1)S(1)} %shard_map.74.refs_0_), channel_id=1, source_target_pairs={{0,8},{8,0},{1,9},{9,1},{2,10},{10,2},{3,11},{11,3},{4,12},{12,4},... | collective-permute-start | bytes 725000 | tf_op jit(solution)/shard_map/ppermute | solution.py:361
  72.6 0.9 %collective-permute-start.8 = (bf16[944,128]{1,0:T(8,128)(2,1)S(1)}, bf16[944,128]{1,0:T(8,128)(2,1)S(1)}, u32[]{:S(2)}, u32[]{:S(2)}) collective-permute-start(bf16[944,128]{1,0:T(8,128)(2,1)S(1)} %shard_map.74.refs_0_), channel_id=1, source_target_pairs={{0,32},{1,33},{2,34},{3,35},{4,36},{5,37},{6,38},{7,39},{8,12},{9,... | collective-permute-start | bytes 725000 | tf_op jit(solution)/shard_map/ppermute | solution.py:378
  73.5 0.6 collective-permute-start.7
  74.1 2.1 %collective-permute-start.6 = (bf16[944,128]{1,0:T(8,128)(2,1)S(1)}, bf16[944,128]{1,0:T(8,128)(2,1)S(1)}, u32[]{:S(2)}, u32[]{:S(2)}) collective-permute-start(bf16[944,128]{1,0:T(8,128)(2,1)S(1)} %shard_map.74.refs_0_), channel_id=1, source_target_pairs={{0,48},{1,49},{2,50},{3,51},{4,52},{5,53},{6,54},{7,55},{8,14},{9,... | collective-permute-start | bytes 725000 | tf_op jit(solution)/shard_map/ppermute | solution.py:378
  76.2 0.1 pad_add_fusion.where
  76.3 1.5 %shard_map.75 = (f32[4096,128]{1,0:T(8,128)}, f32[3456,128]{1,0:T(8,128)}) custom-call(s32[3]{0:T(128)S(1)} %pad_add_fusion.where, bf16[944,128]{1,0:T(8,128)(2,1)S(1)} %shard_map.74.refs_0_, bf16[944,128]{1,0:T(8,128)(2,1)S(1)} %collective-permute-done.5.refs_1_), custom_call_target="tpu_custom_call" | custom-call | bytes 1572864 | tf_op jit(solution)/shard_map/pallas_call | solution.py:408
  77.8 1.7 %collective-permute-done.8.refs_0_ = bf16[944,128]{1,0:T(8,128)(2,1)S(1)} collective-permute-done((bf16[944,128]{1,0:T(8,128)(2,1)S(1)}, bf16[944,128]{1,0:T(8,128)(2,1)S(1)}, u32[]{:S(2)}, u32[]{:S(2)}) %collective-permute-start.8) | collective-permute-done | bytes 241696 | tf_op jit(solution)/shard_map/ppermute | solution.py:378
  79.5 2.5 %collective-permute-done.7.refs_1_ = bf16[944,128]{1,0:T(8,128)(2,1)S(1)} collective-permute-done((bf16[944,128]{1,0:T(8,128)(2,1)S(1)}, bf16[944,128]{1,0:T(8,128)(2,1)S(1)}, u32[]{:S(2)}, u32[]{:S(2)}) %collective-permute-start.7) | collective-permute-done | bytes 241696 | tf_op jit(solution)/shard_map/ppermute | solution.py:378
  82.0 0.9 %collective-permute-start.11 = (bf16[944,128]{1,0:T(8,128)(2,1)S(1)}, bf16[944,128]{1,0:T(8,128)(2,1)S(1)}, u32[]{:S(2)}, u32[]{:S(2)}) collective-permute-start(bf16[944,128]{1,0:T(8,128)(2,1)S(1)} %collective-permute-done.6.refs_0_), channel_id=1, source_target_pairs={{0,8},{8,0},{1,9},{9,1},{2,10},{10,2},{3,11},{11,3},{4,12},{12,4},... | collective-permute-start | bytes 725000 | tf_op jit(solution)/shard_map/ppermute | solution.py:361
  83.0 0.0 collective-permute-start.9
  83.0 0.5 collective-permute-start.10
  83.5 1.5 %shard_map.76 = (f32[4096,128]{1,0:T(8,128)}, f32[3456,128]{1,0:T(8,128)}) custom-call(s32[3]{0:T(128)S(1)} %pad_add_fusion.where, bf16[944,128]{1,0:T(8,128)(2,1)S(1)} %collective-permute-done.8.refs_0_, bf16[944,128]{1,0:T(8,128)(2,1)S(1)} %collective-permute-done.7.refs_1_, ...), custom_call_target="tpu_custom_call", output_to_operand_aliasing={{0}: (3, {}), {1}: (4, {})} | custom-call | bytes 1572864 | tf_op jit(solution)/shard_map/pallas_call | solution.py:408
  85.1 1.9 %shard_map.77 = (f32[4096,128]{1,0:T(8,128)}, f32[3456,128]{1,0:T(8,128)}) custom-call(s32[3]{0:T(128)S(1)} %pad_add_fusion.where, bf16[944,128]{1,0:T(8,128)(2,1)S(1)} %collective-permute-done.6.refs_0_, bf16[944,128]{1,0:T(8,128)(2,1)S(1)} %collective-permute-done.9.refs_1_, ...), custom_call_target="tpu_custom_call", output_to_operand_aliasing={{0}: (5, {}), {1}: (6, {})} | custom-call | bytes 3145728 | tf_op jit(solution)/shard_map/pallas_call | solution.py:408
  (15 shorter events, 0.2 us)
Async XLA Ops:
  0.6 7.6 %copy-start.2 = (bf16[2,8,8,8,128]{4,3,2,1,0:T(8,128)(2,1)S(1)}, bf16[2,8,8,8,128]{4,3,2,1,0:T(8,128)(2,1)}, u32[]{:S(2)}) copy-start(bf16[2,8,8,8,128]{4,3,2,1,0:T(8,128)(2,1)} %param.7) | copy-start | bytes 786436
  0.6 23.6 %copy-start.1 = (bf16[4,4,4,64,128]{4,3,2,1,0:T(8,128)(2,1)S(1)}, bf16[4,4,4,64,128]{4,3,2,1,0:T(8,128)(2,1)}, u32[]{:S(2)}) copy-start(bf16[4,4,4,64,128]{4,3,2,1,0:T(8,128)(2,1)} %param.5) | copy-start | bytes 3145732
  0.7 23.6 %all-to-all-start = ((bf16[8,2,4,64,128]{4,3,2,1,0:T(8,128)(2,1)}), bf16[8,2,4,64,128]{4,3,2,1,0:T(8,128)(2,1)S(1)}, u32[]{:S(2)}, u32[]{:S(2)}) async-start(bf16[8,2,4,64,128]{4,3,2,1,0:T(8,128)(2,1)} %bitcast.19), calls=%async_computation | async-start | bytes 2097152 | tf_op jit(solution)/shard_map/all_to_all | solution.py:430
  8.3 17.4 %copy-start = (bf16[3,3,3,128,128]{4,3,2,1,0:T(8,128)(2,1)S(1)}, bf16[3,3,3,128,128]{4,3,2,1,0:T(8,128)(2,1)}, u32[]{:S(2)}) copy-start(bf16[3,3,3,128,128]{4,3,2,1,0:T(8,128)(2,1)} %param.6) | copy-start | bytes 2654212
  29.0 3.9 %collective-permute-start = (bf16[1728,128]{1,0:T(8,128)(2,1)S(1)}, bf16[1728,128]{1,0:T(8,128)(2,1)S(1)}, u32[]{:S(2)}, u32[]{:S(2)}) collective-permute-start(bf16[1728,128]{1,0:T(8,128)(2,1)S(1)} %get-tuple-element.38), channel_id=1, source_target_pairs={{0,8},{8,0},{1,9},{9,1},{2,10},{10,2},{3,11},{11,3},{4,12},{12,4},... | collective-permute-start | bytes 1327112 | tf_op jit(solution)/shard_map/ppermute | solution.py:361
  34.7 2.0 %collective-permute-start.1 = (bf16[2048,128]{1,0:T(8,128)(2,1)S(1)}, bf16[2048,128]{1,0:T(8,128)(2,1)S(1)}, u32[]{:S(2)}, u32[]{:S(2)}) collective-permute-start(bf16[2048,128]{1,0:T(8,128)(2,1)S(1)} %get-tuple-element.40), channel_id=1, source_target_pairs={{0,8},{8,0},{1,9},{9,1},{2,10},{10,2},{3,11},{11,3},{4,12},{12,4},... | collective-permute-start | bytes 1572872 | tf_op jit(solution)/shard_map/ppermute | solution.py:361
  36.8 6.9 %collective-permute-start.2 = (bf16[944,128]{1,0:T(8,128)(2,1)S(1)}, bf16[944,128]{1,0:T(8,128)(2,1)S(1)}, u32[]{:S(2)}, u32[]{:S(2)}) collective-permute-start(bf16[944,128]{1,0:T(8,128)(2,1)S(1)} %get-tuple-element.43), channel_id=1, source_target_pairs={{0,32},{1,33},{2,34},{3,35},{4,36},{5,37},{6,38},{7,39},{8,12},{9,... | collective-permute-start | bytes 725000 | tf_op jit(solution)/shard_map/ppermute | solution.py:371
  37.5 8.8 %collective-permute-start.3 = (bf16[944,128]{1,0:T(8,128)(2,1)S(1)}, bf16[944,128]{1,0:T(8,128)(2,1)S(1)}, u32[]{:S(2)}, u32[]{:S(2)}) collective-permute-start(bf16[944,128]{1,0:T(8,128)(2,1)S(1)} %get-tuple-element.44), channel_id=1, source_target_pairs={{0,16},{1,17},{2,18},{3,19},{4,20},{5,21},{6,22},{7,23},{8,10},{9,... | collective-permute-start | bytes 725000 | tf_op jit(solution)/shard_map/ppermute | solution.py:371
  38.1 8.2 %collective-permute-start.4 = (bf16[944,128]{1,0:T(8,128)(2,1)S(1)}, bf16[944,128]{1,0:T(8,128)(2,1)S(1)}, u32[]{:S(2)}, u32[]{:S(2)}) collective-permute-start(bf16[944,128]{1,0:T(8,128)(2,1)S(1)} %get-tuple-element.45), channel_id=1, source_target_pairs={{0,48},{1,49},{2,50},{3,51},{4,52},{5,53},{6,54},{7,55},{8,14},{9,... | collective-permute-start | bytes 725000 | tf_op jit(solution)/shard_map/ppermute | solution.py:371
  71.2 5.0 %collective-permute-start.5 = (bf16[944,128]{1,0:T(8,128)(2,1)S(1)}, bf16[944,128]{1,0:T(8,128)(2,1)S(1)}, u32[]{:S(2)}, u32[]{:S(2)}) collective-permute-start(bf16[944,128]{1,0:T(8,128)(2,1)S(1)} %shard_map.74.refs_0_), channel_id=1, source_target_pairs={{0,8},{8,0},{1,9},{9,1},{2,10},{10,2},{3,11},{11,3},{4,12},{12,4},... | collective-permute-start | bytes 725000 | tf_op jit(solution)/shard_map/ppermute | solution.py:361
  72.6 6.8 %collective-permute-start.8 = (bf16[944,128]{1,0:T(8,128)(2,1)S(1)}, bf16[944,128]{1,0:T(8,128)(2,1)S(1)}, u32[]{:S(2)}, u32[]{:S(2)}) collective-permute-start(bf16[944,128]{1,0:T(8,128)(2,1)S(1)} %shard_map.74.refs_0_), channel_id=1, source_target_pairs={{0,32},{1,33},{2,34},{3,35},{4,36},{5,37},{6,38},{7,39},{8,12},{9,... | collective-permute-start | bytes 725000 | tf_op jit(solution)/shard_map/ppermute | solution.py:378
  73.5 8.5 %collective-permute-start.7 = (bf16[944,128]{1,0:T(8,128)(2,1)S(1)}, bf16[944,128]{1,0:T(8,128)(2,1)S(1)}, u32[]{:S(2)}, u32[]{:S(2)}) collective-permute-start(bf16[944,128]{1,0:T(8,128)(2,1)S(1)} %shard_map.74.refs_0_), channel_id=1, source_target_pairs={{0,16},{1,17},{2,18},{3,19},{4,20},{5,21},{6,22},{7,23},{8,10},{9,... | collective-permute-start | bytes 725000 | tf_op jit(solution)/shard_map/ppermute | solution.py:378
  74.1 7.9 %collective-permute-start.6 = (bf16[944,128]{1,0:T(8,128)(2,1)S(1)}, bf16[944,128]{1,0:T(8,128)(2,1)S(1)}, u32[]{:S(2)}, u32[]{:S(2)}) collective-permute-start(bf16[944,128]{1,0:T(8,128)(2,1)S(1)} %shard_map.74.refs_0_), channel_id=1, source_target_pairs={{0,48},{1,49},{2,50},{3,51},{4,52},{5,53},{6,54},{7,55},{8,14},{9,... | collective-permute-start | bytes 725000 | tf_op jit(solution)/shard_map/ppermute | solution.py:378
  82.0 3.0 %collective-permute-start.11 = (bf16[944,128]{1,0:T(8,128)(2,1)S(1)}, bf16[944,128]{1,0:T(8,128)(2,1)S(1)}, u32[]{:S(2)}, u32[]{:S(2)}) collective-permute-start(bf16[944,128]{1,0:T(8,128)(2,1)S(1)} %collective-permute-done.6.refs_0_), channel_id=1, source_target_pairs={{0,8},{8,0},{1,9},{9,1},{2,10},{10,2},{3,11},{11,3},{4,12},{12,4},... | collective-permute-start | bytes 725000 | tf_op jit(solution)/shard_map/ppermute | solution.py:361
  83.0 2.1 %collective-permute-start.9 = (bf16[944,128]{1,0:T(8,128)(2,1)S(1)}, bf16[944,128]{1,0:T(8,128)(2,1)S(1)}, u32[]{:S(2)}, u32[]{:S(2)}) collective-permute-start(bf16[944,128]{1,0:T(8,128)(2,1)S(1)} %collective-permute-done.8.refs_0_), channel_id=1, source_target_pairs={{0,8},{8,0},{1,9},{9,1},{2,10},{10,2},{3,11},{11,3},{4,12},{12,4},... | collective-permute-start | bytes 725000 | tf_op jit(solution)/shard_map/ppermute | solution.py:361
  83.0 2.1 %collective-permute-start.10 = (bf16[944,128]{1,0:T(8,128)(2,1)S(1)}, bf16[944,128]{1,0:T(8,128)(2,1)S(1)}, u32[]{:S(2)}, u32[]{:S(2)}) collective-permute-start(bf16[944,128]{1,0:T(8,128)(2,1)S(1)} %collective-permute-done.7.refs_1_), channel_id=1, source_target_pairs={{0,8},{8,0},{1,9},{9,1},{2,10},{10,2},{3,11},{11,3},{4,12},{12,4},... | collective-permute-start | bytes 725000 | tf_op jit(solution)/shard_map/ppermute | solution.py:361

commit v5 on v4

--- a/solution.py
+++ b/solution.py
@@ -378,12 +378,12 @@
     return [quarter] + [lax.ppermute(quarter, FINE, shifts[by]) for by in order]
 
 
-def place_kernel(origins, where, *refs):
+def place_kernel(origins, core, place, other_place, *refs):
     early, late, wide, sems = refs[-4:]
     copies = []
     for n, (shift, other) in enumerate(origins):
-        half = where[0] ^ other
-        quarter = (where[1 + other] - shift + RING) % RING
+        half = core[0] ^ other
+        quarter = ((other_place if other else place)[0] - shift + RING) % RING
         wide[n] = refs[n][...].astype(F32)
         at_early = pl.multiple_of(half * HALF + quarter * QUARTER, QUARTER)
         at_late = pl.multiple_of(half * HALF_LATE + quarter * QUARTER_LATE, 16)
@@ -403,7 +403,7 @@
         copy.wait()
 
 
-def placed(where, origins, pieces, so_far):
+def placed(scalars, origins, pieces, so_far):
     count = len(pieces)
     return pl.pallas_call(
         functools.partial(place_kernel, origins),
@@ -411,16 +411,16 @@
             jax.ShapeDtypeStruct((2 * HALF, LANES), F32),
             jax.ShapeDtypeStruct((2 * HALF_LATE, LANES), F32),
         ),
-        in_specs=[SMEM] + [VMEM] * count + [ANY] * len(so_far),
+        in_specs=[SMEM] * 3 + [VMEM] * count + [ANY] * len(so_far),
         out_specs=(ANY, ANY),
-        input_output_aliases={1 + count + n: n for n in range(len(so_far))},
+        input_output_aliases={3 + count + n: n for n in range(len(so_far))},
         scratch_shapes=[
             pltpu.VMEM((count, QUARTER + QUARTER_LATE, LANES), F32),
             pltpu.SemaphoreType.DMA((count, 2)),
         ],
         compiler_params=SMALL,
         cost_estimate=pl.CostEstimate(flops=0, bytes_accessed=count * 768 * 1024, transcendentals=0),
-    )(where, *pieces, *so_far)
+    )(*scalars, *pieces, *so_far)
 
 
 def per_device(inputs, conv_early, conv_late, cotangent):
@@ -436,12 +436,12 @@
     error_early, volume_t = backward(taps_late, volume, error, slope_early)
     early, early_sent, late_sum = early_grad(core.reshape(1), error_early, volume_t, late, late_other)
     zero, two, one, three = summed(core, early, swapped(early_sent), late_sum)
-    where = jnp.stack([core, ring_place(core), ring_place(1 - core)])
-    totals = placed(where, ((0, 0), (0, 1)), [zero, swapped(zero)], ())
+    scalars = [value.reshape(1) for value in (core, ring_place(core), ring_place(1 - core))]
+    totals = placed(scalars, ((0, 0), (0, 1)), [zero, swapped(zero)], ())
     *totals, three, one, two = lax.optimization_barrier((*totals, three, one, two))
     swaps = [swapped(piece) for piece in (two, one, three)]
-    totals = placed(where, ((2, 0), (1, 0)), [two, one], totals)
-    early_total, late_total = placed(where, ((3, 0), (2, 1), (1, 1), (3, 1)), [three, *swaps], totals)
+    totals = placed(scalars, ((2, 0), (1, 0)), [two, one], totals)
+    early_total, late_total = placed(scalars, ((3, 0), (2, 1), (1, 1), (3, 1)), [three, *swaps], totals)
     return (
         activated.reshape(cotangent.shape),
         early_total.reshape(conv_early.shape),

time: 87.2 us -> 86.4 us (level)
  Pallas kernels: 13.5 us -> 11.9 us
  waiting for transfers between devices: 28.1 us -> 29 us
    pallas_call x3, Pallas kernels: 4.97 us -> 3.34 us  [placed(): pl.pallas_call(functools.partial(place_kernel, origins), out_shape=(jax.S...]
  transfers between devices with their start and end apart: 13 -> 13, of which waited for: 6 -> 7; matrix products, arithmetic and copies ran while one was open for 0% -> 0% of each run, Pallas kernels for 5% -> 4%
where the time goes in v5:
time: 86.4 us; the launch traced here: 86.2 us
  waiting for transfers between devices  29 us (34%)
  blocking collectives  24.6 us (28%)
  starting transfers between devices  19.8 us (23%)
  Pallas kernels  11.9 us (14%)
    all_to_all x2, blocking collectives, summed(): lax.all_to_all(blocks, FINE, split_axis=0, concat_axis=0, axis_index_grou...  24.6 us
    all_to_all x1, waiting for transfers between devices, per_device(): lax.all_to_all(sent, ('y', 'xh'), split_axis=0, concat_axis=0, tiled=True)  15.9 us
    all_to_all x1, starting transfers between devices, per_device(): lax.all_to_all(sent, ('y', 'xh'), split_axis=0, concat_axis=0, tiled=True)  7.62 us
    ppermute x3, waiting for transfers between devices, summed(): others = [lax.ppermute(blocks[by], FINE, shifts[by]) for by in order]  6.14 us
    ppermute x6, starting transfers between devices, swapped(): return lax.ppermute(block, 'core', [(0, 1), (1, 0)])  5.25 us
    ppermute x3, waiting for transfers between devices, summed(): return [quarter] + [lax.ppermute(quarter, FINE, shifts[by]) for by in order]  4.82 us
    ppermute x3, starting transfers between devices, summed(): return [quarter] + [lax.ppermute(quarter, FINE, shifts[by]) for by in order]  3.57 us
    pallas_call x3, Pallas kernels, placed(): pl.pallas_call(functools.partial(place_kernel, origins), out_shape=(jax.S...  3.34 us
  transfers between devices with their start and end apart: 13, of which 7 were waited for; matrix products, arithmetic and copies ran while one was open for 0% of the time, Pallas kernels for 4%

profile of v5, /device:TPU:1, one launch (start us, length us, event | category | flops | bytes accessed | tf_op | source)
XLA Modules:
  0.0 86.2 jit_solution(8040433684995950410)
XLA Ops:
  0.7 7.6 %all-to-all-start = ((bf16[8,2,4,64,128]{4,3,2,1,0:T(8,128)(2,1)}), bf16[8,2,4,64,128]{4,3,2,1,0:T(8,128)(2,1)S(1)}, u32[]{:S(2)}, u32[]{:S(2)}) async-start(bf16[8,2,4,64,128]{4,3,2,1,0:T(8,128)(2,1)} %bitcast.19), calls=%async_computation | async-start | bytes 2097152 | tf_op jit(solution)/shard_map/all_to_all | solution.py:430
  8.3 0.0 copy-start
  8.3 15.9 %all-to-all-done.received = bf16[8,2,4,64,128]{4,3,2,1,0:T(8,128)(2,1)S(1)} async-done(((bf16[8,2,4,64,128]{4,3,2,1,0:T(8,128)(2,1)}), bf16[8,2,4,64,128]{4,3,2,1,0:T(8,128)(2,1)S(1)}, u32[]{:S(2)}, u32[]{:S(2)}) %all-to-all-start) | async-done | bytes 1048608 | tf_op jit(solution)/shard_map/all_to_all | solution.py:430
  24.3 1.5 %shard_map.67 = (bf16[10,10,16,384]{3,2,1,0:T(8,128)(2,1)S(1)}, bf16[4,9,9,16,256]{4,3,2,1,0:T(8,128)(2,1)S(1)}, f32[1024,128]{1,0:T(8,128)S(1)}) custom-call(bf16[8,2,4,64,128]{4,3,2,1,0:T(8,128)(2,1)S(1)} %all-to-all-done.received, bf16[16,256,128]{2,1,0:T(8,128)(2,1)S(1)} %bitcast.16), custom_call_target="tpu_custom_call" | custom-call | flops 1073741824 | bytes 8388608 | tf_op jit(solution)/shard_map/pallas_call | solution.py:229
  25.8 3.3 %shard_map.68 = (bf16[2,8,64,128]{3,2,1,0:T(8,128)(2,1)}, bf16[1728,128]{1,0:T(8,128)(2,1)S(1)}, bf16[1728,128]{1,0:T(8,128)(2,1)S(1)}, bf16[10,10,16,384]{3,2,1,0:T(8,128)(2,1)S(1)}) custom-call(s32[1]{0:T(128)} %bitcast.core, bf16[10,10,16,384]{3,2,1,0:T(8,128)(2,1)S(1)} %get-tuple-element.30.hidden, bf16[9,384,128]{2,1,0:T(8,128)(2,1)S(1)} %bitcast.13, ...), custom_call_target="tpu_custom_call" | custom-call | flops 1811939328 | bytes 8388608 | tf_op jit(solution)/shard_map/pallas_call | solution.py:245
  29.0 2.2 %collective-permute-start = (bf16[1728,128]{1,0:T(8,128)(2,1)S(1)}, bf16[1728,128]{1,0:T(8,128)(2,1)S(1)}, u32[]{:S(2)}, u32[]{:S(2)}) collective-permute-start(bf16[1728,128]{1,0:T(8,128)(2,1)S(1)} %get-tuple-element.38), channel_id=1, source_target_pairs={{0,8},{8,0},{1,9},{9,1},{2,10},{10,2},{3,11},{11,3},{4,12},{12,4},... | collective-permute-start | bytes 1327112 | tf_op jit(solution)/shard_map/ppermute | solution.py:361
  31.3 1.7 %shard_map.69 = (bf16[10,10,16,128]{3,2,1,0:T(8,128)(2,1)S(1)}, bf16[4,256,1024]{2,1,0:T(8,128)(2,1)S(1)}) custom-call(bf16[9,384,128]{2,1,0:T(8,128)(2,1)S(1)} %bitcast.14, bf16[4,9,9,16,256]{4,3,2,1,0:T(8,128)(2,1)S(1)} %get-tuple-element.32.volume, bf16[10,10,16,384]{3,2,1,0:T(8,128)(2,1)S(1)} %get-tuple-element.33.error, ...), custom_call_target="tpu_custom_call" | custom-call | flops 905969664 | bytes 8388608 | tf_op jit(solution)/shard_map/pallas_call | solution.py:266
  33.0 1.7 %shard_map.70 = (bf16[2048,128]{1,0:T(8,128)(2,1)S(1)}, bf16[2048,128]{1,0:T(8,128)(2,1)S(1)}, bf16[1728,128]{1,0:T(8,128)(2,1)S(1)}) custom-call(s32[1]{0:T(128)} %bitcast.core, bf16[10,10,16,128]{3,2,1,0:T(8,128)(2,1)S(1)} %get-tuple-element.35.error_early, bf16[4,256,1024]{2,1,0:T(8,128)(2,1)S(1)} %get-tuple-element.36.volume_t, ...), custom_call_target="tpu_custom_call" | custom-call | flops 1073741824 | bytes 8388608 | tf_op jit(solution)/shard_map/pallas_call | solution.py:281
  34.7 0.2 collective-permute-start.1
  34.9 1.8 %collective-permute-done.1.early_other = bf16[2048,128]{1,0:T(8,128)(2,1)S(1)} collective-permute-done((bf16[2048,128]{1,0:T(8,128)(2,1)S(1)}, bf16[2048,128]{1,0:T(8,128)(2,1)S(1)}, u32[]{:S(2)}, u32[]{:S(2)}) %collective-permute-start.1) | collective-permute-done | bytes 524320 | tf_op jit(solution)/shard_map/ppermute | solution.py:361
  36.7 0.1 shard_map.71
  36.8 0.7 collective-permute-start.2
  37.5 0.6 collective-permute-start.3
  38.1 2.1 %collective-permute-start.4 = (bf16[944,128]{1,0:T(8,128)(2,1)S(1)}, bf16[944,128]{1,0:T(8,128)(2,1)S(1)}, u32[]{:S(2)}, u32[]{:S(2)}) collective-permute-start(bf16[944,128]{1,0:T(8,128)(2,1)S(1)} %get-tuple-element.45), channel_id=1, source_target_pairs={{0,48},{1,49},{2,50},{3,51},{4,52},{5,53},{6,54},{7,55},{8,14},{9,... | collective-permute-start | bytes 725000 | tf_op jit(solution)/shard_map/ppermute | solution.py:371
  40.2 3.6 %collective-permute-done.2.second = bf16[944,128]{1,0:T(8,128)(2,1)S(1)} collective-permute-done((bf16[944,128]{1,0:T(8,128)(2,1)S(1)}, bf16[944,128]{1,0:T(8,128)(2,1)S(1)}, u32[]{:S(2)}, u32[]{:S(2)}) %collective-permute-start.2) | collective-permute-done | bytes 241696 | tf_op jit(solution)/shard_map/ppermute | solution.py:371
  43.7 2.5 %collective-permute-done.3.third = bf16[944,128]{1,0:T(8,128)(2,1)S(1)} collective-permute-done((bf16[944,128]{1,0:T(8,128)(2,1)S(1)}, bf16[944,128]{1,0:T(8,128)(2,1)S(1)}, u32[]{:S(2)}, u32[]{:S(2)}) %collective-permute-start.3) | collective-permute-done | bytes 241696 | tf_op jit(solution)/shard_map/ppermute | solution.py:371
  46.3 0.2 shard_map.72
  46.5 13.4 %all_to_all.15.shares = bf16[16,64,128]{2,1,0:T(8,128)(2,1)S(1)} all-to-all(bf16[16,64,128]{2,1,0:T(8,128)(2,1)S(1)} %shard_map.72), channel_id=1, replica_groups={{0,1,2,3,4,5,6,7,64,65,66,67,68,69,70,71},{16,17,18,19,20,21,22,23,80,8..., dimensions={0} | all-to-all | bytes 524288 | tf_op jit(solution)/shard_map/all_to_all | solution.py:366
  60.0 11.2 %all_to_all.16.shares = bf16[16,64,128]{2,1,0:T(8,128)(2,1)S(1)} all-to-all(bf16[16,64,128]{2,1,0:T(8,128)(2,1)S(1)} %shard_map.73), channel_id=1, replica_groups={{0,1,2,3,4,5,6,7,64,65,66,67,68,69,70,71},{16,17,18,19,20,21,22,23,80,8..., dimensions={0} | all-to-all | bytes 524288 | tf_op jit(solution)/shard_map/all_to_all | solution.py:366
  71.2 1.4 %collective-permute-start.5 = (bf16[944,128]{1,0:T(8,128)(2,1)S(1)}, bf16[944,128]{1,0:T(8,128)(2,1)S(1)}, u32[]{:S(2)}, u32[]{:S(2)}) collective-permute-start(bf16[944,128]{1,0:T(8,128)(2,1)S(1)} %shard_map.74.refs_0_), channel_id=1, source_target_pairs={{0,8},{8,0},{1,9},{9,1},{2,10},{10,2},{3,11},{11,3},{4,12},{12,4},... | collective-permute-start | bytes 725000 | tf_op jit(solution)/shard_map/ppermute | solution.py:361
  72.6 0.9 %collective-permute-start.8 = (bf16[944,128]{1,0:T(8,128)(2,1)S(1)}, bf16[944,128]{1,0:T(8,128)(2,1)S(1)}, u32[]{:S(2)}, u32[]{:S(2)}) collective-permute-start(bf16[944,128]{1,0:T(8,128)(2,1)S(1)} %shard_map.74.refs_0_), channel_id=1, source_target_pairs={{0,32},{1,33},{2,34},{3,35},{4,36},{5,37},{6,38},{7,39},{8,12},{9,... | collective-permute-start | bytes 725000 | tf_op jit(solution)/shard_map/ppermute | solution.py:378
  73.5 0.6 collective-permute-start.7
  74.1 2.1 %collective-permute-start.6 = (bf16[944,128]{1,0:T(8,128)(2,1)S(1)}, bf16[944,128]{1,0:T(8,128)(2,1)S(1)}, u32[]{:S(2)}, u32[]{:S(2)}) collective-permute-start(bf16[944,128]{1,0:T(8,128)(2,1)S(1)} %shard_map.74.refs_0_), channel_id=1, source_target_pairs={{0,48},{1,49},{2,50},{3,51},{4,52},{5,53},{6,54},{7,55},{8,14},{9,... | collective-permute-start | bytes 725000 | tf_op jit(solution)/shard_map/ppermute | solution.py:378
  76.2 1.0 %shard_map.75 = (f32[4096,128]{1,0:T(8,128)}, f32[3456,128]{1,0:T(8,128)}) custom-call(s32[1]{0:T(128)} %bitcast.core, s32[1]{0:T(128)} %bitcast.8.place, s32[1]{0:T(128)} %bitcast.9.other_place, bf16[944,128]{1,0:T(8,128)(2,1)S(1)} %shard_map.74.refs_0_, bf16[944,128]{1,0:T(8,128)(2,1)S(1)} %collective-permute-done.5.refs_1_), custom_call_target="tpu_custom_call" | custom-call | bytes 1572864 | tf_op jit(solution)/shard_map/pallas_call | solution.py:408
  77.2 2.3 %collective-permute-done.8.refs_0_ = bf16[944,128]{1,0:T(8,128)(2,1)S(1)} collective-permute-done((bf16[944,128]{1,0:T(8,128)(2,1)S(1)}, bf16[944,128]{1,0:T(8,128)(2,1)S(1)}, u32[]{:S(2)}, u32[]{:S(2)}) %collective-permute-start.8) | collective-permute-done | bytes 241696 | tf_op jit(solution)/shard_map/ppermute | solution.py:378
  79.5 2.5 %collective-permute-done.7.refs_1_ = bf16[944,128]{1,0:T(8,128)(2,1)S(1)} collective-permute-done((bf16[944,128]{1,0:T(8,128)(2,1)S(1)}, bf16[944,128]{1,0:T(8,128)(2,1)S(1)}, u32[]{:S(2)}, u32[]{:S(2)}) %collective-permute-start.7) | collective-permute-done | bytes 241696 | tf_op jit(solution)/shard_map/ppermute | solution.py:378
  82.0 0.9 %collective-permute-start.11 = (bf16[944,128]{1,0:T(8,128)(2,1)S(1)}, bf16[944,128]{1,0:T(8,128)(2,1)S(1)}, u32[]{:S(2)}, u32[]{:S(2)}) collective-permute-start(bf16[944,128]{1,0:T(8,128)(2,1)S(1)} %collective-permute-done.6.refs_0_), channel_id=1, source_target_pairs={{0,8},{8,0},{1,9},{9,1},{2,10},{10,2},{3,11},{11,3},{4,12},{12,4},... | collective-permute-start | bytes 725000 | tf_op jit(solution)/shard_map/ppermute | solution.py:361
  83.0 0.0 collective-permute-start.9
  83.0 0.5 collective-permute-start.10
  83.5 1.0 %shard_map.76 = (f32[4096,128]{1,0:T(8,128)}, f32[3456,128]{1,0:T(8,128)}) custom-call(s32[1]{0:T(128)} %bitcast.core, s32[1]{0:T(128)} %bitcast.8.place, s32[1]{0:T(128)} %bitcast.9.other_place, bf16[944,128]{1,0:T(8,128)(2,1)S(1)} %collective-permute-done.8.refs_0_, ...), custom_call_target="tpu_custom_call", output_to_operand_aliasing={{0}: (5, {}), {1}: (6, {})} | custom-call | bytes 1572864 | tf_op jit(solution)/shard_map/pallas_call | solution.py:408
  84.5 0.3 collective-permute-done.10.refs_2_
  84.8 1.3 %shard_map.77 = (f32[4096,128]{1,0:T(8,128)}, f32[3456,128]{1,0:T(8,128)}) custom-call(s32[1]{0:T(128)} %bitcast.core, s32[1]{0:T(128)} %bitcast.8.place, s32[1]{0:T(128)} %bitcast.9.other_place, bf16[944,128]{1,0:T(8,128)(2,1)S(1)} %collective-permute-done.6.refs_0_, ...), custom_call_target="tpu_custom_call", output_to_operand_aliasing={{0}: (7, {}), {1}: (8, {})} | custom-call | bytes 3145728 | tf_op jit(solution)/shard_map/pallas_call | solution.py:408
  (14 shorter events, 0.2 us)
Async XLA Ops:
  0.6 7.6 %copy-start.2 = (bf16[2,8,8,8,128]{4,3,2,1,0:T(8,128)(2,1)S(1)}, bf16[2,8,8,8,128]{4,3,2,1,0:T(8,128)(2,1)}, u32[]{:S(2)}) copy-start(bf16[2,8,8,8,128]{4,3,2,1,0:T(8,128)(2,1)} %param.7) | copy-start | bytes 786436
  0.6 23.6 %copy-start.1 = (bf16[4,4,4,64,128]{4,3,2,1,0:T(8,128)(2,1)S(1)}, bf16[4,4,4,64,128]{4,3,2,1,0:T(8,128)(2,1)}, u32[]{:S(2)}) copy-start(bf16[4,4,4,64,128]{4,3,2,1,0:T(8,128)(2,1)} %param.5) | copy-start | bytes 3145732
  0.7 23.6 %all-to-all-start = ((bf16[8,2,4,64,128]{4,3,2,1,0:T(8,128)(2,1)}), bf16[8,2,4,64,128]{4,3,2,1,0:T(8,128)(2,1)S(1)}, u32[]{:S(2)}, u32[]{:S(2)}) async-start(bf16[8,2,4,64,128]{4,3,2,1,0:T(8,128)(2,1)} %bitcast.19), calls=%async_computation | async-start | bytes 2097152 | tf_op jit(solution)/shard_map/all_to_all | solution.py:430
  8.3 17.4 %copy-start = (bf16[3,3,3,128,128]{4,3,2,1,0:T(8,128)(2,1)S(1)}, bf16[3,3,3,128,128]{4,3,2,1,0:T(8,128)(2,1)}, u32[]{:S(2)}) copy-start(bf16[3,3,3,128,128]{4,3,2,1,0:T(8,128)(2,1)} %param.6) | copy-start | bytes 2654212
  29.0 3.9 %collective-permute-start = (bf16[1728,128]{1,0:T(8,128)(2,1)S(1)}, bf16[1728,128]{1,0:T(8,128)(2,1)S(1)}, u32[]{:S(2)}, u32[]{:S(2)}) collective-permute-start(bf16[1728,128]{1,0:T(8,128)(2,1)S(1)} %get-tuple-element.38), channel_id=1, source_target_pairs={{0,8},{8,0},{1,9},{9,1},{2,10},{10,2},{3,11},{11,3},{4,12},{12,4},... | collective-permute-start | bytes 1327112 | tf_op jit(solution)/shard_map/ppermute | solution.py:361
  34.7 2.0 %collective-permute-start.1 = (bf16[2048,128]{1,0:T(8,128)(2,1)S(1)}, bf16[2048,128]{1,0:T(8,128)(2,1)S(1)}, u32[]{:S(2)}, u32[]{:S(2)}) collective-permute-start(bf16[2048,128]{1,0:T(8,128)(2,1)S(1)} %get-tuple-element.40), channel_id=1, source_target_pairs={{0,8},{8,0},{1,9},{9,1},{2,10},{10,2},{3,11},{11,3},{4,12},{12,4},... | collective-permute-start | bytes 1572872 | tf_op jit(solution)/shard_map/ppermute | solution.py:361
  36.8 6.9 %collective-permute-start.2 = (bf16[944,128]{1,0:T(8,128)(2,1)S(1)}, bf16[944,128]{1,0:T(8,128)(2,1)S(1)}, u32[]{:S(2)}, u32[]{:S(2)}) collective-permute-start(bf16[944,128]{1,0:T(8,128)(2,1)S(1)} %get-tuple-element.43), channel_id=1, source_target_pairs={{0,32},{1,33},{2,34},{3,35},{4,36},{5,37},{6,38},{7,39},{8,12},{9,... | collective-permute-start | bytes 725000 | tf_op jit(solution)/shard_map/ppermute | solution.py:371
  37.5 8.8 %collective-permute-start.3 = (bf16[944,128]{1,0:T(8,128)(2,1)S(1)}, bf16[944,128]{1,0:T(8,128)(2,1)S(1)}, u32[]{:S(2)}, u32[]{:S(2)}) collective-permute-start(bf16[944,128]{1,0:T(8,128)(2,1)S(1)} %get-tuple-element.44), channel_id=1, source_target_pairs={{0,16},{1,17},{2,18},{3,19},{4,20},{5,21},{6,22},{7,23},{8,10},{9,... | collective-permute-start | bytes 725000 | tf_op jit(solution)/shard_map/ppermute | solution.py:371
  38.1 8.2 %collective-permute-start.4 = (bf16[944,128]{1,0:T(8,128)(2,1)S(1)}, bf16[944,128]{1,0:T(8,128)(2,1)S(1)}, u32[]{:S(2)}, u32[]{:S(2)}) collective-permute-start(bf16[944,128]{1,0:T(8,128)(2,1)S(1)} %get-tuple-element.45), channel_id=1, source_target_pairs={{0,48},{1,49},{2,50},{3,51},{4,52},{5,53},{6,54},{7,55},{8,14},{9,... | collective-permute-start | bytes 725000 | tf_op jit(solution)/shard_map/ppermute | solution.py:371
  71.2 5.0 %collective-permute-start.5 = (bf16[944,128]{1,0:T(8,128)(2,1)S(1)}, bf16[944,128]{1,0:T(8,128)(2,1)S(1)}, u32[]{:S(2)}, u32[]{:S(2)}) collective-permute-start(bf16[944,128]{1,0:T(8,128)(2,1)S(1)} %shard_map.74.refs_0_), channel_id=1, source_target_pairs={{0,8},{8,0},{1,9},{9,1},{2,10},{10,2},{3,11},{11,3},{4,12},{12,4},... | collective-permute-start | bytes 725000 | tf_op jit(solution)/shard_map/ppermute | solution.py:361
  72.6 6.8 %collective-permute-start.8 = (bf16[944,128]{1,0:T(8,128)(2,1)S(1)}, bf16[944,128]{1,0:T(8,128)(2,1)S(1)}, u32[]{:S(2)}, u32[]{:S(2)}) collective-permute-start(bf16[944,128]{1,0:T(8,128)(2,1)S(1)} %shard_map.74.refs_0_), channel_id=1, source_target_pairs={{0,32},{1,33},{2,34},{3,35},{4,36},{5,37},{6,38},{7,39},{8,12},{9,... | collective-permute-start | bytes 725000 | tf_op jit(solution)/shard_map/ppermute | solution.py:378
  73.5 8.5 %collective-permute-start.7 = (bf16[944,128]{1,0:T(8,128)(2,1)S(1)}, bf16[944,128]{1,0:T(8,128)(2,1)S(1)}, u32[]{:S(2)}, u32[]{:S(2)}) collective-permute-start(bf16[944,128]{1,0:T(8,128)(2,1)S(1)} %shard_map.74.refs_0_), channel_id=1, source_target_pairs={{0,16},{1,17},{2,18},{3,19},{4,20},{5,21},{6,22},{7,23},{8,10},{9,... | collective-permute-start | bytes 725000 | tf_op jit(solution)/shard_map/ppermute | solution.py:378
  74.1 7.9 %collective-permute-start.6 = (bf16[944,128]{1,0:T(8,128)(2,1)S(1)}, bf16[944,128]{1,0:T(8,128)(2,1)S(1)}, u32[]{:S(2)}, u32[]{:S(2)}) collective-permute-start(bf16[944,128]{1,0:T(8,128)(2,1)S(1)} %shard_map.74.refs_0_), channel_id=1, source_target_pairs={{0,48},{1,49},{2,50},{3,51},{4,52},{5,53},{6,54},{7,55},{8,14},{9,... | collective-permute-start | bytes 725000 | tf_op jit(solution)/shard_map/ppermute | solution.py:378
  82.0 2.5 %collective-permute-start.11 = (bf16[944,128]{1,0:T(8,128)(2,1)S(1)}, bf16[944,128]{1,0:T(8,128)(2,1)S(1)}, u32[]{:S(2)}, u32[]{:S(2)}) collective-permute-start(bf16[944,128]{1,0:T(8,128)(2,1)S(1)} %collective-permute-done.6.refs_0_), channel_id=1, source_target_pairs={{0,8},{8,0},{1,9},{9,1},{2,10},{10,2},{3,11},{11,3},{4,12},{12,4},... | collective-permute-start | bytes 725000 | tf_op jit(solution)/shard_map/ppermute | solution.py:361
  83.0 1.5 %collective-permute-start.9 = (bf16[944,128]{1,0:T(8,128)(2,1)S(1)}, bf16[944,128]{1,0:T(8,128)(2,1)S(1)}, u32[]{:S(2)}, u32[]{:S(2)}) collective-permute-start(bf16[944,128]{1,0:T(8,128)(2,1)S(1)} %collective-permute-done.8.refs_0_), channel_id=1, source_target_pairs={{0,8},{8,0},{1,9},{9,1},{2,10},{10,2},{3,11},{11,3},{4,12},{12,4},... | collective-permute-start | bytes 725000 | tf_op jit(solution)/shard_map/ppermute | solution.py:361
  83.0 1.8 %collective-permute-start.10 = (bf16[944,128]{1,0:T(8,128)(2,1)S(1)}, bf16[944,128]{1,0:T(8,128)(2,1)S(1)}, u32[]{:S(2)}, u32[]{:S(2)}) collective-permute-start(bf16[944,128]{1,0:T(8,128)(2,1)S(1)} %collective-permute-done.7.refs_1_), channel_id=1, source_target_pairs={{0,8},{8,0},{1,9},{9,1},{2,10},{10,2},{3,11},{11,3},{4,12},{12,4},... | collective-permute-start | bytes 725000 | tf_op jit(solution)/shard_map/ppermute | solution.py:361

commit v6 on v5

--- a/solution.py
+++ b/solution.py
@@ -438,10 +438,11 @@
     zero, two, one, three = summed(core, early, swapped(early_sent), late_sum)
     scalars = [value.reshape(1) for value in (core, ring_place(core), ring_place(1 - core))]
     totals = placed(scalars, ((0, 0), (0, 1)), [zero, swapped(zero)], ())
-    *totals, three, one, two = lax.optimization_barrier((*totals, three, one, two))
-    swaps = [swapped(piece) for piece in (two, one, three)]
-    totals = placed(scalars, ((2, 0), (1, 0)), [two, one], totals)
-    early_total, late_total = placed(scalars, ((3, 0), (2, 1), (1, 1), (3, 1)), [three, *swaps], totals)
+    *totals, three, one = lax.optimization_barrier((*totals, three, one))
+    totals = placed(scalars, ((2, 0), (2, 1)), [two, swapped(two)], totals)
+    early_total, late_total = placed(
+        scalars, ((1, 0), (3, 0), (1, 1), (3, 1)), [one, three, swapped(one), swapped(three)], totals
+    )
     return (
         activated.reshape(cotangent.shape),
         early_total.reshape(conv_early.shape),

time: 86.4 us -> 86 us (level)
  waiting for transfers between devices: 29 us -> 25 us
  starting transfers between devices: 19.8 us -> 23.3 us
    ppermute x6, starting transfers between devices: 5.25 us -> 9.62 us  [swapped(): return lax.ppermute(block, 'core', [(0, 1), (1, 0)])]
    ppermute x3, waiting for transfers between devices: 4.82 us -> 0.64 us  [summed(): return [quarter] + [lax.ppermute(quarter, FINE, shifts[by]) for by in order]]
  transfers between devices with their start and end apart: 13 -> 13, of which waited for: 7 -> 8; matrix products, arithmetic and copies ran while one was open for 0% -> 0% of each run, Pallas kernels for 4% -> 4%
where the time goes in v6:
time: 86 us; the launch traced here: 85.7 us
  waiting for transfers between devices  25 us (29%)
  blocking collectives  24.6 us (29%)
  starting transfers between devices  23.3 us (27%)
  Pallas kernels  11.9 us (14%)
    all_to_all x2, blocking collectives, summed(): lax.all_to_all(blocks, FINE, split_axis=0, concat_axis=0, axis_index_grou...  24.6 us
    all_to_all x1, waiting for transfers between devices, per_device(): lax.all_to_all(sent, ('y', 'xh'), split_axis=0, concat_axis=0, tiled=True)  15.9 us
    ppermute x6, starting transfers between devices, swapped(): return lax.ppermute(block, 'core', [(0, 1), (1, 0)])  9.62 us
    all_to_all x1, starting transfers between devices, per_device(): lax.all_to_all(sent, ('y', 'xh'), split_axis=0, concat_axis=0, tiled=True)  7.62 us
    ppermute x3, waiting for transfers between devices, summed(): others = [lax.ppermute(blocks[by], FINE, shifts[by]) for by in order]  6.14 us
    pallas_call x3, Pallas kernels, placed(): pl.pallas_call(functools.partial(place_kernel, origins), out_shape=(jax.S...  3.34 us
    ppermute x3, starting transfers between devices, summed(): others = [lax.ppermute(blocks[by], FINE, shifts[by]) for by in order]  3.33 us
    pallas_call x1, Pallas kernels, late_layer(): pl.pallas_call(late_kernel, out_shape=(jax.ShapeDtypeStruct((2, SIDE, SID...  3.26 us
  transfers between devices with their start and end apart: 13, of which 8 were waited for; matrix products, arithmetic and copies ran while one was open for 0% of the time, Pallas kernels for 4%

profile of v6, /device:TPU:1, one launch (start us, length us, event | category | flops | bytes accessed | tf_op | source)
XLA Modules:
  0.0 85.7 jit_solution(13085756908076608927)
XLA Ops:
  0.7 7.6 %all-to-all-start = ((bf16[8,2,4,64,128]{4,3,2,1,0:T(8,128)(2,1)}), bf16[8,2,4,64,128]{4,3,2,1,0:T(8,128)(2,1)S(1)}, u32[]{:S(2)}, u32[]{:S(2)}) async-start(bf16[8,2,4,64,128]{4,3,2,1,0:T(8,128)(2,1)} %bitcast.19), calls=%async_computation | async-start | bytes 2097152 | tf_op jit(solution)/shard_map/all_to_all | solution.py:430
  8.3 0.0 copy-start
  8.3 15.9 %all-to-all-done.received = bf16[8,2,4,64,128]{4,3,2,1,0:T(8,128)(2,1)S(1)} async-done(((bf16[8,2,4,64,128]{4,3,2,1,0:T(8,128)(2,1)}), bf16[8,2,4,64,128]{4,3,2,1,0:T(8,128)(2,1)S(1)}, u32[]{:S(2)}, u32[]{:S(2)}) %all-to-all-start) | async-done | bytes 1048608 | tf_op jit(solution)/shard_map/all_to_all | solution.py:430
  24.3 1.5 %shard_map.67 = (bf16[10,10,16,384]{3,2,1,0:T(8,128)(2,1)S(1)}, bf16[4,9,9,16,256]{4,3,2,1,0:T(8,128)(2,1)S(1)}, f32[1024,128]{1,0:T(8,128)S(1)}) custom-call(bf16[8,2,4,64,128]{4,3,2,1,0:T(8,128)(2,1)S(1)} %all-to-all-done.received, bf16[16,256,128]{2,1,0:T(8,128)(2,1)S(1)} %bitcast.16), custom_call_target="tpu_custom_call" | custom-call | flops 1073741824 | bytes 8388608 | tf_op jit(solution)/shard_map/pallas_call | solution.py:229
  25.8 3.3 %shard_map.68 = (bf16[2,8,64,128]{3,2,1,0:T(8,128)(2,1)}, bf16[1728,128]{1,0:T(8,128)(2,1)S(1)}, bf16[1728,128]{1,0:T(8,128)(2,1)S(1)}, bf16[10,10,16,384]{3,2,1,0:T(8,128)(2,1)S(1)}) custom-call(s32[1]{0:T(128)} %bitcast.core, bf16[10,10,16,384]{3,2,1,0:T(8,128)(2,1)S(1)} %get-tuple-element.29.hidden, bf16[9,384,128]{2,1,0:T(8,128)(2,1)S(1)} %bitcast.13, ...), custom_call_target="tpu_custom_call" | custom-call | flops 1811939328 | bytes 8388608 | tf_op jit(solution)/shard_map/pallas_call | solution.py:245
  29.0 2.2 %collective-permute-start = (bf16[1728,128]{1,0:T(8,128)(2,1)S(1)}, bf16[1728,128]{1,0:T(8,128)(2,1)S(1)}, u32[]{:S(2)}, u32[]{:S(2)}) collective-permute-start(bf16[1728,128]{1,0:T(8,128)(2,1)S(1)} %get-tuple-element.37), channel_id=1, source_target_pairs={{0,8},{8,0},{1,9},{9,1},{2,10},{10,2},{3,11},{11,3},{4,12},{12,4},... | collective-permute-start | bytes 1327112 | tf_op jit(solution)/shard_map/ppermute | solution.py:361
  31.3 1.7 %shard_map.69 = (bf16[10,10,16,128]{3,2,1,0:T(8,128)(2,1)S(1)}, bf16[4,256,1024]{2,1,0:T(8,128)(2,1)S(1)}) custom-call(bf16[9,384,128]{2,1,0:T(8,128)(2,1)S(1)} %bitcast.14, bf16[4,9,9,16,256]{4,3,2,1,0:T(8,128)(2,1)S(1)} %get-tuple-element.31.volume, bf16[10,10,16,384]{3,2,1,0:T(8,128)(2,1)S(1)} %get-tuple-element.32.error, ...), custom_call_target="tpu_custom_call" | custom-call | flops 905969664 | bytes 8388608 | tf_op jit(solution)/shard_map/pallas_call | solution.py:266
  33.0 1.7 %shard_map.70 = (bf16[2048,128]{1,0:T(8,128)(2,1)S(1)}, bf16[2048,128]{1,0:T(8,128)(2,1)S(1)}, bf16[1728,128]{1,0:T(8,128)(2,1)S(1)}) custom-call(s32[1]{0:T(128)} %bitcast.core, bf16[10,10,16,128]{3,2,1,0:T(8,128)(2,1)S(1)} %get-tuple-element.34.error_early, bf16[4,256,1024]{2,1,0:T(8,128)(2,1)S(1)} %get-tuple-element.35.volume_t, ...), custom_call_target="tpu_custom_call" | custom-call | flops 1073741824 | bytes 8388608 | tf_op jit(solution)/shard_map/pallas_call | solution.py:281
  34.7 0.2 collective-permute-start.1
  34.9 1.8 %collective-permute-done.1.early_other = bf16[2048,128]{1,0:T(8,128)(2,1)S(1)} collective-permute-done((bf16[2048,128]{1,0:T(8,128)(2,1)S(1)}, bf16[2048,128]{1,0:T(8,128)(2,1)S(1)}, u32[]{:S(2)}, u32[]{:S(2)}) %collective-permute-start.1) | collective-permute-done | bytes 524320 | tf_op jit(solution)/shard_map/ppermute | solution.py:361
  36.7 0.1 shard_map.71
  36.8 0.7 collective-permute-start.2
  37.5 0.6 collective-permute-start.3
  38.1 2.1 %collective-permute-start.4 = (bf16[944,128]{1,0:T(8,128)(2,1)S(1)}, bf16[944,128]{1,0:T(8,128)(2,1)S(1)}, u32[]{:S(2)}, u32[]{:S(2)}) collective-permute-start(bf16[944,128]{1,0:T(8,128)(2,1)S(1)} %get-tuple-element.44), channel_id=1, source_target_pairs={{0,48},{1,49},{2,50},{3,51},{4,52},{5,53},{6,54},{7,55},{8,14},{9,... | collective-permute-start | bytes 725000 | tf_op jit(solution)/shard_map/ppermute | solution.py:371
  40.2 3.6 %collective-permute-done.2.second = bf16[944,128]{1,0:T(8,128)(2,1)S(1)} collective-permute-done((bf16[944,128]{1,0:T(8,128)(2,1)S(1)}, bf16[944,128]{1,0:T(8,128)(2,1)S(1)}, u32[]{:S(2)}, u32[]{:S(2)}) %collective-permute-start.2) | collective-permute-done | bytes 241696 | tf_op jit(solution)/shard_map/ppermute | solution.py:371
  43.7 2.5 %collective-permute-done.3.third = bf16[944,128]{1,0:T(8,128)(2,1)S(1)} collective-permute-done((bf16[944,128]{1,0:T(8,128)(2,1)S(1)}, bf16[944,128]{1,0:T(8,128)(2,1)S(1)}, u32[]{:S(2)}, u32[]{:S(2)}) %collective-permute-start.3) | collective-permute-done | bytes 241696 | tf_op jit(solution)/shard_map/ppermute | solution.py:371
  46.3 0.2 shard_map.72
  46.5 13.4 %all_to_all.15.shares = bf16[16,64,128]{2,1,0:T(8,128)(2,1)S(1)} all-to-all(bf16[16,64,128]{2,1,0:T(8,128)(2,1)S(1)} %shard_map.72), channel_id=1, replica_groups={{0,1,2,3,4,5,6,7,64,65,66,67,68,69,70,71},{16,17,18,19,20,21,22,23,80,8..., dimensions={0} | all-to-all | bytes 524288 | tf_op jit(solution)/shard_map/all_to_all | solution.py:366
  60.0 11.2 %all_to_all.16.shares = bf16[16,64,128]{2,1,0:T(8,128)(2,1)S(1)} all-to-all(bf16[16,64,128]{2,1,0:T(8,128)(2,1)S(1)} %shard_map.73), channel_id=1, replica_groups={{0,1,2,3,4,5,6,7,64,65,66,67,68,69,70,71},{16,17,18,19,20,21,22,23,80,8..., dimensions={0} | all-to-all | bytes 524288 | tf_op jit(solution)/shard_map/all_to_all | solution.py:366
  71.2 0.1 collective-permute-start.10
  71.3 4.0 %collective-permute-start.5 = (bf16[944,128]{1,0:T(8,128)(2,1)S(1)}, bf16[944,128]{1,0:T(8,128)(2,1)S(1)}, u32[]{:S(2)}, u32[]{:S(2)}) collective-permute-start(bf16[944,128]{1,0:T(8,128)(2,1)S(1)} %shard_map.74.refs_0_), channel_id=1, source_target_pairs={{0,8},{8,0},{1,9},{9,1},{2,10},{10,2},{3,11},{11,3},{4,12},{12,4},... | collective-permute-start | bytes 725000 | tf_op jit(solution)/shard_map/ppermute | solution.py:361
  75.3 0.1 collective-permute-start.7
  75.4 2.6 %collective-permute-start.6 = (bf16[944,128]{1,0:T(8,128)(2,1)S(1)}, bf16[944,128]{1,0:T(8,128)(2,1)S(1)}, u32[]{:S(2)}, u32[]{:S(2)}) collective-permute-start(bf16[944,128]{1,0:T(8,128)(2,1)S(1)} %shard_map.74.refs_0_), channel_id=1, source_target_pairs={{0,48},{1,49},{2,50},{3,51},{4,52},{5,53},{6,54},{7,55},{8,14},{9,... | collective-permute-start | bytes 725000 | tf_op jit(solution)/shard_map/ppermute | solution.py:378
  78.0 0.1 collective-permute-done.10.refs_0_
  78.1 2.2 %collective-permute-start.11 = (bf16[944,128]{1,0:T(8,128)(2,1)S(1)}, bf16[944,128]{1,0:T(8,128)(2,1)S(1)}, u32[]{:S(2)}, u32[]{:S(2)}) collective-permute-start(bf16[944,128]{1,0:T(8,128)(2,1)S(1)} %collective-permute-done.10.refs_0_), channel_id=1, source_target_pairs={{0,8},{8,0},{1,9},{9,1},{2,10},{10,2},{3,11},{11,3},{4,12},{12,4},... | collective-permute-start | bytes 725000 | tf_op jit(solution)/shard_map/ppermute | solution.py:361
  80.3 1.0 %shard_map.75 = (f32[4096,128]{1,0:T(8,128)}, f32[3456,128]{1,0:T(8,128)}) custom-call(s32[1]{0:T(128)} %bitcast.core, s32[1]{0:T(128)} %bitcast.8.place, s32[1]{0:T(128)} %bitcast.9.other_place, bf16[944,128]{1,0:T(8,128)(2,1)S(1)} %shard_map.74.refs_0_, bf16[944,128]{1,0:T(8,128)(2,1)S(1)} %collective-permute-done.5.refs_1_), custom_call_target="tpu_custom_call" | custom-call | bytes 1572864 | tf_op jit(solution)/shard_map/pallas_call | solution.py:408
  81.3 0.5 collective-permute-done.7.refs_0_
  81.8 1.1 %collective-permute-start.8 = (bf16[944,128]{1,0:T(8,128)(2,1)S(1)}, bf16[944,128]{1,0:T(8,128)(2,1)S(1)}, u32[]{:S(2)}, u32[]{:S(2)}) collective-permute-start(bf16[944,128]{1,0:T(8,128)(2,1)S(1)} %collective-permute-done.7.refs_0_), channel_id=1, source_target_pairs={{0,8},{8,0},{1,9},{9,1},{2,10},{10,2},{3,11},{11,3},{4,12},{12,4},... | collective-permute-start | bytes 725000 | tf_op jit(solution)/shard_map/ppermute | solution.py:361
  82.9 1.0 %shard_map.76 = (f32[4096,128]{1,0:T(8,128)}, f32[3456,128]{1,0:T(8,128)}) custom-call(s32[1]{0:T(128)} %bitcast.core, s32[1]{0:T(128)} %bitcast.8.place, s32[1]{0:T(128)} %bitcast.9.other_place, bf16[944,128]{1,0:T(8,128)(2,1)S(1)} %collective-permute-done.10.refs_0_, ...), custom_call_target="tpu_custom_call", output_to_operand_aliasing={{0}: (5, {}), {1}: (6, {})} | custom-call | bytes 1572864 | tf_op jit(solution)/shard_map/pallas_call | solution.py:408
  83.9 0.1 collective-permute-done.8.refs_2_
  84.0 0.4 collective-permute-done.9.refs_3_
  84.4 1.3 %shard_map.77 = (f32[4096,128]{1,0:T(8,128)}, f32[3456,128]{1,0:T(8,128)}) custom-call(s32[1]{0:T(128)} %bitcast.core, s32[1]{0:T(128)} %bitcast.8.place, s32[1]{0:T(128)} %bitcast.9.other_place, bf16[944,128]{1,0:T(8,128)(2,1)S(1)} %collective-permute-done.7.refs_0_, ...), custom_call_target="tpu_custom_call", output_to_operand_aliasing={{0}: (7, {}), {1}: (8, {})} | custom-call | bytes 3145728 | tf_op jit(solution)/shard_map/pallas_call | solution.py:408
  (14 shorter events, 0.2 us)
Async XLA Ops:
  0.6 7.6 %copy-start.2 = (bf16[2,8,8,8,128]{4,3,2,1,0:T(8,128)(2,1)S(1)}, bf16[2,8,8,8,128]{4,3,2,1,0:T(8,128)(2,1)}, u32[]{:S(2)}) copy-start(bf16[2,8,8,8,128]{4,3,2,1,0:T(8,128)(2,1)} %param.7) | copy-start | bytes 786436
  0.6 23.6 %copy-start.1 = (bf16[4,4,4,64,128]{4,3,2,1,0:T(8,128)(2,1)S(1)}, bf16[4,4,4,64,128]{4,3,2,1,0:T(8,128)(2,1)}, u32[]{:S(2)}) copy-start(bf16[4,4,4,64,128]{4,3,2,1,0:T(8,128)(2,1)} %param.5) | copy-start | bytes 3145732
  0.7 23.6 %all-to-all-start = ((bf16[8,2,4,64,128]{4,3,2,1,0:T(8,128)(2,1)}), bf16[8,2,4,64,128]{4,3,2,1,0:T(8,128)(2,1)S(1)}, u32[]{:S(2)}, u32[]{:S(2)}) async-start(bf16[8,2,4,64,128]{4,3,2,1,0:T(8,128)(2,1)} %bitcast.19), calls=%async_computation | async-start | bytes 2097152 | tf_op jit(solution)/shard_map/all_to_all | solution.py:430
  8.3 17.4 %copy-start = (bf16[3,3,3,128,128]{4,3,2,1,0:T(8,128)(2,1)S(1)}, bf16[3,3,3,128,128]{4,3,2,1,0:T(8,128)(2,1)}, u32[]{:S(2)}) copy-start(bf16[3,3,3,128,128]{4,3,2,1,0:T(8,128)(2,1)} %param.6) | copy-start | bytes 2654212
  29.0 3.9 %collective-permute-start = (bf16[1728,128]{1,0:T(8,128)(2,1)S(1)}, bf16[1728,128]{1,0:T(8,128)(2,1)S(1)}, u32[]{:S(2)}, u32[]{:S(2)}) collective-permute-start(bf16[1728,128]{1,0:T(8,128)(2,1)S(1)} %get-tuple-element.37), channel_id=1, source_target_pairs={{0,8},{8,0},{1,9},{9,1},{2,10},{10,2},{3,11},{11,3},{4,12},{12,4},... | collective-permute-start | bytes 1327112 | tf_op jit(solution)/shard_map/ppermute | solution.py:361
  34.7 2.0 %collective-permute-start.1 = (bf16[2048,128]{1,0:T(8,128)(2,1)S(1)}, bf16[2048,128]{1,0:T(8,128)(2,1)S(1)}, u32[]{:S(2)}, u32[]{:S(2)}) collective-permute-start(bf16[2048,128]{1,0:T(8,128)(2,1)S(1)} %get-tuple-element.39), channel_id=1, source_target_pairs={{0,8},{8,0},{1,9},{9,1},{2,10},{10,2},{3,11},{11,3},{4,12},{12,4},... | collective-permute-start | bytes 1572872 | tf_op jit(solution)/shard_map/ppermute | solution.py:361
  36.8 6.9 %collective-permute-start.2 = (bf16[944,128]{1,0:T(8,128)(2,1)S(1)}, bf16[944,128]{1,0:T(8,128)(2,1)S(1)}, u32[]{:S(2)}, u32[]{:S(2)}) collective-permute-start(bf16[944,128]{1,0:T(8,128)(2,1)S(1)} %get-tuple-element.42), channel_id=1, source_target_pairs={{0,32},{1,33},{2,34},{3,35},{4,36},{5,37},{6,38},{7,39},{8,12},{9,... | collective-permute-start | bytes 725000 | tf_op jit(solution)/shard_map/ppermute | solution.py:371
  37.5 8.8 %collective-permute-start.3 = (bf16[944,128]{1,0:T(8,128)(2,1)S(1)}, bf16[944,128]{1,0:T(8,128)(2,1)S(1)}, u32[]{:S(2)}, u32[]{:S(2)}) collective-permute-start(bf16[944,128]{1,0:T(8,128)(2,1)S(1)} %get-tuple-element.43), channel_id=1, source_target_pairs={{0,16},{1,17},{2,18},{3,19},{4,20},{5,21},{6,22},{7,23},{8,10},{9,... | collective-permute-start | bytes 725000 | tf_op jit(solution)/shard_map/ppermute | solution.py:371
  38.1 8.2 %collective-permute-start.4 = (bf16[944,128]{1,0:T(8,128)(2,1)S(1)}, bf16[944,128]{1,0:T(8,128)(2,1)S(1)}, u32[]{:S(2)}, u32[]{:S(2)}) collective-permute-start(bf16[944,128]{1,0:T(8,128)(2,1)S(1)} %get-tuple-element.44), channel_id=1, source_target_pairs={{0,48},{1,49},{2,50},{3,51},{4,52},{5,53},{6,54},{7,55},{8,14},{9,... | collective-permute-start | bytes 725000 | tf_op jit(solution)/shard_map/ppermute | solution.py:371
  71.2 6.9 %collective-permute-start.10 = (bf16[944,128]{1,0:T(8,128)(2,1)S(1)}, bf16[944,128]{1,0:T(8,128)(2,1)S(1)}, u32[]{:S(2)}, u32[]{:S(2)}) collective-permute-start(bf16[944,128]{1,0:T(8,128)(2,1)S(1)} %shard_map.74.refs_0_), channel_id=1, source_target_pairs={{0,32},{1,33},{2,34},{3,35},{4,36},{5,37},{6,38},{7,39},{8,12},{9,... | collective-permute-start | bytes 725000 | tf_op jit(solution)/shard_map/ppermute | solution.py:378
  71.3 9.0 %collective-permute-start.5 = (bf16[944,128]{1,0:T(8,128)(2,1)S(1)}, bf16[944,128]{1,0:T(8,128)(2,1)S(1)}, u32[]{:S(2)}, u32[]{:S(2)}) collective-permute-start(bf16[944,128]{1,0:T(8,128)(2,1)S(1)} %shard_map.74.refs_0_), channel_id=1, source_target_pairs={{0,8},{8,0},{1,9},{9,1},{2,10},{10,2},{3,11},{11,3},{4,12},{12,4},... | collective-permute-start | bytes 725000 | tf_op jit(solution)/shard_map/ppermute | solution.py:361
  75.3 6.5 %collective-permute-start.7 = (bf16[944,128]{1,0:T(8,128)(2,1)S(1)}, bf16[944,128]{1,0:T(8,128)(2,1)S(1)}, u32[]{:S(2)}, u32[]{:S(2)}) collective-permute-start(bf16[944,128]{1,0:T(8,128)(2,1)S(1)} %shard_map.74.refs_0_), channel_id=1, source_target_pairs={{0,16},{1,17},{2,18},{3,19},{4,20},{5,21},{6,22},{7,23},{8,10},{9,... | collective-permute-start | bytes 725000 | tf_op jit(solution)/shard_map/ppermute | solution.py:378
  75.4 6.4 %collective-permute-start.6 = (bf16[944,128]{1,0:T(8,128)(2,1)S(1)}, bf16[944,128]{1,0:T(8,128)(2,1)S(1)}, u32[]{:S(2)}, u32[]{:S(2)}) collective-permute-start(bf16[944,128]{1,0:T(8,128)(2,1)S(1)} %shard_map.74.refs_0_), channel_id=1, source_target_pairs={{0,48},{1,49},{2,50},{3,51},{4,52},{5,53},{6,54},{7,55},{8,14},{9,... | collective-permute-start | bytes 725000 | tf_op jit(solution)/shard_map/ppermute | solution.py:378
  78.1 4.8 %collective-permute-start.11 = (bf16[944,128]{1,0:T(8,128)(2,1)S(1)}, bf16[944,128]{1,0:T(8,128)(2,1)S(1)}, u32[]{:S(2)}, u32[]{:S(2)}) collective-permute-start(bf16[944,128]{1,0:T(8,128)(2,1)S(1)} %collective-permute-done.10.refs_0_), channel_id=1, source_target_pairs={{0,8},{8,0},{1,9},{9,1},{2,10},{10,2},{3,11},{11,3},{4,12},{12,4},... | collective-permute-start | bytes 725000 | tf_op jit(solution)/shard_map/ppermute | solution.py:361
  81.8 2.2 %collective-permute-start.8 = (bf16[944,128]{1,0:T(8,128)(2,1)S(1)}, bf16[944,128]{1,0:T(8,128)(2,1)S(1)}, u32[]{:S(2)}, u32[]{:S(2)}) collective-permute-start(bf16[944,128]{1,0:T(8,128)(2,1)S(1)} %collective-permute-done.7.refs_0_), channel_id=1, source_target_pairs={{0,8},{8,0},{1,9},{9,1},{2,10},{10,2},{3,11},{11,3},{4,12},{12,4},... | collective-permute-start | bytes 725000 | tf_op jit(solution)/shard_map/ppermute | solution.py:361
  82.9 1.5 %collective-permute-start.9 = (bf16[944,128]{1,0:T(8,128)(2,1)S(1)}, bf16[944,128]{1,0:T(8,128)(2,1)S(1)}, u32[]{:S(2)}, u32[]{:S(2)}) collective-permute-start(bf16[944,128]{1,0:T(8,128)(2,1)S(1)} %collective-permute-done.6.refs_1_), channel_id=1, source_target_pairs={{0,8},{8,0},{1,9},{9,1},{2,10},{10,2},{3,11},{11,3},{4,12},{12,4},... | collective-permute-start | bytes 725000 | tf_op jit(solution)/shard_map/ppermute | solution.py:361

commit v7 on v6

--- a/solution.py
+++ b/solution.py
@@ -439,10 +439,11 @@
     scalars = [value.reshape(1) for value in (core, ring_place(core), ring_place(1 - core))]
     totals = placed(scalars, ((0, 0), (0, 1)), [zero, swapped(zero)], ())
     *totals, three, one = lax.optimization_barrier((*totals, three, one))
-    totals = placed(scalars, ((2, 0), (2, 1)), [two, swapped(two)], totals)
-    early_total, late_total = placed(
-        scalars, ((1, 0), (3, 0), (1, 1), (3, 1)), [one, three, swapped(one), swapped(three)], totals
+    swaps = [swapped(one), swapped(three)]
+    totals = placed(
+        scalars, ((2, 0), (1, 0), (3, 0), (2, 1)), [two, one, three, swapped(two)], totals
     )
+    early_total, late_total = placed(scalars, ((1, 1), (3, 1)), swaps, totals)
     return (
         activated.reshape(cotangent.shape),
         early_total.reshape(conv_early.shape),

time: 86 us -> 85.6 us (level)
  transfers between devices with their start and end apart: 13 -> 13, of which waited for: 8 -> 7; matrix products, arithmetic and copies ran while one was open for 0% -> 0% of each run, Pallas kernels for 4% -> 5%
where the time goes in v7:
time: 85.6 us; the launch traced here: 85.4 us
  waiting for transfers between devices  24.7 us (29%)
  blocking collectives  24.6 us (29%)
  starting transfers between devices  23.3 us (27%)
  Pallas kernels  11.9 us (14%)
    all_to_all x2, blocking collectives, summed(): lax.all_to_all(blocks, FINE, split_axis=0, concat_axis=0, axis_index_grou...  24.6 us
    all_to_all x1, waiting for transfers between devices, per_device(): lax.all_to_all(sent, ('y', 'xh'), split_axis=0, concat_axis=0, tiled=True)  15.9 us
    ppermute x6, starting transfers between devices, swapped(): return lax.ppermute(block, 'core', [(0, 1), (1, 0)])  9.62 us
    all_to_all x1, starting transfers between devices, per_device(): lax.all_to_all(sent, ('y', 'xh'), split_axis=0, concat_axis=0, tiled=True)  7.62 us
    ppermute x3, waiting for transfers between devices, summed(): others = [lax.ppermute(blocks[by], FINE, shifts[by]) for by in order]  6.14 us
    pallas_call x3, Pallas kernels, placed(): pl.pallas_call(functools.partial(place_kernel, origins), out_shape=(jax.S...  3.34 us
    ppermute x3, starting transfers between devices, summed(): others = [lax.ppermute(blocks[by], FINE, shifts[by]) for by in order]  3.33 us
    pallas_call x1, Pallas kernels, late_layer(): pl.pallas_call(late_kernel, out_shape=(jax.ShapeDtypeStruct((2, SIDE, SID...  3.26 us
  transfers between devices with their start and end apart: 13, of which 7 were waited for; matrix products, arithmetic and copies ran while one was open for 0% of the time, Pallas kernels for 5%

profile of v7, /device:TPU:1, one launch (start us, length us, event | category | flops | bytes accessed | tf_op | source)
XLA Modules:
  0.0 85.4 jit_solution(10815744870246466736)
XLA Ops:
  0.7 7.6 %all-to-all-start = ((bf16[8,2,4,64,128]{4,3,2,1,0:T(8,128)(2,1)}), bf16[8,2,4,64,128]{4,3,2,1,0:T(8,128)(2,1)S(1)}, u32[]{:S(2)}, u32[]{:S(2)}) async-start(bf16[8,2,4,64,128]{4,3,2,1,0:T(8,128)(2,1)} %bitcast.19), calls=%async_computation | async-start | bytes 2097152 | tf_op jit(solution)/shard_map/all_to_all | solution.py:430
  8.3 0.0 copy-start
  8.3 15.9 %all-to-all-done.received = bf16[8,2,4,64,128]{4,3,2,1,0:T(8,128)(2,1)S(1)} async-done(((bf16[8,2,4,64,128]{4,3,2,1,0:T(8,128)(2,1)}), bf16[8,2,4,64,128]{4,3,2,1,0:T(8,128)(2,1)S(1)}, u32[]{:S(2)}, u32[]{:S(2)}) %all-to-all-start) | async-done | bytes 1048608 | tf_op jit(solution)/shard_map/all_to_all | solution.py:430
  24.3 1.5 %shard_map.67 = (bf16[10,10,16,384]{3,2,1,0:T(8,128)(2,1)S(1)}, bf16[4,9,9,16,256]{4,3,2,1,0:T(8,128)(2,1)S(1)}, f32[1024,128]{1,0:T(8,128)S(1)}) custom-call(bf16[8,2,4,64,128]{4,3,2,1,0:T(8,128)(2,1)S(1)} %all-to-all-done.received, bf16[16,256,128]{2,1,0:T(8,128)(2,1)S(1)} %bitcast.16), custom_call_target="tpu_custom_call" | custom-call | flops 1073741824 | bytes 8388608 | tf_op jit(solution)/shard_map/pallas_call | solution.py:229
  25.8 3.3 %shard_map.68 = (bf16[2,8,64,128]{3,2,1,0:T(8,128)(2,1)}, bf16[1728,128]{1,0:T(8,128)(2,1)S(1)}, bf16[1728,128]{1,0:T(8,128)(2,1)S(1)}, bf16[10,10,16,384]{3,2,1,0:T(8,128)(2,1)S(1)}) custom-call(s32[1]{0:T(128)} %bitcast.core, bf16[10,10,16,384]{3,2,1,0:T(8,128)(2,1)S(1)} %get-tuple-element.29.hidden, bf16[9,384,128]{2,1,0:T(8,128)(2,1)S(1)} %bitcast.13, ...), custom_call_target="tpu_custom_call" | custom-call | flops 1811939328 | bytes 8388608 | tf_op jit(solution)/shard_map/pallas_call | solution.py:245
  29.0 2.2 %collective-permute-start = (bf16[1728,128]{1,0:T(8,128)(2,1)S(1)}, bf16[1728,128]{1,0:T(8,128)(2,1)S(1)}, u32[]{:S(2)}, u32[]{:S(2)}) collective-permute-start(bf16[1728,128]{1,0:T(8,128)(2,1)S(1)} %get-tuple-element.37), channel_id=1, source_target_pairs={{0,8},{8,0},{1,9},{9,1},{2,10},{10,2},{3,11},{11,3},{4,12},{12,4},... | collective-permute-start | bytes 1327112 | tf_op jit(solution)/shard_map/ppermute | solution.py:361
  31.3 1.7 %shard_map.69 = (bf16[10,10,16,128]{3,2,1,0:T(8,128)(2,1)S(1)}, bf16[4,256,1024]{2,1,0:T(8,128)(2,1)S(1)}) custom-call(bf16[9,384,128]{2,1,0:T(8,128)(2,1)S(1)} %bitcast.14, bf16[4,9,9,16,256]{4,3,2,1,0:T(8,128)(2,1)S(1)} %get-tuple-element.31.volume, bf16[10,10,16,384]{3,2,1,0:T(8,128)(2,1)S(1)} %get-tuple-element.32.error, ...), custom_call_target="tpu_custom_call" | custom-call | flops 905969664 | bytes 8388608 | tf_op jit(solution)/shard_map/pallas_call | solution.py:266
  33.0 1.7 %shard_map.70 = (bf16[2048,128]{1,0:T(8,128)(2,1)S(1)}, bf16[2048,128]{1,0:T(8,128)(2,1)S(1)}, bf16[1728,128]{1,0:T(8,128)(2,1)S(1)}) custom-call(s32[1]{0:T(128)} %bitcast.core, bf16[10,10,16,128]{3,2,1,0:T(8,128)(2,1)S(1)} %get-tuple-element.34.error_early, bf16[4,256,1024]{2,1,0:T(8,128)(2,1)S(1)} %get-tuple-element.35.volume_t, ...), custom_call_target="tpu_custom_call" | custom-call | flops 1073741824 | bytes 8388608 | tf_op jit(solution)/shard_map/pallas_call | solution.py:281
  34.7 0.2 collective-permute-start.1
  34.9 1.8 %collective-permute-done.1.early_other = bf16[2048,128]{1,0:T(8,128)(2,1)S(1)} collective-permute-done((bf16[2048,128]{1,0:T(8,128)(2,1)S(1)}, bf16[2048,128]{1,0:T(8,128)(2,1)S(1)}, u32[]{:S(2)}, u32[]{:S(2)}) %collective-permute-start.1) | collective-permute-done | bytes 524320 | tf_op jit(solution)/shard_map/ppermute | solution.py:361
  36.7 0.1 shard_map.71
  36.8 0.7 collective-permute-start.2
  37.5 0.6 collective-permute-start.3
  38.1 2.1 %collective-permute-start.4 = (bf16[944,128]{1,0:T(8,128)(2,1)S(1)}, bf16[944,128]{1,0:T(8,128)(2,1)S(1)}, u32[]{:S(2)}, u32[]{:S(2)}) collective-permute-start(bf16[944,128]{1,0:T(8,128)(2,1)S(1)} %get-tuple-element.44), channel_id=1, source_target_pairs={{0,48},{1,49},{2,50},{3,51},{4,52},{5,53},{6,54},{7,55},{8,14},{9,... | collective-permute-start | bytes 725000 | tf_op jit(solution)/shard_map/ppermute | solution.py:371
  40.2 3.6 %collective-permute-done.2.second = bf16[944,128]{1,0:T(8,128)(2,1)S(1)} collective-permute-done((bf16[944,128]{1,0:T(8,128)(2,1)S(1)}, bf16[944,128]{1,0:T(8,128)(2,1)S(1)}, u32[]{:S(2)}, u32[]{:S(2)}) %collective-permute-start.2) | collective-permute-done | bytes 241696 | tf_op jit(solution)/shard_map/ppermute | solution.py:371
  43.7 2.5 %collective-permute-done.3.third = bf16[944,128]{1,0:T(8,128)(2,1)S(1)} collective-permute-done((bf16[944,128]{1,0:T(8,128)(2,1)S(1)}, bf16[944,128]{1,0:T(8,128)(2,1)S(1)}, u32[]{:S(2)}, u32[]{:S(2)}) %collective-permute-start.3) | collective-permute-done | bytes 241696 | tf_op jit(solution)/shard_map/ppermute | solution.py:371
  46.3 0.2 shard_map.72
  46.5 13.4 %all_to_all.15.shares = bf16[16,64,128]{2,1,0:T(8,128)(2,1)S(1)} all-to-all(bf16[16,64,128]{2,1,0:T(8,128)(2,1)S(1)} %shard_map.72), channel_id=1, replica_groups={{0,1,2,3,4,5,6,7,64,65,66,67,68,69,70,71},{16,17,18,19,20,21,22,23,80,8..., dimensions={0} | all-to-all | bytes 524288 | tf_op jit(solution)/shard_map/all_to_all | solution.py:366
  60.0 11.2 %all_to_all.16.shares = bf16[16,64,128]{2,1,0:T(8,128)(2,1)S(1)} all-to-all(bf16[16,64,128]{2,1,0:T(8,128)(2,1)S(1)} %shard_map.73), channel_id=1, replica_groups={{0,1,2,3,4,5,6,7,64,65,66,67,68,69,70,71},{16,17,18,19,20,21,22,23,80,8..., dimensions={0} | all-to-all | bytes 524288 | tf_op jit(solution)/shard_map/all_to_all | solution.py:366
  71.2 0.1 collective-permute-start.10
  71.3 4.0 %collective-permute-start.5 = (bf16[944,128]{1,0:T(8,128)(2,1)S(1)}, bf16[944,128]{1,0:T(8,128)(2,1)S(1)}, u32[]{:S(2)}, u32[]{:S(2)}) collective-permute-start(bf16[944,128]{1,0:T(8,128)(2,1)S(1)} %shard_map.74.refs_0_), channel_id=1, source_target_pairs={{0,8},{8,0},{1,9},{9,1},{2,10},{10,2},{3,11},{11,3},{4,12},{12,4},... | collective-permute-start | bytes 725000 | tf_op jit(solution)/shard_map/ppermute | solution.py:361
  75.3 0.1 collective-permute-start.7
  75.4 2.6 %collective-permute-start.6 = (bf16[944,128]{1,0:T(8,128)(2,1)S(1)}, bf16[944,128]{1,0:T(8,128)(2,1)S(1)}, u32[]{:S(2)}, u32[]{:S(2)}) collective-permute-start(bf16[944,128]{1,0:T(8,128)(2,1)S(1)} %shard_map.74.refs_0_), channel_id=1, source_target_pairs={{0,48},{1,49},{2,50},{3,51},{4,52},{5,53},{6,54},{7,55},{8,14},{9,... | collective-permute-start | bytes 725000 | tf_op jit(solution)/shard_map/ppermute | solution.py:378
  78.0 0.1 collective-permute-done.10.refs_0_
  78.1 2.2 %collective-permute-start.11 = (bf16[944,128]{1,0:T(8,128)(2,1)S(1)}, bf16[944,128]{1,0:T(8,128)(2,1)S(1)}, u32[]{:S(2)}, u32[]{:S(2)}) collective-permute-start(bf16[944,128]{1,0:T(8,128)(2,1)S(1)} %collective-permute-done.10.refs_0_), channel_id=1, source_target_pairs={{0,8},{8,0},{1,9},{9,1},{2,10},{10,2},{3,11},{11,3},{4,12},{12,4},... | collective-permute-start | bytes 725000 | tf_op jit(solution)/shard_map/ppermute | solution.py:361
  80.3 1.0 %shard_map.75 = (f32[4096,128]{1,0:T(8,128)}, f32[3456,128]{1,0:T(8,128)}) custom-call(s32[1]{0:T(128)} %bitcast.core, s32[1]{0:T(128)} %bitcast.8.place, s32[1]{0:T(128)} %bitcast.9.other_place, bf16[944,128]{1,0:T(8,128)(2,1)S(1)} %shard_map.74.refs_0_, bf16[944,128]{1,0:T(8,128)(2,1)S(1)} %collective-permute-done.5.refs_1_), custom_call_target="tpu_custom_call" | custom-call | bytes 1572864 | tf_op jit(solution)/shard_map/pallas_call | solution.py:408
  81.3 0.5 collective-permute-done.7.refs_1_
  81.8 1.1 %collective-permute-start.8 = (bf16[944,128]{1,0:T(8,128)(2,1)S(1)}, bf16[944,128]{1,0:T(8,128)(2,1)S(1)}, u32[]{:S(2)}, u32[]{:S(2)}) collective-permute-start(bf16[944,128]{1,0:T(8,128)(2,1)S(1)} %collective-permute-done.7.refs_1_), channel_id=1, source_target_pairs={{0,8},{8,0},{1,9},{9,1},{2,10},{10,2},{3,11},{11,3},{4,12},{12,4},... | collective-permute-start | bytes 725000 | tf_op jit(solution)/shard_map/ppermute | solution.py:361
  82.9 0.0 collective-permute-start.9
  82.9 1.3 %shard_map.76 = (f32[4096,128]{1,0:T(8,128)}, f32[3456,128]{1,0:T(8,128)}) custom-call(s32[1]{0:T(128)} %bitcast.core, s32[1]{0:T(128)} %bitcast.8.place, s32[1]{0:T(128)} %bitcast.9.other_place, bf16[944,128]{1,0:T(8,128)(2,1)S(1)} %collective-permute-done.10.refs_0_, ...), custom_call_target="tpu_custom_call", output_to_operand_aliasing={{0}: (7, {}), {1}: (8, {})} | custom-call | bytes 3145728 | tf_op jit(solution)/shard_map/pallas_call | solution.py:408
  84.2 0.1 collective-permute-done.9.refs_1_
  84.4 1.0 %shard_map.77 = (f32[4096,128]{1,0:T(8,128)}, f32[3456,128]{1,0:T(8,128)}) custom-call(s32[1]{0:T(128)} %bitcast.core, s32[1]{0:T(128)} %bitcast.8.place, s32[1]{0:T(128)} %bitcast.9.other_place, bf16[944,128]{1,0:T(8,128)(2,1)S(1)} %collective-permute-done.8.refs_0_, ...), custom_call_target="tpu_custom_call", output_to_operand_aliasing={{0}: (5, {}), {1}: (6, {})} | custom-call | bytes 1572864 | tf_op jit(solution)/shard_map/pallas_call | solution.py:408
  (14 shorter events, 0.2 us)
Async XLA Ops:
  0.6 7.6 %copy-start.2 = (bf16[2,8,8,8,128]{4,3,2,1,0:T(8,128)(2,1)S(1)}, bf16[2,8,8,8,128]{4,3,2,1,0:T(8,128)(2,1)}, u32[]{:S(2)}) copy-start(bf16[2,8,8,8,128]{4,3,2,1,0:T(8,128)(2,1)} %param.7) | copy-start | bytes 786436
  0.6 23.6 %copy-start.1 = (bf16[4,4,4,64,128]{4,3,2,1,0:T(8,128)(2,1)S(1)}, bf16[4,4,4,64,128]{4,3,2,1,0:T(8,128)(2,1)}, u32[]{:S(2)}) copy-start(bf16[4,4,4,64,128]{4,3,2,1,0:T(8,128)(2,1)} %param.5) | copy-start | bytes 3145732
  0.7 23.6 %all-to-all-start = ((bf16[8,2,4,64,128]{4,3,2,1,0:T(8,128)(2,1)}), bf16[8,2,4,64,128]{4,3,2,1,0:T(8,128)(2,1)S(1)}, u32[]{:S(2)}, u32[]{:S(2)}) async-start(bf16[8,2,4,64,128]{4,3,2,1,0:T(8,128)(2,1)} %bitcast.19), calls=%async_computation | async-start | bytes 2097152 | tf_op jit(solution)/shard_map/all_to_all | solution.py:430
  8.3 17.4 %copy-start = (bf16[3,3,3,128,128]{4,3,2,1,0:T(8,128)(2,1)S(1)}, bf16[3,3,3,128,128]{4,3,2,1,0:T(8,128)(2,1)}, u32[]{:S(2)}) copy-start(bf16[3,3,3,128,128]{4,3,2,1,0:T(8,128)(2,1)} %param.6) | copy-start | bytes 2654212
  29.0 3.9 %collective-permute-start = (bf16[1728,128]{1,0:T(8,128)(2,1)S(1)}, bf16[1728,128]{1,0:T(8,128)(2,1)S(1)}, u32[]{:S(2)}, u32[]{:S(2)}) collective-permute-start(bf16[1728,128]{1,0:T(8,128)(2,1)S(1)} %get-tuple-element.37), channel_id=1, source_target_pairs={{0,8},{8,0},{1,9},{9,1},{2,10},{10,2},{3,11},{11,3},{4,12},{12,4},... | collective-permute-start | bytes 1327112 | tf_op jit(solution)/shard_map/ppermute | solution.py:361
  34.7 2.0 %collective-permute-start.1 = (bf16[2048,128]{1,0:T(8,128)(2,1)S(1)}, bf16[2048,128]{1,0:T(8,128)(2,1)S(1)}, u32[]{:S(2)}, u32[]{:S(2)}) collective-permute-start(bf16[2048,128]{1,0:T(8,128)(2,1)S(1)} %get-tuple-element.39), channel_id=1, source_target_pairs={{0,8},{8,0},{1,9},{9,1},{2,10},{10,2},{3,11},{11,3},{4,12},{12,4},... | collective-permute-start | bytes 1572872 | tf_op jit(solution)/shard_map/ppermute | solution.py:361
  36.8 6.9 %collective-permute-start.2 = (bf16[944,128]{1,0:T(8,128)(2,1)S(1)}, bf16[944,128]{1,0:T(8,128)(2,1)S(1)}, u32[]{:S(2)}, u32[]{:S(2)}) collective-permute-start(bf16[944,128]{1,0:T(8,128)(2,1)S(1)} %get-tuple-element.42), channel_id=1, source_target_pairs={{0,32},{1,33},{2,34},{3,35},{4,36},{5,37},{6,38},{7,39},{8,12},{9,... | collective-permute-start | bytes 725000 | tf_op jit(solution)/shard_map/ppermute | solution.py:371
  37.5 8.8 %collective-permute-start.3 = (bf16[944,128]{1,0:T(8,128)(2,1)S(1)}, bf16[944,128]{1,0:T(8,128)(2,1)S(1)}, u32[]{:S(2)}, u32[]{:S(2)}) collective-permute-start(bf16[944,128]{1,0:T(8,128)(2,1)S(1)} %get-tuple-element.43), channel_id=1, source_target_pairs={{0,16},{1,17},{2,18},{3,19},{4,20},{5,21},{6,22},{7,23},{8,10},{9,... | collective-permute-start | bytes 725000 | tf_op jit(solution)/shard_map/ppermute | solution.py:371
  38.1 8.2 %collective-permute-start.4 = (bf16[944,128]{1,0:T(8,128)(2,1)S(1)}, bf16[944,128]{1,0:T(8,128)(2,1)S(1)}, u32[]{:S(2)}, u32[]{:S(2)}) collective-permute-start(bf16[944,128]{1,0:T(8,128)(2,1)S(1)} %get-tuple-element.44), channel_id=1, source_target_pairs={{0,48},{1,49},{2,50},{3,51},{4,52},{5,53},{6,54},{7,55},{8,14},{9,... | collective-permute-start | bytes 725000 | tf_op jit(solution)/shard_map/ppermute | solution.py:371
  71.2 6.9 %collective-permute-start.10 = (bf16[944,128]{1,0:T(8,128)(2,1)S(1)}, bf16[944,128]{1,0:T(8,128)(2,1)S(1)}, u32[]{:S(2)}, u32[]{:S(2)}) collective-permute-start(bf16[944,128]{1,0:T(8,128)(2,1)S(1)} %shard_map.74.refs_0_), channel_id=1, source_target_pairs={{0,32},{1,33},{2,34},{3,35},{4,36},{5,37},{6,38},{7,39},{8,12},{9,... | collective-permute-start | bytes 725000 | tf_op jit(solution)/shard_map/ppermute | solution.py:378
  71.3 9.0 %collective-permute-start.5 = (bf16[944,128]{1,0:T(8,128)(2,1)S(1)}, bf16[944,128]{1,0:T(8,128)(2,1)S(1)}, u32[]{:S(2)}, u32[]{:S(2)}) collective-permute-start(bf16[944,128]{1,0:T(8,128)(2,1)S(1)} %shard_map.74.refs_0_), channel_id=1, source_target_pairs={{0,8},{8,0},{1,9},{9,1},{2,10},{10,2},{3,11},{11,3},{4,12},{12,4},... | collective-permute-start | bytes 725000 | tf_op jit(solution)/shard_map/ppermute | solution.py:361
  75.3 6.5 %collective-permute-start.7 = (bf16[944,128]{1,0:T(8,128)(2,1)S(1)}, bf16[944,128]{1,0:T(8,128)(2,1)S(1)}, u32[]{:S(2)}, u32[]{:S(2)}) collective-permute-start(bf16[944,128]{1,0:T(8,128)(2,1)S(1)} %shard_map.74.refs_0_), channel_id=1, source_target_pairs={{0,16},{1,17},{2,18},{3,19},{4,20},{5,21},{6,22},{7,23},{8,10},{9,... | collective-permute-start | bytes 725000 | tf_op jit(solution)/shard_map/ppermute | solution.py:378
  75.4 6.4 %collective-permute-start.6 = (bf16[944,128]{1,0:T(8,128)(2,1)S(1)}, bf16[944,128]{1,0:T(8,128)(2,1)S(1)}, u32[]{:S(2)}, u32[]{:S(2)}) collective-permute-start(bf16[944,128]{1,0:T(8,128)(2,1)S(1)} %shard_map.74.refs_0_), channel_id=1, source_target_pairs={{0,48},{1,49},{2,50},{3,51},{4,52},{5,53},{6,54},{7,55},{8,14},{9,... | collective-permute-start | bytes 725000 | tf_op jit(solution)/shard_map/ppermute | solution.py:378
  78.1 4.8 %collective-permute-start.11 = (bf16[944,128]{1,0:T(8,128)(2,1)S(1)}, bf16[944,128]{1,0:T(8,128)(2,1)S(1)}, u32[]{:S(2)}, u32[]{:S(2)}) collective-permute-start(bf16[944,128]{1,0:T(8,128)(2,1)S(1)} %collective-permute-done.10.refs_0_), channel_id=1, source_target_pairs={{0,8},{8,0},{1,9},{9,1},{2,10},{10,2},{3,11},{11,3},{4,12},{12,4},... | collective-permute-start | bytes 725000 | tf_op jit(solution)/shard_map/ppermute | solution.py:361
  81.8 2.4 %collective-permute-start.8 = (bf16[944,128]{1,0:T(8,128)(2,1)S(1)}, bf16[944,128]{1,0:T(8,128)(2,1)S(1)}, u32[]{:S(2)}, u32[]{:S(2)}) collective-permute-start(bf16[944,128]{1,0:T(8,128)(2,1)S(1)} %collective-permute-done.7.refs_1_), channel_id=1, source_target_pairs={{0,8},{8,0},{1,9},{9,1},{2,10},{10,2},{3,11},{11,3},{4,12},{12,4},... | collective-permute-start | bytes 725000 | tf_op jit(solution)/shard_map/ppermute | solution.py:361
  82.9 1.5 %collective-permute-start.9 = (bf16[944,128]{1,0:T(8,128)(2,1)S(1)}, bf16[944,128]{1,0:T(8,128)(2,1)S(1)}, u32[]{:S(2)}, u32[]{:S(2)}) collective-permute-start(bf16[944,128]{1,0:T(8,128)(2,1)S(1)} %collective-permute-done.6.refs_2_), channel_id=1, source_target_pairs={{0,8},{8,0},{1,9},{9,1},{2,10},{10,2},{3,11},{11,3},{4,12},{12,4},... | collective-permute-start | bytes 725000 | tf_op jit(solution)/shard_map/ppermute | solution.py:361

commit v8 on v7

--- a/solution.py
+++ b/solution.py
@@ -438,7 +438,7 @@
     zero, two, one, three = summed(core, early, swapped(early_sent), late_sum)
     scalars = [value.reshape(1) for value in (core, ring_place(core), ring_place(1 - core))]
     totals = placed(scalars, ((0, 0), (0, 1)), [zero, swapped(zero)], ())
-    *totals, three, one = lax.optimization_barrier((*totals, three, one))
+    *totals, three = lax.optimization_barrier((*totals, three))
     swaps = [swapped(one), swapped(three)]
     totals = placed(
         scalars, ((2, 0), (1, 0), (3, 0), (2, 1)), [two, one, three, swapped(two)], totals

time: 85.6 us -> 86.5 us (1.011)
    ppermute x6, starting transfers between devices: 9.62 us -> 11.1 us  [swapped(): return lax.ppermute(block, 'core', [(0, 1), (1, 0)])]
    ppermute x3, starting transfers between devices: 2.76 us -> 1.55 us  [summed(): return [quarter] + [lax.ppermute(quarter, FINE, shifts[by]) for by in order]]
  transfers between devices with their start and end apart: 13 -> 13, of which waited for: 7 -> 5; matrix products, arithmetic and copies ran while one was open for 0% -> 0% of each run, Pallas kernels for 5% -> 5%
where the time goes in v8:
time: 86.5 us; the launch traced here: 86.2 us
  waiting for transfers between devices  25.3 us (29%)
  blocking collectives  24.6 us (28%)
  starting transfers between devices  23.6 us (27%)
  Pallas kernels  11.9 us (14%)
    all_to_all x2, blocking collectives, summed(): lax.all_to_all(blocks, FINE, split_axis=0, concat_axis=0, axis_index_grou...  24.6 us
    all_to_all x1, waiting for transfers between devices, per_device(): lax.all_to_all(sent, ('y', 'xh'), split_axis=0, concat_axis=0, tiled=True)  15.9 us
    ppermute x6, starting transfers between devices, swapped(): return lax.ppermute(block, 'core', [(0, 1), (1, 0)])  11.1 us
    all_to_all x1, starting transfers between devices, per_device(): lax.all_to_all(sent, ('y', 'xh'), split_axis=0, concat_axis=0, tiled=True)  7.62 us
    ppermute x3, waiting for transfers between devices, summed(): others = [lax.ppermute(blocks[by], FINE, shifts[by]) for by in order]  6.14 us
    pallas_call x3, Pallas kernels, placed(): pl.pallas_call(functools.partial(place_kernel, origins), out_shape=(jax.S...  3.35 us
    ppermute x3, starting transfers between devices, summed(): others = [lax.ppermute(blocks[by], FINE, shifts[by]) for by in order]  3.33 us
    pallas_call x1, Pallas kernels, late_layer(): pl.pallas_call(late_kernel, out_shape=(jax.ShapeDtypeStruct((2, SIDE, SID...  3.26 us
  transfers between devices with their start and end apart: 13, of which 5 were waited for; matrix products, arithmetic and copies ran while one was open for 0% of the time, Pallas kernels for 5%

profile of v8, /device:TPU:1, one launch (start us, length us, event | category | flops | bytes accessed | tf_op | source)
XLA Modules:
  0.0 86.2 jit_solution(13893181718492743454)
XLA Ops:
  0.7 7.6 %all-to-all-start = ((bf16[8,2,4,64,128]{4,3,2,1,0:T(8,128)(2,1)}), bf16[8,2,4,64,128]{4,3,2,1,0:T(8,128)(2,1)S(1)}, u32[]{:S(2)}, u32[]{:S(2)}) async-start(bf16[8,2,4,64,128]{4,3,2,1,0:T(8,128)(2,1)} %bitcast.19), calls=%async_computation | async-start | bytes 2097152 | tf_op jit(solution)/shard_map/all_to_all | solution.py:430
  8.3 0.0 copy-start
  8.3 15.9 %all-to-all-done.received = bf16[8,2,4,64,128]{4,3,2,1,0:T(8,128)(2,1)S(1)} async-done(((bf16[8,2,4,64,128]{4,3,2,1,0:T(8,128)(2,1)}), bf16[8,2,4,64,128]{4,3,2,1,0:T(8,128)(2,1)S(1)}, u32[]{:S(2)}, u32[]{:S(2)}) %all-to-all-start) | async-done | bytes 1048608 | tf_op jit(solution)/shard_map/all_to_all | solution.py:430
  24.3 1.5 %shard_map.67 = (bf16[10,10,16,384]{3,2,1,0:T(8,128)(2,1)S(1)}, bf16[4,9,9,16,256]{4,3,2,1,0:T(8,128)(2,1)S(1)}, f32[1024,128]{1,0:T(8,128)S(1)}) custom-call(bf16[8,2,4,64,128]{4,3,2,1,0:T(8,128)(2,1)S(1)} %all-to-all-done.received, bf16[16,256,128]{2,1,0:T(8,128)(2,1)S(1)} %bitcast.16), custom_call_target="tpu_custom_call" | custom-call | flops 1073741824 | bytes 8388608 | tf_op jit(solution)/shard_map/pallas_call | solution.py:229
  25.8 3.3 %shard_map.68 = (bf16[2,8,64,128]{3,2,1,0:T(8,128)(2,1)}, bf16[1728,128]{1,0:T(8,128)(2,1)S(1)}, bf16[1728,128]{1,0:T(8,128)(2,1)S(1)}, bf16[10,10,16,384]{3,2,1,0:T(8,128)(2,1)S(1)}) custom-call(s32[1]{0:T(128)} %bitcast.core, bf16[10,10,16,384]{3,2,1,0:T(8,128)(2,1)S(1)} %get-tuple-element.28.hidden, bf16[9,384,128]{2,1,0:T(8,128)(2,1)S(1)} %bitcast.13, ...), custom_call_target="tpu_custom_call" | custom-call | flops 1811939328 | bytes 8388608 | tf_op jit(solution)/shard_map/pallas_call | solution.py:245
  29.0 2.2 %collective-permute-start = (bf16[1728,128]{1,0:T(8,128)(2,1)S(1)}, bf16[1728,128]{1,0:T(8,128)(2,1)S(1)}, u32[]{:S(2)}, u32[]{:S(2)}) collective-permute-start(bf16[1728,128]{1,0:T(8,128)(2,1)S(1)} %get-tuple-element.36), channel_id=1, source_target_pairs={{0,8},{8,0},{1,9},{9,1},{2,10},{10,2},{3,11},{11,3},{4,12},{12,4},... | collective-permute-start | bytes 1327112 | tf_op jit(solution)/shard_map/ppermute | solution.py:361
  31.3 1.7 %shard_map.69 = (bf16[10,10,16,128]{3,2,1,0:T(8,128)(2,1)S(1)}, bf16[4,256,1024]{2,1,0:T(8,128)(2,1)S(1)}) custom-call(bf16[9,384,128]{2,1,0:T(8,128)(2,1)S(1)} %bitcast.14, bf16[4,9,9,16,256]{4,3,2,1,0:T(8,128)(2,1)S(1)} %get-tuple-element.30.volume, bf16[10,10,16,384]{3,2,1,0:T(8,128)(2,1)S(1)} %get-tuple-element.31.error, ...), custom_call_target="tpu_custom_call" | custom-call | flops 905969664 | bytes 8388608 | tf_op jit(solution)/shard_map/pallas_call | solution.py:266
  33.0 0.0 collective-permute-done.late_other
  33.0 1.7 %shard_map.70 = (bf16[2048,128]{1,0:T(8,128)(2,1)S(1)}, bf16[2048,128]{1,0:T(8,128)(2,1)S(1)}, bf16[1728,128]{1,0:T(8,128)(2,1)S(1)}) custom-call(s32[1]{0:T(128)} %bitcast.core, bf16[10,10,16,128]{3,2,1,0:T(8,128)(2,1)S(1)} %get-tuple-element.33.error_early, bf16[4,256,1024]{2,1,0:T(8,128)(2,1)S(1)} %get-tuple-element.34.volume_t, ...), custom_call_target="tpu_custom_call" | custom-call | flops 1073741824 | bytes 8388608 | tf_op jit(solution)/shard_map/pallas_call | solution.py:281
  34.7 0.2 collective-permute-start.1
  34.9 1.8 %collective-permute-done.1.early_other = bf16[2048,128]{1,0:T(8,128)(2,1)S(1)} collective-permute-done((bf16[2048,128]{1,0:T(8,128)(2,1)S(1)}, bf16[2048,128]{1,0:T(8,128)(2,1)S(1)}, u32[]{:S(2)}, u32[]{:S(2)}) %collective-permute-start.1) | collective-permute-done | bytes 524320 | tf_op jit(solution)/shard_map/ppermute | solution.py:361
  36.7 0.1 shard_map.71
  36.8 0.7 collective-permute-start.2
  37.5 0.6 collective-permute-start.3
  38.1 2.1 %collective-permute-start.4 = (bf16[944,128]{1,0:T(8,128)(2,1)S(1)}, bf16[944,128]{1,0:T(8,128)(2,1)S(1)}, u32[]{:S(2)}, u32[]{:S(2)}) collective-permute-start(bf16[944,128]{1,0:T(8,128)(2,1)S(1)} %get-tuple-element.43), channel_id=1, source_target_pairs={{0,48},{1,49},{2,50},{3,51},{4,52},{5,53},{6,54},{7,55},{8,14},{9,... | collective-permute-start | bytes 725000 | tf_op jit(solution)/shard_map/ppermute | solution.py:371
  40.2 3.6 %collective-permute-done.2.second = bf16[944,128]{1,0:T(8,128)(2,1)S(1)} collective-permute-done((bf16[944,128]{1,0:T(8,128)(2,1)S(1)}, bf16[944,128]{1,0:T(8,128)(2,1)S(1)}, u32[]{:S(2)}, u32[]{:S(2)}) %collective-permute-start.2) | collective-permute-done | bytes 241696 | tf_op jit(solution)/shard_map/ppermute | solution.py:371
  43.7 2.5 %collective-permute-done.3.third = bf16[944,128]{1,0:T(8,128)(2,1)S(1)} collective-permute-done((bf16[944,128]{1,0:T(8,128)(2,1)S(1)}, bf16[944,128]{1,0:T(8,128)(2,1)S(1)}, u32[]{:S(2)}, u32[]{:S(2)}) %collective-permute-start.3) | collective-permute-done | bytes 241696 | tf_op jit(solution)/shard_map/ppermute | solution.py:371
  46.3 0.0 collective-permute-done.4.fourth
  46.3 0.2 shard_map.72
  46.5 13.4 %all_to_all.15.shares = bf16[16,64,128]{2,1,0:T(8,128)(2,1)S(1)} all-to-all(bf16[16,64,128]{2,1,0:T(8,128)(2,1)S(1)} %shard_map.72), channel_id=1, replica_groups={{0,1,2,3,4,5,6,7,64,65,66,67,68,69,70,71},{16,17,18,19,20,21,22,23,80,8..., dimensions={0} | all-to-all | bytes 524288 | tf_op jit(solution)/shard_map/all_to_all | solution.py:366
  60.0 11.2 %all_to_all.16.shares = bf16[16,64,128]{2,1,0:T(8,128)(2,1)S(1)} all-to-all(bf16[16,64,128]{2,1,0:T(8,128)(2,1)S(1)} %shard_map.73), channel_id=1, replica_groups={{0,1,2,3,4,5,6,7,64,65,66,67,68,69,70,71},{16,17,18,19,20,21,22,23,80,8..., dimensions={0} | all-to-all | bytes 524288 | tf_op jit(solution)/shard_map/all_to_all | solution.py:366
  71.2 0.1 collective-permute-start.10
  71.3 4.0 %collective-permute-start.7 = (bf16[944,128]{1,0:T(8,128)(2,1)S(1)}, bf16[944,128]{1,0:T(8,128)(2,1)S(1)}, u32[]{:S(2)}, u32[]{:S(2)}) collective-permute-start(bf16[944,128]{1,0:T(8,128)(2,1)S(1)} %shard_map.74.refs_0_), channel_id=1, source_target_pairs={{0,8},{8,0},{1,9},{9,1},{2,10},{10,2},{3,11},{11,3},{4,12},{12,4},... | collective-permute-start | bytes 725000 | tf_op jit(solution)/shard_map/ppermute | solution.py:361
  75.3 1.0 %collective-permute-start.8 = (bf16[944,128]{1,0:T(8,128)(2,1)S(1)}, bf16[944,128]{1,0:T(8,128)(2,1)S(1)}, u32[]{:S(2)}, u32[]{:S(2)}) collective-permute-start(bf16[944,128]{1,0:T(8,128)(2,1)S(1)} %shard_map.74.refs_0_), channel_id=1, source_target_pairs={{0,48},{1,49},{2,50},{3,51},{4,52},{5,53},{6,54},{7,55},{8,14},{9,... | collective-permute-start | bytes 725000 | tf_op jit(solution)/shard_map/ppermute | solution.py:378
  76.3 0.4 collective-permute-start.5
  76.8 1.3 %collective-permute-done.10.refs_0_ = bf16[944,128]{1,0:T(8,128)(2,1)S(1)} collective-permute-done((bf16[944,128]{1,0:T(8,128)(2,1)S(1)}, bf16[944,128]{1,0:T(8,128)(2,1)S(1)}, u32[]{:S(2)}, u32[]{:S(2)}) %collective-permute-start.10) | collective-permute-done | bytes 241696 | tf_op jit(solution)/shard_map/ppermute | solution.py:378
  78.1 2.2 %collective-permute-start.11 = (bf16[944,128]{1,0:T(8,128)(2,1)S(1)}, bf16[944,128]{1,0:T(8,128)(2,1)S(1)}, u32[]{:S(2)}, u32[]{:S(2)}) collective-permute-start(bf16[944,128]{1,0:T(8,128)(2,1)S(1)} %collective-permute-done.10.refs_0_), channel_id=1, source_target_pairs={{0,8},{8,0},{1,9},{9,1},{2,10},{10,2},{3,11},{11,3},{4,12},{12,4},... | collective-permute-start | bytes 725000 | tf_op jit(solution)/shard_map/ppermute | solution.py:361
  80.3 1.0 %shard_map.75 = (f32[4096,128]{1,0:T(8,128)}, f32[3456,128]{1,0:T(8,128)}) custom-call(s32[1]{0:T(128)} %bitcast.core, s32[1]{0:T(128)} %bitcast.8.place, s32[1]{0:T(128)} %bitcast.9.other_place, bf16[944,128]{1,0:T(8,128)(2,1)S(1)} %shard_map.74.refs_0_, bf16[944,128]{1,0:T(8,128)(2,1)S(1)} %collective-permute-done.7.refs_1_), custom_call_target="tpu_custom_call" | custom-call | bytes 1572864 | tf_op jit(solution)/shard_map/pallas_call | solution.py:408
  81.3 1.6 %collective-permute-start.9 = (bf16[944,128]{1,0:T(8,128)(2,1)S(1)}, bf16[944,128]{1,0:T(8,128)(2,1)S(1)}, u32[]{:S(2)}, u32[]{:S(2)}) collective-permute-start(bf16[944,128]{1,0:T(8,128)(2,1)S(1)} %collective-permute-done.8.refs_2_), channel_id=1, source_target_pairs={{0,8},{8,0},{1,9},{9,1},{2,10},{10,2},{3,11},{11,3},{4,12},{12,4},... | collective-permute-start | bytes 725000 | tf_op jit(solution)/shard_map/ppermute | solution.py:361
  82.9 0.9 %collective-permute-start.6 = (bf16[944,128]{1,0:T(8,128)(2,1)S(1)}, bf16[944,128]{1,0:T(8,128)(2,1)S(1)}, u32[]{:S(2)}, u32[]{:S(2)}) collective-permute-start(bf16[944,128]{1,0:T(8,128)(2,1)S(1)} %collective-permute-done.5.refs_1_), channel_id=1, source_target_pairs={{0,8},{8,0},{1,9},{9,1},{2,10},{10,2},{3,11},{11,3},{4,12},{12,4},... | collective-permute-start | bytes 725000 | tf_op jit(solution)/shard_map/ppermute | solution.py:361
  83.8 1.4 %shard_map.76 = (f32[4096,128]{1,0:T(8,128)}, f32[3456,128]{1,0:T(8,128)}) custom-call(s32[1]{0:T(128)} %bitcast.core, s32[1]{0:T(128)} %bitcast.8.place, s32[1]{0:T(128)} %bitcast.9.other_place, bf16[944,128]{1,0:T(8,128)(2,1)S(1)} %collective-permute-done.10.refs_0_, ...), custom_call_target="tpu_custom_call", output_to_operand_aliasing={{0}: (7, {}), {1}: (8, {})} | custom-call | bytes 3145728 | tf_op jit(solution)/shard_map/pallas_call | solution.py:408
  85.2 1.0 %shard_map.77 = (f32[4096,128]{1,0:T(8,128)}, f32[3456,128]{1,0:T(8,128)}) custom-call(s32[1]{0:T(128)} %bitcast.core, s32[1]{0:T(128)} %bitcast.8.place, s32[1]{0:T(128)} %bitcast.9.other_place, bf16[944,128]{1,0:T(8,128)(2,1)S(1)} %collective-permute-done.6.refs_0_, ...), custom_call_target="tpu_custom_call", output_to_operand_aliasing={{0}: (5, {}), {1}: (6, {})} | custom-call | bytes 1572864 | tf_op jit(solution)/shard_map/pallas_call | solution.py:408
  (14 shorter events, 0.2 us)
Async XLA Ops:
  0.6 7.6 %copy-start.2 = (bf16[2,8,8,8,128]{4,3,2,1,0:T(8,128)(2,1)S(1)}, bf16[2,8,8,8,128]{4,3,2,1,0:T(8,128)(2,1)}, u32[]{:S(2)}) copy-start(bf16[2,8,8,8,128]{4,3,2,1,0:T(8,128)(2,1)} %param.7) | copy-start | bytes 786436
  0.6 23.6 %copy-start.1 = (bf16[4,4,4,64,128]{4,3,2,1,0:T(8,128)(2,1)S(1)}, bf16[4,4,4,64,128]{4,3,2,1,0:T(8,128)(2,1)}, u32[]{:S(2)}) copy-start(bf16[4,4,4,64,128]{4,3,2,1,0:T(8,128)(2,1)} %param.5) | copy-start | bytes 3145732
  0.7 23.6 %all-to-all-start = ((bf16[8,2,4,64,128]{4,3,2,1,0:T(8,128)(2,1)}), bf16[8,2,4,64,128]{4,3,2,1,0:T(8,128)(2,1)S(1)}, u32[]{:S(2)}, u32[]{:S(2)}) async-start(bf16[8,2,4,64,128]{4,3,2,1,0:T(8,128)(2,1)} %bitcast.19), calls=%async_computation | async-start | bytes 2097152 | tf_op jit(solution)/shard_map/all_to_all | solution.py:430
  8.3 17.4 %copy-start = (bf16[3,3,3,128,128]{4,3,2,1,0:T(8,128)(2,1)S(1)}, bf16[3,3,3,128,128]{4,3,2,1,0:T(8,128)(2,1)}, u32[]{:S(2)}) copy-start(bf16[3,3,3,128,128]{4,3,2,1,0:T(8,128)(2,1)} %param.6) | copy-start | bytes 2654212
  29.0 3.9 %collective-permute-start = (bf16[1728,128]{1,0:T(8,128)(2,1)S(1)}, bf16[1728,128]{1,0:T(8,128)(2,1)S(1)}, u32[]{:S(2)}, u32[]{:S(2)}) collective-permute-start(bf16[1728,128]{1,0:T(8,128)(2,1)S(1)} %get-tuple-element.36), channel_id=1, source_target_pairs={{0,8},{8,0},{1,9},{9,1},{2,10},{10,2},{3,11},{11,3},{4,12},{12,4},... | collective-permute-start | bytes 1327112 | tf_op jit(solution)/shard_map/ppermute | solution.py:361
  34.7 2.0 %collective-permute-start.1 = (bf16[2048,128]{1,0:T(8,128)(2,1)S(1)}, bf16[2048,128]{1,0:T(8,128)(2,1)S(1)}, u32[]{:S(2)}, u32[]{:S(2)}) collective-permute-start(bf16[2048,128]{1,0:T(8,128)(2,1)S(1)} %get-tuple-element.38), channel_id=1, source_target_pairs={{0,8},{8,0},{1,9},{9,1},{2,10},{10,2},{3,11},{11,3},{4,12},{12,4},... | collective-permute-start | bytes 1572872 | tf_op jit(solution)/shard_map/ppermute | solution.py:361
  36.8 6.9 %collective-permute-start.2 = (bf16[944,128]{1,0:T(8,128)(2,1)S(1)}, bf16[944,128]{1,0:T(8,128)(2,1)S(1)}, u32[]{:S(2)}, u32[]{:S(2)}) collective-permute-start(bf16[944,128]{1,0:T(8,128)(2,1)S(1)} %get-tuple-element.41), channel_id=1, source_target_pairs={{0,32},{1,33},{2,34},{3,35},{4,36},{5,37},{6,38},{7,39},{8,12},{9,... | collective-permute-start | bytes 725000 | tf_op jit(solution)/shard_map/ppermute | solution.py:371
  37.5 8.8 %collective-permute-start.3 = (bf16[944,128]{1,0:T(8,128)(2,1)S(1)}, bf16[944,128]{1,0:T(8,128)(2,1)S(1)}, u32[]{:S(2)}, u32[]{:S(2)}) collective-permute-start(bf16[944,128]{1,0:T(8,128)(2,1)S(1)} %get-tuple-element.42), channel_id=1, source_target_pairs={{0,16},{1,17},{2,18},{3,19},{4,20},{5,21},{6,22},{7,23},{8,10},{9,... | collective-permute-start | bytes 725000 | tf_op jit(solution)/shard_map/ppermute | solution.py:371
  38.1 8.2 %collective-permute-start.4 = (bf16[944,128]{1,0:T(8,128)(2,1)S(1)}, bf16[944,128]{1,0:T(8,128)(2,1)S(1)}, u32[]{:S(2)}, u32[]{:S(2)}) collective-permute-start(bf16[944,128]{1,0:T(8,128)(2,1)S(1)} %get-tuple-element.43), channel_id=1, source_target_pairs={{0,48},{1,49},{2,50},{3,51},{4,52},{5,53},{6,54},{7,55},{8,14},{9,... | collective-permute-start | bytes 725000 | tf_op jit(solution)/shard_map/ppermute | solution.py:371
  71.2 6.9 %collective-permute-start.10 = (bf16[944,128]{1,0:T(8,128)(2,1)S(1)}, bf16[944,128]{1,0:T(8,128)(2,1)S(1)}, u32[]{:S(2)}, u32[]{:S(2)}) collective-permute-start(bf16[944,128]{1,0:T(8,128)(2,1)S(1)} %shard_map.74.refs_0_), channel_id=1, source_target_pairs={{0,32},{1,33},{2,34},{3,35},{4,36},{5,37},{6,38},{7,39},{8,12},{9,... | collective-permute-start | bytes 725000 | tf_op jit(solution)/shard_map/ppermute | solution.py:378
  71.3 9.0 %collective-permute-start.7 = (bf16[944,128]{1,0:T(8,128)(2,1)S(1)}, bf16[944,128]{1,0:T(8,128)(2,1)S(1)}, u32[]{:S(2)}, u32[]{:S(2)}) collective-permute-start(bf16[944,128]{1,0:T(8,128)(2,1)S(1)} %shard_map.74.refs_0_), channel_id=1, source_target_pairs={{0,8},{8,0},{1,9},{9,1},{2,10},{10,2},{3,11},{11,3},{4,12},{12,4},... | collective-permute-start | bytes 725000 | tf_op jit(solution)/shard_map/ppermute | solution.py:361
  75.3 6.0 %collective-permute-start.8 = (bf16[944,128]{1,0:T(8,128)(2,1)S(1)}, bf16[944,128]{1,0:T(8,128)(2,1)S(1)}, u32[]{:S(2)}, u32[]{:S(2)}) collective-permute-start(bf16[944,128]{1,0:T(8,128)(2,1)S(1)} %shard_map.74.refs_0_), channel_id=1, source_target_pairs={{0,48},{1,49},{2,50},{3,51},{4,52},{5,53},{6,54},{7,55},{8,14},{9,... | collective-permute-start | bytes 725000 | tf_op jit(solution)/shard_map/ppermute | solution.py:378
  76.3 6.6 %collective-permute-start.5 = (bf16[944,128]{1,0:T(8,128)(2,1)S(1)}, bf16[944,128]{1,0:T(8,128)(2,1)S(1)}, u32[]{:S(2)}, u32[]{:S(2)}) collective-permute-start(bf16[944,128]{1,0:T(8,128)(2,1)S(1)} %shard_map.74.refs_0_), channel_id=1, source_target_pairs={{0,16},{1,17},{2,18},{3,19},{4,20},{5,21},{6,22},{7,23},{8,10},{9,... | collective-permute-start | bytes 725000 | tf_op jit(solution)/shard_map/ppermute | solution.py:378
  78.1 5.7 %collective-permute-start.11 = (bf16[944,128]{1,0:T(8,128)(2,1)S(1)}, bf16[944,128]{1,0:T(8,128)(2,1)S(1)}, u32[]{:S(2)}, u32[]{:S(2)}) collective-permute-start(bf16[944,128]{1,0:T(8,128)(2,1)S(1)} %collective-permute-done.10.refs_0_), channel_id=1, source_target_pairs={{0,8},{8,0},{1,9},{9,1},{2,10},{10,2},{3,11},{11,3},{4,12},{12,4},... | collective-permute-start | bytes 725000 | tf_op jit(solution)/shard_map/ppermute | solution.py:361
  81.3 3.9 %collective-permute-start.9 = (bf16[944,128]{1,0:T(8,128)(2,1)S(1)}, bf16[944,128]{1,0:T(8,128)(2,1)S(1)}, u32[]{:S(2)}, u32[]{:S(2)}) collective-permute-start(bf16[944,128]{1,0:T(8,128)(2,1)S(1)} %collective-permute-done.8.refs_2_), channel_id=1, source_target_pairs={{0,8},{8,0},{1,9},{9,1},{2,10},{10,2},{3,11},{11,3},{4,12},{12,4},... | collective-permute-start | bytes 725000 | tf_op jit(solution)/shard_map/ppermute | solution.py:361
  82.9 2.3 %collective-permute-start.6 = (bf16[944,128]{1,0:T(8,128)(2,1)S(1)}, bf16[944,128]{1,0:T(8,128)(2,1)S(1)}, u32[]{:S(2)}, u32[]{:S(2)}) collective-permute-start(bf16[944,128]{1,0:T(8,128)(2,1)S(1)} %collective-permute-done.5.refs_1_), channel_id=1, source_target_pairs={{0,8},{8,0},{1,9},{9,1},{2,10},{10,2},{3,11},{11,3},{4,12},{12,4},... | collective-permute-start | bytes 725000 | tf_op jit(solution)/shard_map/ppermute | solution.py:361
